TPU v7x, 32 devices: a whole 2x2x4 slice. The times are simulated.
32 devices in a mesh: seq: 8 (over y, x, core), mp: 4 (over z).
Axes of the slice: x: 2, y: 2, z: 4, core: 2. Of those that a mesh axis runs over, the one named last changes fastest.
Arguments:
- layer_in: bfloat16 [4, 2048, 2048], P(None, ('seq', 'mp')), may hold values from -6 to 6
- w_qkv: bfloat16 [3, 2048, 2048], P(None, None, 'mp'), may hold values from -0.125 to 0.125
- w_out: bfloat16 [2048, 2048], P('mp'), may hold values from -3 to 3
- w_gate_up: bfloat16 [2, 2048, 8192], P(None, None, 'mp'), may hold values from -0.125 to 0.125
- w_down: bfloat16 [8192, 2048], P('mp'), may hold values from -0.0625 to 0.0625
- a_in: bfloat16 [4, 5, 16, 2048], replicated, may hold values from -0.125 to 0.125
- b_qkv: bfloat16 [4, 3, 16, 2048], P(None, None, None, 'mp'), may hold values from -1.5 to 1.5
- b_gate_up: bfloat16 [4, 2, 16, 8192], P(None, None, None, 'mp'), may hold values from -1.5 to 1.5
- a_out: bfloat16 [4, 16, 2048], P(None, None, 'mp'), may hold values from -3 to 3
- a_down: bfloat16 [4, 16, 8192], P(None, None, 'mp'), may hold values from -0.0625 to 0.0625
- b_out_down: bfloat16 [4, 2, 16, 2048], replicated, may hold values from -1.5 to 1.5
- set_index: int32 [4], replicated, may hold values from 0 to 3
- positions: int32 [4, 2048], P(None, 'seq'), may hold values from 0 to 4094, as said below
- cotangent: bfloat16 [4, 2048, 2048], P(None, ('seq', 'mp')), may hold values from -6 to 6
Outputs:
- result: bfloat16 [4, 2048, 2048], P(None, ('seq', 'mp'))
- grad_in: bfloat16 [4, 2048, 2048], P(None, ('seq', 'mp'))
- grad_a_in: float32 [4, 5, 16, 2048], replicated
- grad_b_qkv: float32 [4, 3, 16, 2048], P(None, None, None, 'mp')
- grad_b_gate_up: float32 [4, 2, 16, 8192], P(None, None, None, 'mp')
- grad_a_out: float32 [4, 16, 2048], P(None, None, 'mp')
- grad_a_down: float32 [4, 16, 8192], P(None, None, 'mp')
- grad_b_out_down: float32 [4, 2, 16, 2048], replicated
Inputs may be any that keep to these rules, and one draw needn't show every extreme that they name: Along each sequence the positions start at 0 and rise by one or two from each token to the next; in one sequence they rise by two throughout.
All inputs are finite; a program needn't handle non-finite values.
Results may differ from a plain program's by a relative error of at most 0.025.
Values may be sent and summed in bfloat16 or wider, within the bound.
A program may use at most 512 MiB of HBM per device.

v0:
```python
import math

import jax
import jax.numpy as jnp
from jax import lax
from jax.sharding import PartitionSpec as P

HDIM = 128


adapt_scale = 0.5
norm_eps = 1e-05
rope_base = 10000.0
far_below = -1e30
highest = lax.Precision.HIGHEST


def layer_norm(values):
    centred = values - jnp.mean(values, axis=-1, keepdims=True)
    inverse = lax.rsqrt(jnp.mean(centred * centred, axis=-1, keepdims=True) + norm_eps)
    return (centred * inverse, inverse)


def norm_back(gradient, normed, inverse):
    return inverse * (
        gradient
        - jnp.mean(gradient, axis=-1, keepdims=True)
        - normed * jnp.mean(gradient * normed, axis=-1, keepdims=True)
    )


def gather_rows(values):
    return lax.all_gather(values, "mp", axis=1, tiled=True)


def scatter_rows(values):
    return lax.psum_scatter(
        values.astype(jnp.bfloat16), "mp", scatter_dimension=1, tiled=True
    ).astype(jnp.float32)


def rope_tables(positions):
    half_dim = HDIM // 2
    frequency = jnp.exp(
        jnp.arange(half_dim, dtype=jnp.float32) * (-2.0 * math.log(rope_base) / HDIM)
    )
    angles = jnp.transpose(positions).astype(jnp.float32)[:, :, None, None] * frequency
    return (jnp.cos(angles), jnp.sin(angles))


def rotate(values, cosine_table, sine_table):
    half_dim = values.shape[-1] // 2
    first_half = values[..., :half_dim]
    second_half = values[..., half_dim:]
    return jnp.concatenate(
        [
            first_half * cosine_table - second_half * sine_table,
            second_half * cosine_table + first_half * sine_table,
        ],
        axis=-1,
    )


def rotate_back(gradient, cosine_table, sine_table):
    half_dim = gradient.shape[-1] // 2
    first_half = gradient[..., :half_dim]
    second_half = gradient[..., half_dim:]
    return jnp.concatenate(
        [
            first_half * cosine_table + second_half * sine_table,
            second_half * cosine_table - first_half * sine_table,
        ],
        axis=-1,
    )


def masked_scores(queries, key_rows, query_first, key_first, score_scale):
    raw_scores = (
        jnp.einsum("qshd,kshd->shqk", queries, key_rows, preferred_element_type=jnp.float32)
        * score_scale
    )
    query_index = query_first + jnp.arange(queries.shape[0])
    key_index = key_first + jnp.arange(key_rows.shape[0])
    return (raw_scores, key_index[None, :] <= query_index[:, None])


def blockwise(fold_step, state_carry, pieces, start_row):
    row_count = pieces[0].shape[0]
    block_size = 512

    def block_turn(block_id, running):
        blocks = tuple(
            (
                lax.dynamic_slice_in_dim(shard_piece, block_id * block_size, block_size, 0)
                for shard_piece in pieces
            )
        )
        return fold_step(running, blocks, start_row + block_id * block_size)

    return lax.fori_loop(0, row_count // block_size, block_turn, state_carry)


def forward_step(queries, query_first, score_scale):
    query_last = query_first + queries.shape[0] - 1

    def fold_step(state_carry, blocks, key_first):
        key_rows, value_rows = blocks

        def compute(running):
            running_max, running_sum, weighted = running
            scores, allowed = masked_scores(queries, key_rows, query_first, key_first, score_scale)
            new_max = jnp.maximum(
                running_max, jnp.max(jnp.where(allowed, scores, far_below), axis=-1)
            )
            exponent = jnp.where(allowed, jnp.exp(scores - new_max[..., None]), 0.0)
            factor = jnp.exp(running_max - new_max)
            running_sum = running_sum * factor + jnp.sum(exponent, axis=-1)
            weighted = weighted * factor[..., None] + jnp.einsum(
                "shqk,kshd->shqd",
                exponent.astype(jnp.bfloat16),
                value_rows,
                preferred_element_type=jnp.float32,
            )
            return (new_max, running_sum, weighted)

        return lax.cond(key_first <= query_last, compute, lambda running: running, state_carry)

    return fold_step


def query_grad_step(queries, grad_heads, log_total, row_dots, query_first, score_scale):
    query_last = query_first + queries.shape[0] - 1

    def fold_step(state_carry, blocks, key_first):
        key_rows, value_rows = blocks

        def compute(running):
            scores, allowed = masked_scores(queries, key_rows, query_first, key_first, score_scale)
            attn_probs = jnp.where(allowed, jnp.exp(scores - log_total[..., None]), 0.0)
            grad_probs = jnp.einsum(
                "qshd,kshd->shqk", grad_heads, value_rows, preferred_element_type=jnp.float32
            )
            grad_scores = (attn_probs * (grad_probs - row_dots[..., None])).astype(jnp.bfloat16)
            return running + score_scale * jnp.einsum(
                "shqk,kshd->qshd", grad_scores, key_rows, preferred_element_type=jnp.float32
            )

        return lax.cond(key_first <= query_last, compute, lambda running: running, state_carry)

    return fold_step


def key_grad_step(key_rows, value_rows, key_first, score_scale):

    def fold_step(state_carry, blocks, query_first):
        queries, grad_heads, log_total_tok, row_dots_tok = blocks
        query_last = query_first + queries.shape[0] - 1

        def compute(running):
            scores, allowed = masked_scores(queries, key_rows, query_first, key_first, score_scale)
            log_total = jnp.transpose(log_total_tok, (1, 2, 0))
            row_dots = jnp.transpose(row_dots_tok, (1, 2, 0))
            attn_probs = jnp.where(allowed, jnp.exp(scores - log_total[..., None]), 0.0)
            grad_value_rows = jnp.einsum(
                "shqk,qshd->kshd",
                attn_probs.astype(jnp.bfloat16),
                grad_heads,
                preferred_element_type=jnp.float32,
            )
            grad_probs = jnp.einsum(
                "qshd,kshd->shqk", grad_heads, value_rows, preferred_element_type=jnp.float32
            )
            grad_scores = (attn_probs * (grad_probs - row_dots[..., None])).astype(jnp.bfloat16)
            grad_key_rows = score_scale * jnp.einsum(
                "shqk,qshd->kshd", grad_scores, queries, preferred_element_type=jnp.float32
            )
            return (grad_key_rows, grad_value_rows)

        return lax.cond(key_first <= query_last, compute, lambda running: running, state_carry)

    return fold_step


def project_in(token_rows, weight, a_chosen, b_chosen):
    main_term = jnp.einsum("scd,dw->csw", token_rows, weight, preferred_element_type=jnp.float32)
    low_rank = jnp.einsum("scd,srd->scr", token_rows, a_chosen, preferred_element_type=jnp.float32)
    side_term = jnp.einsum(
        "scr,srw->csw", low_rank, b_chosen.astype(jnp.float32), precision=highest
    )
    return (main_term + adapt_scale * side_term, low_rank)


def project_out(middle, weight, a_chosen, b_chosen):
    main_term = jnp.einsum("csw,wd->scd", middle, weight, preferred_element_type=jnp.float32)
    low_rank = jnp.einsum("csw,srw->scr", middle, a_chosen, preferred_element_type=jnp.float32)
    side_term = jnp.einsum(
        "scr,srd->scd", low_rank, b_chosen.astype(jnp.float32), precision=highest
    )
    return (main_term + adapt_scale * side_term, low_rank)


def back_in(gradient, weight, a_chosen, b_chosen, token_rows, low_rank):
    back_rank = jnp.einsum("csw,srw->scr", gradient, b_chosen, preferred_element_type=jnp.float32)
    grad_rows = jnp.einsum("csw,dw->scd", gradient, weight, preferred_element_type=jnp.float32)
    grad_rows = grad_rows + adapt_scale * jnp.einsum(
        "scr,srd->scd", back_rank, a_chosen.astype(jnp.float32), precision=highest
    )
    grad_a = adapt_scale * jnp.einsum("scr,scd->srd", back_rank, token_rows, precision=highest)
    grad_b = adapt_scale * jnp.einsum("scr,csw->srw", low_rank, gradient, precision=highest)
    return (grad_rows, grad_a, grad_b)


def back_out(gradient, weight, a_chosen, b_chosen, middle, low_rank):
    back_rank = jnp.einsum("scd,srd->scr", gradient, b_chosen, preferred_element_type=jnp.float32)
    grad_middle = jnp.einsum("scd,wd->csw", gradient, weight, preferred_element_type=jnp.float32)
    grad_middle = grad_middle + adapt_scale * jnp.einsum(
        "scr,srw->csw", back_rank, a_chosen.astype(jnp.float32), precision=highest
    )
    grad_a = adapt_scale * jnp.einsum("scr,csw->srw", back_rank, middle, precision=highest)
    grad_b = adapt_scale * jnp.einsum("scr,scd->srd", low_rank, gradient, precision=highest)
    return (grad_middle, grad_a, grad_b)


def pick_set(onehot, set_table):
    flattened = set_table.reshape(set_table.shape[0], -1)
    chosen = jnp.dot(onehot, flattened, preferred_element_type=jnp.float32).astype(jnp.bfloat16)
    return chosen.reshape((onehot.shape[0],) + set_table.shape[1:])


def spread_sets(onehot, per_sequence):
    flattened = per_sequence.reshape(per_sequence.shape[0], -1)
    summed = jnp.dot(onehot.astype(jnp.float32).T, flattened, precision=highest)
    return summed.reshape((onehot.shape[1],) + per_sequence.shape[1:])


def per_device(
    layer_in,
    w_qkv,
    w_out,
    w_gate_up,
    w_down,
    a_in,
    b_qkv,
    b_gate_up,
    a_out,
    a_down,
    b_out_down,
    set_index,
    positions,
    cotangent,
):
    local_len = positions.shape[1]
    seq_count = positions.shape[0]
    score_scale = 1.0 / math.sqrt(HDIM)
    my_first = lax.axis_index("seq") * local_len
    onehot = (set_index[:, None] == jnp.arange(a_in.shape[0])[None, :]).astype(jnp.bfloat16)
    chosen_a_in = pick_set(onehot, a_in)
    chosen_b_qkv = pick_set(onehot, b_qkv)
    chosen_b_gate_up = pick_set(onehot, b_gate_up)
    chosen_a_out = pick_set(onehot, a_out)
    chosen_a_down = pick_set(onehot, a_down)
    chosen_b_out_down = pick_set(onehot, b_out_down)

    def to_heads(values):
        return values.reshape(local_len, seq_count, -1, HDIM)

    residual_in = layer_in.astype(jnp.float32)
    normed_attn, inverse_attn = layer_norm(residual_in)
    rows_attn = gather_rows(normed_attn.astype(jnp.bfloat16))
    projected = [
        project_in(rows_attn, w_qkv[member], chosen_a_in[:, member], chosen_b_qkv[:, member])
        for member in range(3)
    ]
    cosine_table, sine_table = rope_tables(positions)
    queries = rotate(to_heads(projected[0][0]), cosine_table, sine_table).astype(jnp.bfloat16)
    key_rows = rotate(to_heads(projected[1][0]), cosine_table, sine_table).astype(jnp.bfloat16)
    value_rows = to_heads(projected[2][0]).astype(jnp.bfloat16)
    stat_shape = (seq_count, queries.shape[2], local_len)
    initial = (
        jnp.full(stat_shape, far_below, jnp.float32),
        jnp.zeros(stat_shape, jnp.float32),
        jnp.zeros(stat_shape + (HDIM,), jnp.float32),
    )
    attend = forward_step(queries, my_first, score_scale)
    running_max, running_sum, weighted = blockwise(
        attend,
        initial,
        (
            lax.all_gather(key_rows, "seq", axis=0, tiled=True),
            lax.all_gather(value_rows, "seq", axis=0, tiled=True),
        ),
        jnp.int32(0),
    )
    log_total = running_max + jnp.log(running_sum)
    attn_output = jnp.transpose(weighted / running_sum[..., None], (2, 0, 1, 3))
    mixed = attn_output.reshape(local_len, seq_count, -1).astype(jnp.bfloat16)
    attn_term, rank_out = project_out(mixed, w_out, chosen_a_out, chosen_b_out_down[:, 0])
    residual = residual_in + scatter_rows(attn_term)
    normed_mlp, inverse_mlp = layer_norm(residual)
    rows_mlp = gather_rows(normed_mlp.astype(jnp.bfloat16))
    gate_proj, rank_gate = project_in(
        rows_mlp, w_gate_up[0], chosen_a_in[:, 3], chosen_b_gate_up[:, 0]
    )
    up_proj, rank_up = project_in(rows_mlp, w_gate_up[1], chosen_a_in[:, 4], chosen_b_gate_up[:, 1])
    sigmoid_gate = jax.nn.sigmoid(gate_proj)
    activation = (gate_proj * sigmoid_gate * up_proj).astype(jnp.bfloat16)
    down_term, rank_down = project_out(activation, w_down, chosen_a_down, chosen_b_out_down[:, 1])
    result = (residual + scatter_rows(down_term)).astype(jnp.bfloat16)
    grad_down = gather_rows(cotangent)
    grad_activation, grad_a_down, grad_b_down = back_out(
        grad_down, w_down, chosen_a_down, chosen_b_out_down[:, 1], activation, rank_down
    )
    grad_up = (grad_activation * gate_proj * sigmoid_gate).astype(jnp.bfloat16)
    grad_gate = (
        grad_activation * up_proj * sigmoid_gate * (1.0 + gate_proj * (1.0 - sigmoid_gate))
    ).astype(jnp.bfloat16)
    rows_from_gate, grad_a_gate, grad_b_gate = back_in(
        grad_gate, w_gate_up[0], chosen_a_in[:, 3], chosen_b_gate_up[:, 0], rows_mlp, rank_gate
    )
    rows_from_up, grad_a_up, grad_b_up = back_in(
        grad_up, w_gate_up[1], chosen_a_in[:, 4], chosen_b_gate_up[:, 1], rows_mlp, rank_up
    )
    grad_residual = cotangent.astype(jnp.float32) + norm_back(
        scatter_rows(rows_from_gate + rows_from_up), normed_mlp, inverse_mlp
    )
    grad_attn_rows = gather_rows(grad_residual.astype(jnp.bfloat16))
    grad_mixed, grad_a_out, grad_b_out = back_out(
        grad_attn_rows, w_out, chosen_a_out, chosen_b_out_down[:, 0], mixed, rank_out
    )
    grad_heads = to_heads(grad_mixed.astype(jnp.bfloat16))
    row_dots_tok = jnp.sum(grad_heads.astype(jnp.float32) * attn_output, axis=-1)
    row_dots = jnp.transpose(row_dots_tok, (1, 2, 0))
    log_total_tok = jnp.transpose(log_total, (2, 0, 1))
    query_step = query_grad_step(queries, grad_heads, log_total, row_dots, my_first, score_scale)
    zero_heads = jnp.zeros(queries.shape, jnp.float32)
    every_key, every_value = (
        lax.all_gather(key_rows, "seq", axis=0, tiled=True),
        lax.all_gather(value_rows, "seq", axis=0, tiled=True),
    )
    grad_queries = blockwise(query_step, zero_heads, (every_key, every_value), 0)
    block_size = 512

    def one_block(block_id):
        first_key = block_id * block_size
        block_keys = lax.dynamic_slice_in_dim(every_key, first_key, block_size, 0)
        block_values = lax.dynamic_slice_in_dim(every_value, first_key, block_size, 0)
        zero_block = jnp.zeros(block_keys.shape, jnp.float32)
        block_step = key_grad_step(block_keys, block_values, first_key, score_scale)
        grad_key_block, grad_value_block = block_step(
            (zero_block, zero_block), (queries, grad_heads, log_total_tok, row_dots_tok), my_first
        )
        return jnp.concatenate([grad_key_block, grad_value_block], axis=-1)

    stacked = lax.map(one_block, jnp.arange(local_len * lax.axis_size("seq") // block_size))
    stacked_terms = lax.psum_scatter(
        stacked.reshape((local_len * lax.axis_size("seq"),) + stacked.shape[2:]).astype(
            jnp.bfloat16
        ),
        "seq",
        scatter_dimension=0,
        tiled=True,
    ).astype(jnp.float32)
    grad_keys = stacked_terms[..., :HDIM]
    grad_values = stacked_terms[..., HDIM:]
    grad_query_raw = (
        rotate_back(grad_queries, cosine_table, sine_table)
        .astype(jnp.bfloat16)
        .reshape(local_len, seq_count, -1)
    )
    grad_key_raw = (
        rotate_back(grad_keys, cosine_table, sine_table)
        .astype(jnp.bfloat16)
        .reshape(local_len, seq_count, -1)
    )
    grad_value_raw = grad_values.astype(jnp.bfloat16).reshape(local_len, seq_count, -1)
    back_parts = [
        back_in(
            gradient,
            w_qkv[member],
            chosen_a_in[:, member],
            chosen_b_qkv[:, member],
            rows_attn,
            projected[member][1],
        )
        for member, gradient in enumerate((grad_query_raw, grad_key_raw, grad_value_raw))
    ]
    grad_rows_attn = back_parts[0][0] + back_parts[1][0] + back_parts[2][0]
    grad_in = (
        grad_residual + norm_back(scatter_rows(grad_rows_attn), normed_attn, inverse_attn)
    ).astype(jnp.bfloat16)
    per_seq_a_in = jnp.stack(
        [back_parts[0][1], back_parts[1][1], back_parts[2][1], grad_a_gate, grad_a_up], axis=1
    )
    per_seq_b_qkv = jnp.stack([bundle[2] for bundle in back_parts], axis=1)
    per_seq_b_gate_up = jnp.stack([grad_b_gate, grad_b_up], axis=1)
    per_seq_b_out_down = jnp.stack([grad_b_out, grad_b_down], axis=1)
    sums_seq = (
        lax.psum(spread_sets(onehot, per_seq_b_qkv).astype(jnp.bfloat16), "seq").astype(
            jnp.float32
        ),
        lax.psum(spread_sets(onehot, per_seq_b_gate_up).astype(jnp.bfloat16), "seq").astype(
            jnp.float32
        ),
        lax.psum(spread_sets(onehot, grad_a_out).astype(jnp.bfloat16), "seq").astype(jnp.float32),
        lax.psum(spread_sets(onehot, grad_a_down).astype(jnp.bfloat16), "seq").astype(jnp.float32),
    )
    sums_all = lax.psum(
        (spread_sets(onehot, per_seq_a_in), spread_sets(onehot, per_seq_b_out_down)), ("seq", "mp")
    )
    return (
        result,
        grad_in,
        sums_all[0],
        sums_seq[0],
        sums_seq[1],
        sums_seq[2],
        sums_seq[3],
        sums_all[1],
    )


def solution(mesh):
    placed = (
        P(None, ("seq", "mp"), None),
        P(None, None, "mp"),
        P("mp", None),
        P(None, None, "mp"),
        P("mp", None),
        P(),
        P(None, None, None, "mp"),
        P(None, None, None, "mp"),
        P(None, None, "mp"),
        P(None, None, "mp"),
        P(),
        P(),
        P(None, "seq"),
        P(None, ("seq", "mp"), None),
    )
    return jax.shard_map(
        per_device,
        mesh=mesh,
        in_specs=placed,
        out_specs=(
            P(None, ("seq", "mp"), None),
            P(None, ("seq", "mp"), None),
            P(),
            P(None, None, None, "mp"),
            P(None, None, None, "mp"),
            P(None, None, "mp"),
            P(None, None, "mp"),
            P(),
        ),
        check_vma=False,
    )
```

profile of v0, /device:TPU:13, one launch (start us, length us, event | category | flops | bytes accessed | tf_op | source)
XLA Modules:
  0.0 1435.4 jit_solution(1802582353969299468)
XLA Ops:
  19.2 73.5 %all-gather.7.cloned.1.call-done = bf16[4,256,2048]{2,1,0:T(8,128)(2,1)} async-done(((bf16[4,64,2048]{2,1,0:T(8,128)(2,1)}), bf16[4,256,2048]{2,1,0:T(8,128)(2,1)}) %all-gather.7.cloned.1.call-update) | async-done | bytes 4194320 | tf_op jit(solution)/shard_map/all_gather | solution.py:33
  133.6 7.3 fusion.241
  145.2 11.1 reduce-scatter.6.cloned.1.call-start
  160.8 8.8 copy.127
  169.7 47.8 %all-gather.9.cloned.1.call-done = bf16[2048,4,4,128]{3,0,2,1:T(8,128)(2,1)} async-done(((bf16[256,4,4,128]{3,0,2,1:T(8,128)(2,1)}), bf16[2048,4,4,128]{3,0,2,1:T(8,128)(2,1)}) %all-gather.9.cloned.1.call-update) | async-done | bytes 8388624 | tf_op jit(solution)/shard_map/all_gather | solution.py:289
  219.0 31.6 %while.45 = (s32[]{:T(128)}, f32[4,4,256]{2,1,0:T(4,128)S(1)}, f32[4,4,256]{2,1,0:T(4,128)S(1)}, f32[4,4,256,128]{3,2,1,0:T(8,128)}, s32[]{:T(128)}, /*index=5*/...) while((s32[]{:T(128)}, f32[4,4,256]{2,1,0:T(4,128)S(1)}, ...), condition=%wide.region_7.8_spmd, body=%wide.region_2.7_spmd.sunk | while | flops 1097999104 | bytes 52173160 | solution.py:100
  219.0 10.5 conditional.6
  229.6 10.5 conditional.6
  240.1 10.5 conditional.6
  265.3 86.6 %reduce-scatter.6.cloned.1.call-done = bf16[4,64,2048]{2,1,0:T(8,128)(2,1)} async-done(((bf16[4,256,2048]{2,1,0:T(8,128)(2,1)}), bf16[4,64,2048]{2,1,0:T(8,128)(2,1)}) %reduce-scatter.6.cloned.1.call-update) | async-done | bytes 1048592 | tf_op jit(solution)/shard_map/reduce_scatter | solution.py:37
  361.1 71.1 %all-gather.15.cloned.1.call-done = bf16[4,256,2048]{2,1,0:T(8,128)(2,1)} async-done(((bf16[4,64,2048]{2,1,0:T(8,128)(2,1)}), bf16[4,256,2048]{2,1,0:T(8,128)(2,1)}) %all-gather.15.cloned.1.call-update) | async-done | bytes 4194320 | tf_op jit(solution)/shard_map/all_gather | solution.py:33
  439.2 13.8 bitcast_add_fusion.6
  452.9 60.7 %all-gather.13.cloned.1.call-done = bf16[4,256,2048]{2,1,0:T(8,128)(2,1)} async-done(((bf16[4,64,2048]{2,1,0:T(8,128)(2,1)}), bf16[4,256,2048]{2,1,0:T(8,128)(2,1)}) %all-gather.13.cloned.1.call-update) | async-done | bytes 4194320 | tf_op jit(solution)/shard_map/all_gather | solution.py:33
  528.5 13.6 bitcast_add_fusion.8
  542.0 24.9 %multiply_convert_fusion.1 = (bf16[256,4,2048]{2,0,1:T(8,128)(2,1)}, bf16[256,4,2048]{2,0,1:T(8,128)(2,1)}, bf16[256,4,2048]{2,0,1:T(8,128)(2,1)}) fusion(f32[256,4,2048]{2,0,1:T(8,128)} %bitcast_add_fusion.6, f32[256,4,2048]{2,0,1:T(8,128)} %bitcast_add_fusion.8, f32[4,2048,256]{1,2,0:T(8,128)} %fusion.208, ...), kind=kOutput, calls=%fused_computation.111 | convolution fusion | flops 8627683328 | bytes 50331648 | tf_op jit(solution)/shard_map/scd,dw->csw/dot_general | solution.py:185
  570.6 13.7 fusion.92
  585.5 6.7 fusion.213
  592.2 6.7 fusion.209
  598.9 19.5 %fusion.86 = bf16[4,256,2048]{2,1,0:T(8,128)(2,1)} fusion(f32[256,4,2048]{2,0,1:T(8,128)} %fusion.92, f32[4,256,2048]{2,1,0:T(8,128)} %fusion.213, f32[4,256,2048]{2,1,0:T(8,128)} %fusion.209, bf16[256,4,2048]{2,0,1:T(8,128)(2,1)} %get-tuple-element.978, bf16[2,2048,2048]{2,1,0:T(8,128)(2,1)} %param.29), kind=kOutput, calls=%fused_computation.89 | convolution fusion | flops 8602517504 | bytes 41943040 | tf_op jit(solution)/shard_map/csw,dw->scd/dot_general | solution.py:204
  618.9 77.4 %reduce-scatter.10.cloned.1.call-done = bf16[4,64,2048]{2,1,0:T(8,128)(2,1)} async-done(((bf16[4,256,2048]{2,1,0:T(8,128)(2,1)}), bf16[4,64,2048]{2,1,0:T(8,128)(2,1)}) %reduce-scatter.10.cloned.1.call-update) | async-done | bytes 1048592 | tf_op jit(solution)/shard_map/reduce_scatter | solution.py:37
  704.0 78.8 %all-gather.17.cloned.1.call-done = bf16[4,256,2048]{2,1,0:T(8,128)(2,1)} async-done(((bf16[4,64,2048]{2,1,0:T(8,128)(2,1)}), bf16[4,256,2048]{2,1,0:T(8,128)(2,1)}) %all-gather.17.cloned.1.call-update) | async-done | bytes 4194320 | tf_op jit(solution)/shard_map/all_gather | solution.py:33
  796.0 85.5 %while.47 = (s32[]{:T(128)}, bf16[4,512,4,4,256]{4,1,0,3,2:T(8,128)(2,1)}, s32[4]{0:T(128)S(1)}, s32[]{:T(128)}, s32[]{:T(128)}, /*index=5*/bf16[2048,4,4,128]{3...) while((s32[]{:T(128)}, ...), condition=%wide.region_23.24_spmd, body=%wide.region_20.23_spmd.sunk | while | flops 2179072768 | bytes 50780492 | solution.py:354
  797.3 20.6 %conditional.8 = (bf16[512,4,4,128]{3,0,2,1:T(8,128)(2,1)}, bf16[512,4,4,128]{3,0,2,1:T(8,128)(2,1)S(1)}) conditional(s32[]{:T(128)} %convert_element_type.415, () %tuple.167, (s32[]{:T(128)}, s32[]{:T(128)}, bf16[2048,4,4,128]{3,0,2,1:T(8,128)(2,1)}, bf16[256,4,4,128]{3,0,2,1:T(8,128)(2,1)S(1)}, f32[4,4,256]{2,1,0:T(4,128)S(1)}, ...), branch_computations={%region_21.21_spmd, %region_22.22_spmd} | conditional | flops 2170684160 | bytes 42391648 | solution.py:179
  797.3 6.3 fusion.68
  803.7 8.9 multiply_bitcast_fusion
  823.2 20.6 %conditional.8 = (bf16[512,4,4,128]{3,0,2,1:T(8,128)(2,1)}, bf16[512,4,4,128]{3,0,2,1:T(8,128)(2,1)S(1)}) conditional(s32[]{:T(128)} %convert_element_type.415, () %tuple.167, (s32[]{:T(128)}, s32[]{:T(128)}, bf16[2048,4,4,128]{3,0,2,1:T(8,128)(2,1)}, bf16[256,4,4,128]{3,0,2,1:T(8,128)(2,1)S(1)}, f32[4,4,256]{2,1,0:T(4,128)S(1)}, ...), branch_computations={%region_21.21_spmd, %region_22.22_spmd} | conditional | flops 2170684160 | bytes 42391648 | solution.py:179
  823.3 6.3 fusion.68
  829.7 8.9 multiply_bitcast_fusion
  849.2 20.6 %conditional.8 = (bf16[512,4,4,128]{3,0,2,1:T(8,128)(2,1)}, bf16[512,4,4,128]{3,0,2,1:T(8,128)(2,1)S(1)}) conditional(s32[]{:T(128)} %convert_element_type.415, () %tuple.167, (s32[]{:T(128)}, s32[]{:T(128)}, bf16[2048,4,4,128]{3,0,2,1:T(8,128)(2,1)}, bf16[256,4,4,128]{3,0,2,1:T(8,128)(2,1)S(1)}, f32[4,4,256]{2,1,0:T(4,128)S(1)}, ...), branch_computations={%region_21.21_spmd, %region_22.22_spmd} | conditional | flops 2170684160 | bytes 42391648 | solution.py:179
  849.3 6.3 fusion.68
  855.7 8.9 multiply_bitcast_fusion
  903.2 51.9 %while.46 = (s32[]{:T(128)}, f32[256,4,4,128]{3,0,2,1:T(8,128)S(1)}, s32[]{:T(128)}, s32[]{:T(128)}, bf16[2048,4,4,128]{3,0,2,1:T(8,128)(2,1)}, /*index=5*/bf16[...) while((s32[]{:T(128)}, ...), condition=%wide.region_19.20_spmd, body=%wide.region_16.19_spmd.sunk | while | flops 1624376064 | bytes 29662476 | solution.py:100
  903.3 19.0 %conditional.7 = (f32[256,4,4,128]{3,0,2,1:T(8,128)S(1)}) conditional(s32[]{:T(128)} %convert_element_type.414, f32[256,4,4,128]{3,0,2,1:T(8,128)S(1)} %get-tuple-element.1254, (s32[]{:T(128)}, s32[]{:T(128)}, bf16[2048,4,4,128]{3,0,2,1:T(8,128)(2,1)}, bf16[256,4,4,128]{3,0,2,1:T(8,128)(2,1)S(1)}, f32[4,4,256]{2,1,0:T(4,128)S(1)}, ...), branch_computations={%region_17.17_spmd, %region_18.18_spmd} | conditional | flops 1624376064 | bytes 29662262 | solution.py:148
  903.5 7.1 fusion.31
  910.6 11.7 bitcast_add_fusion
  922.3 16.6 %conditional.7 = (f32[256,4,4,128]{3,0,2,1:T(8,128)S(1)}) conditional(s32[]{:T(128)} %convert_element_type.414, f32[256,4,4,128]{3,0,2,1:T(8,128)S(1)} %get-tuple-element.1254, (s32[]{:T(128)}, s32[]{:T(128)}, bf16[2048,4,4,128]{3,0,2,1:T(8,128)(2,1)}, bf16[256,4,4,128]{3,0,2,1:T(8,128)(2,1)S(1)}, f32[4,4,256]{2,1,0:T(4,128)S(1)}, ...), branch_computations={%region_17.17_spmd, %region_18.18_spmd} | conditional | flops 1624376064 | bytes 29662262 | solution.py:148
  922.5 7.0 fusion.31
  929.5 9.3 bitcast_add_fusion
  938.9 16.2 %conditional.7 = (f32[256,4,4,128]{3,0,2,1:T(8,128)S(1)}) conditional(s32[]{:T(128)} %convert_element_type.414, f32[256,4,4,128]{3,0,2,1:T(8,128)S(1)} %get-tuple-element.1254, (s32[]{:T(128)}, s32[]{:T(128)}, bf16[2048,4,4,128]{3,0,2,1:T(8,128)(2,1)}, bf16[256,4,4,128]{3,0,2,1:T(8,128)(2,1)S(1)}, f32[4,4,256]{2,1,0:T(4,128)S(1)}, ...), branch_computations={%region_17.17_spmd, %region_18.18_spmd} | conditional | flops 1624376064 | bytes 29662262 | solution.py:148
  945.2 9.8 bitcast_add_fusion
  961.6 55.4 %reduce-scatter.12.cloned.1.call-done = bf16[256,4,4,256]{3,0,2,1:T(8,128)(2,1)} async-done(((bf16[2048,4,4,256]{3,0,2,1:T(8,128)(2,1)}), bf16[256,4,4,256]{3,0,2,1:T(8,128)(2,1)}) %reduce-scatter.12.cloned.1.call-update) | async-done | bytes 2097168 | tf_op jit(solution)/shard_map/reduce_scatter | solution.py:355
  1023.6 7.5 fusion.155
  1067.4 7.6 fusion.151
  1076.6 17.6 %fusion.83 = bf16[4,256,2048]{2,1,0:T(8,128)(2,1)} fusion(f32[256,4,2048]{2,0,1:T(8,128)} %fusion.155, f32[256,4,2048]{2,0,1:T(8,128)} %fusion.151, f32[4,256,2048]{2,1,0:T(8,128)} %fusion.203, f32[4,256,2048]{2,1,0:T(8,128)} %fusion.199, f32[4,256,2048]{2,1,0:T(8,128)} %fusion.201, bf16[3,2048,512]{2,1,0:T(8,128)(2,1)} %param.27, ...), kind=kOutput, calls=%fused_computation.83 | convolution fusion | flops 2166358016 | bytes 49283072 | tf_op jit(solution)/shard_map/csw,dw->scd/dot_general | solution.py:204
  1094.6 12.6 fusion.90
  1125.9 137.4 %all-reduce.5.cloned.1.call-done = (f32[4,5,16,2048]{3,0,2,1:T(4,128)}, f32[4,2,16,2048]{3,0,2,1:T(4,128)}) async-done(((f32[4,5,16,2048]{3,0,2,1:T(4,128)}, f32[4,2,16,2048]{3,0,2,1:T(4,128)}), (f32[4,5,16,2048]{3,0,2,1:T(4,128)}, f32[4,2,16,2048]{3,0,2,1:T(4,128)})) %all-reduce.5.cloned.1.call-update) | async-done | bytes 3670032 | tf_op jit(solution)/shard_map/psum | solution.py:407
  1269.8 74.0 %reduce-scatter.14.cloned.1.call-done = bf16[4,64,2048]{2,1,0:T(8,128)(2,1)} async-done(((bf16[4,256,2048]{2,1,0:T(8,128)(2,1)}), bf16[4,64,2048]{2,1,0:T(8,128)(2,1)}) %reduce-scatter.14.cloned.1.call-update) | async-done | bytes 1048592 | tf_op jit(solution)/shard_map/reduce_scatter | solution.py:37
  1345.9 77.5 %reduce-scatter.8.cloned.1.call-done = bf16[4,64,2048]{2,1,0:T(8,128)(2,1)} async-done(((bf16[4,256,2048]{2,1,0:T(8,128)(2,1)}), bf16[4,64,2048]{2,1,0:T(8,128)(2,1)}) %reduce-scatter.8.cloned.1.call-update) | async-done | bytes 1048592 | tf_op jit(solution)/shard_map/reduce_scatter | solution.py:37
  (391 shorter events, 316.6 us)
Async XLA Ops:
  7.2 252.7 %copy-start = (bf16[512,2048]{1,0:T(8,128)(2,1)S(1)}, bf16[512,2048]{1,0:T(8,128)(2,1)}, u32[]{:S(2)}) copy-start(bf16[512,2048]{1,0:T(8,128)(2,1)} %param.28) | copy-start | bytes 6291460
  7.2 5.9 copy-start.64
  7.2 6.1 copy-start.67
  7.2 85.4 %all-gather.7.cloned.1.call-start = ((), (), s32[]{:S(2)}) async-start(), calls=%async_computation.5 | async-start | bytes 5242880 | tf_op jit(solution)/shard_map/all_gather | solution.py:33
  13.1 147.7 %all-gather.11.cloned.1.call-start = ((), (), s32[]{:S(2)}) async-start(), calls=%async_computation.7 | async-start | bytes 9437184 | tf_op jit(solution)/shard_map/all_gather | solution.py:290
  13.7 114.5 %copy-start.52 = (bf16[1,4,48,512]{3,2,1,0:T(8,128)(2,1)}, bf16[1,4,48,512]{3,2,1,0:T(8,128)(2,1)S(1)}, u32[]{:S(2)}) copy-start(bf16[1,4,48,512]{3,2,1,0:T(8,128)(2,1)S(1)} %copy.208) | copy-start | bytes 589828
  105.0 112.5 %all-gather.9.cloned.1.call-start = ((), (), s32[]{:S(2)}) async-start(), calls=%async_computation.6 | async-start | bytes 9437184 | tf_op jit(solution)/shard_map/all_gather | solution.py:289
  105.3 5.7 copy-start.3
  107.2 33.7 %copy-start.31 = (f32[256,4,64]{2,0,1:T(8,128)}, f32[256,4,64]{2,0,1:T(8,128)S(1)}, u32[]{:S(2)}) copy-start(f32[256,4,64]{2,0,1:T(8,128)S(1)} %get-tuple-element.999) | copy-start | bytes 786436
  107.2 33.7 %copy-start.33 = (f32[256,4,64]{2,0,1:T(8,128)}, f32[256,4,64]{2,0,1:T(8,128)S(1)}, u32[]{:S(2)}) copy-start(f32[256,4,64]{2,0,1:T(8,128)S(1)} %get-tuple-element.1000) | copy-start | bytes 786436
  143.6 12.7 copy-start.69
  143.6 12.7 copy-start.60
  145.2 206.7 %reduce-scatter.6.cloned.1.call-start = ((), (), s32[]{:S(2)}) async-start(), calls=%async_computation.8 | async-start | bytes 5242880 | tf_op jit(solution)/shard_map/reduce_scatter | solution.py:37
  264.4 167.7 %all-gather.15.cloned.1.call-start = ((), (), s32[]{:S(2)}) async-start(), calls=%async_computation.11 | async-start | bytes 5242880 | tf_op jit(solution)/shard_map/all_gather | solution.py:33
  265.0 92.4 %copy-start.63 = (bf16[4,16,2048]{2,1,0:T(8,128)(2,1)S(1)}, bf16[4,16,2048]{2,1,0:T(8,128)(2,1)}, u32[]{:S(2)}) copy-start(bf16[4,16,2048]{2,1,0:T(8,128)(2,1)} %param.35) | copy-start | bytes 786436
  265.1 248.6 %all-gather.13.cloned.1.call-start = ((), (), s32[]{:S(2)}) async-start(), calls=%async_computation.9 | async-start | bytes 5242880 | tf_op jit(solution)/shard_map/all_gather | solution.py:33
  353.9 345.2 %copy-start.65 = (f32[4,64]{1,0:T(4,128)}, f32[4,64]{1,0:T(4,128)S(1)}, u32[]{:S(2)}) copy-start(f32[4,64]{1,0:T(4,128)S(1)} %broadcast_multiply_fusion.4) | copy-start | bytes 3076
  356.0 343.1 %copy-start.70 = (f32[4,64]{1,0:T(4,128)}, f32[4,64]{1,0:T(4,128)S(1)}, u32[]{:S(2)}) copy-start(f32[4,64]{1,0:T(4,128)S(1)} %add_rsqrt_fusion) | copy-start | bytes 3076
  357.4 338.9 %reduce-scatter.10.cloned.1.call-start = ((), (), s32[]{:S(2)}) async-start(), calls=%async_computation.12 | async-start | bytes 5242880 | tf_op jit(solution)/shard_map/reduce_scatter | solution.py:37
  361.1 78.1 %copy-start.36 = (bf16[4,32768]{1,0:T(4,128)(2,1)}, bf16[4,32768]{1,0:T(4,128)(2,1)S(1)}, u32[]{:S(2)}) copy-start(bf16[4,32768]{1,0:T(4,128)(2,1)S(1)} %convolution_convert_fusion.3) | copy-start | bytes 786436
  570.5 14.9 %copy-start.40 = (f32[4,256,16]{1,2,0:T(8,128)}, f32[4,256,16]{1,2,0:T(8,128)S(1)}, u32[]{:S(2)}) copy-start(f32[4,256,16]{1,2,0:T(8,128)S(1)} %fusion.211) | copy-start | bytes 196612
  570.5 13.7 copy-start.16
  570.5 13.7 copy-start.30
  585.5 6.7 copy-start.42
  618.4 164.5 %all-gather.17.cloned.1.call-start = ((), (), s32[]{:S(2)}) async-start(), calls=%async_computation.13 | async-start | bytes 5242880 | tf_op jit(solution)/shard_map/all_gather | solution.py:33
  699.1 87.3 %copy-start.76 = (f32[4,64]{1,0:T(4,128)}, f32[4,64]{1,0:T(4,128)S(1)}, u32[]{:S(2)}) copy-start(f32[4,64]{1,0:T(4,128)S(1)} %broadcast_multiply_fusion.3) | copy-start | bytes 3076
  704.0 313.0 %reduce-scatter.12.cloned.1.call-start = ((), (), s32[]{:S(2)}) async-start(), calls=%async_computation.14 | async-start | bytes 18874368 | tf_op jit(solution)/shard_map/reduce_scatter | solution.py:355
  797.3 6.4 copy-start.38
  823.3 6.4 copy-start.38
  849.2 6.4 copy-start.38
  881.5 236.8 %all-reduce.7.cloned.1.call-start = ((), (), s32[]{:S(2)}) async-start(), calls=%async_computation.17 | async-start | bytes 2097152 | tf_op jit(solution)/shard_map/psum | solution.py:398
  903.2 51.9 %copy-start.59 = (f32[4,256,16]{1,2,0:T(8,128)S(1)}, f32[4,256,16]{1,2,0:T(8,128)}, u32[]{:S(2)}) copy-start(f32[4,256,16]{1,2,0:T(8,128)} %copy-done.58) | copy-start | bytes 196612
  958.2 60.8 %copy-start.32 = (f32[256,4,64]{2,0,1:T(8,128)S(1)}, f32[256,4,64]{2,0,1:T(8,128)}, u32[]{:S(2)}) copy-start(f32[256,4,64]{2,0,1:T(8,128)} %copy-done.31) | copy-start | bytes 786436
  958.2 60.8 %copy-start.34 = (f32[256,4,64]{2,0,1:T(8,128)S(1)}, f32[256,4,64]{2,0,1:T(8,128)}, u32[]{:S(2)}) copy-start(f32[256,4,64]{2,0,1:T(8,128)} %copy-done.33) | copy-start | bytes 786436
  1023.5 7.5 copy-start.25
  1023.5 7.5 copy-start.62
  1063.0 200.3 %all-reduce.5.cloned.1.call-start = ((), (), s32[]{:S(2)}) async-start(), calls=%async_computation.16 | async-start | bytes 7340032 | tf_op jit(solution)/shard_map/psum | solution.py:407
  1075.1 268.7 %reduce-scatter.14.cloned.1.call-start = ((), (), s32[]{:S(2)}) async-start(), calls=%async_computation.15 | async-start | bytes 5242880 | tf_op jit(solution)/shard_map/reduce_scatter | solution.py:37
  1094.2 12.9 copy-start.28
  1094.2 329.1 %reduce-scatter.8.cloned.1.call-start = ((), (), s32[]{:S(2)}) async-start(), calls=%async_computation.10 | async-start | bytes 5242880 | tf_op jit(solution)/shard_map/reduce_scatter | solution.py:37
  1123.5 220.3 %copy-start.9 = (bf16[4,64,2048]{2,1,0:T(8,128)(2,1)S(1)}, bf16[4,64,2048]{2,1,0:T(8,128)(2,1)}, u32[]{:S(2)}) copy-start(bf16[4,64,2048]{2,1,0:T(8,128)(2,1)} %param.26) | copy-start | bytes 3145732
  1123.5 220.3 %copy-start.73 = (f32[4,64]{1,0:T(4,128)S(1)}, f32[4,64]{1,0:T(4,128)}, u32[]{:S(2)}) copy-start(f32[4,64]{1,0:T(4,128)} %copy-done.72) | copy-start | bytes 3076
  1123.5 220.3 %copy-start.75 = (f32[4,64]{1,0:T(4,128)S(1)}, f32[4,64]{1,0:T(4,128)}, u32[]{:S(2)}) copy-start(f32[4,64]{1,0:T(4,128)} %copy-done.74) | copy-start | bytes 3076
  1263.3 160.0 %copy-start.66 = (f32[4,64]{1,0:T(4,128)S(1)}, f32[4,64]{1,0:T(4,128)}, u32[]{:S(2)}) copy-start(f32[4,64]{1,0:T(4,128)} %copy-done.65) | copy-start | bytes 3076
  1263.3 160.0 %copy-start.71 = (f32[4,64]{1,0:T(4,128)S(1)}, f32[4,64]{1,0:T(4,128)}, u32[]{:S(2)}) copy-start(f32[4,64]{1,0:T(4,128)} %copy-done.70) | copy-start | bytes 3076
  1263.3 160.0 %copy-start.77 = (f32[4,64]{1,0:T(4,128)S(1)}, f32[4,64]{1,0:T(4,128)}, u32[]{:S(2)}) copy-start(f32[4,64]{1,0:T(4,128)} %copy-done.76) | copy-start | bytes 3076
  1263.4 160.0 %copy-start.79 = (f32[4,64]{1,0:T(4,128)S(1)}, f32[4,64]{1,0:T(4,128)}, u32[]{:S(2)}) copy-start(f32[4,64]{1,0:T(4,128)} %copy-done.78) | copy-start | bytes 3076
  1345.9 82.5 %copy-start.1 = (bf16[512,2048]{1,0:T(8,128)(2,1)S(1)}, bf16[512,2048]{1,0:T(8,128)(2,1)}, u32[]{:S(2)}) copy-start(bf16[512,2048]{1,0:T(8,128)(2,1)} %param.28) | copy-start | bytes 6291460
  (52 other events, 160.0 us)
Sparse Core Ops, SparseCore 0:
  13.2 79.4 all-gather.6
  105.1 55.4 all-gather.10
  163.1 54.3 all-gather.8
  264.6 87.2 reduce-scatter.5
  353.4 78.7 all-gather.14
  434.2 79.3 all-gather.12
  618.5 77.7 reduce-scatter.9
  704.1 78.7 all-gather.16
  881.7 135.2 reduce-scatter.11
  1063.2 55.1 all-reduce.6
  1124.6 138.6 all-reduce.4
  1265.6 78.1 reduce-scatter.13
  1346.1 77.2 reduce-scatter.7
where the time goes:
time: 1440 us
  waiting for transfers between devices  847 us (59%)
  matrix products  415 us (29%)
  local copies, waits for them, and re-layouts  77.3 us (5%)
  other arithmetic  65.1 us (5%)
  between operations  15.4 us (1%)
    reduce_scatter x4, waiting for transfers between devices, scatter_rows(): lax.psum_scatter(values.astype(jnp.bfloat16), 'mp', scatter_dimension=1,...  315 us
    all_gather x4, waiting for transfers between devices, gather_rows(): return lax.all_gather(values, 'mp', axis=1, tiled=True)  284 us
    psum x1, waiting for transfers between devices, per_device(): lax.psum((spread_sets(onehot, per_seq_a_in), spread_sets(onehot, per_seq_...  137 us
    dot_general x5, matrix products, back_in(): jnp.einsum('csw,dw->scd', gradient, weight, preferred_element_type=jnp.fl...  65.8 us
    reduce_scatter x1, waiting for transfers between devices, per_device(): lax.psum_scatter(stacked.reshape((local_len * lax.axis_size('seq'),) + st...  55.4 us
    dot_general x5, matrix products, project_in(): jnp.einsum('scd,dw->csw', token_rows, weight, preferred_element_type=jnp....  50.3 us
    dot_general x9, matrix products, masked_scores(): jnp.einsum('qshd,kshd->shqk', queries, key_rows, preferred_element_type=j...  48 us
    all_gather x1, waiting for transfers between devices, per_device(): lax.all_gather(key_rows, 'seq', axis=0, tiled=True)  47.8 us
  transfers between devices with their start and end apart: 13, of which 12 were waited for; matrix products, arithmetic and copies ran while one was open for 16% of the time, Pallas kernels for 0%

commit v1 on v0

--- a/solution.py
+++ b/solution.py
@@ -3,6 +3,8 @@
 import jax
 import jax.numpy as jnp
 from jax import lax
+from jax.experimental import pallas as pl
+from jax.experimental.pallas import tpu as pltpu
 from jax.sharding import PartitionSpec as P
 
 HDIM = 128
@@ -419,7 +421,1357 @@
     )
 
 
+log2e = 1.4426950408889634
+attn_tile = 512
+hidden_tile = 512
+
+
+def dot_nt(a, b):
+    return lax.dot_general(a, b, (((1,), (1,)), ((), ())), preferred_element_type=jnp.float32)
+
+
+def dot_tn(a, b):
+    return lax.dot_general(a, b, (((0,), (0,)), ((), ())), preferred_element_type=jnp.float32)
+
+
+def dot_nn(a, b):
+    return jnp.dot(a, b, preferred_element_type=jnp.float32)
+
+
+def causal(block_t, first_row, first_col):
+    rows = first_row + lax.broadcasted_iota(jnp.int32, block_t.shape, 0)
+    cols = first_col + lax.broadcasted_iota(jnp.int32, block_t.shape, 1)
+    return rows <= cols
+
+
+def attend_kernel(q_ref, k_ref, v_ref, o_ref, lse_ref):
+    i = pl.program_id(1)
+    tile = q_ref.shape[0]
+    factor = log2e / math.sqrt(HDIM)
+    q = q_ref[...]
+
+    def fold(j, carry, diagonal):
+        top, total, acc = carry
+        at = pl.ds(pl.multiple_of(j * tile, tile), tile)
+        scores = dot_nt(k_ref[at, :], q)
+        if diagonal:
+            scores = jnp.where(causal(scores, 0, 0), scores, far_below)
+        new_top = jnp.maximum(top, jnp.max(scores, axis=0, keepdims=True))
+        weight = jnp.exp2(scores * factor - new_top * factor)
+        keep = jnp.exp2((top - new_top) * factor)
+        total = total * keep + jnp.sum(weight, axis=0, keepdims=True)
+        acc = acc * keep + dot_tn(v_ref[at, :], weight.astype(jnp.bfloat16))
+        return (new_top, total, acc)
+
+    carry = (
+        jnp.full((1, tile), far_below, jnp.float32),
+        jnp.zeros((1, tile), jnp.float32),
+        jnp.zeros((HDIM, tile), jnp.float32),
+    )
+    carry = lax.fori_loop(0, i, lambda j, c: fold(j, c, False), carry)
+    top, total, acc = fold(i, carry, True)
+    o_ref[...] = jnp.transpose(acc / total).astype(o_ref.dtype)
+    lse_ref[0] = top * factor + jnp.log2(total)
+
+
+def attend(q, k, v):
+    length = q.shape[0]
+    heads = q.shape[1] // HDIM
+    tile = attn_tile
+    return pl.pallas_call(
+        attend_kernel,
+        grid=(heads, length // tile),
+        in_specs=[
+            pl.BlockSpec((tile, HDIM), lambda h, i: (i, h)),
+            pl.BlockSpec((length, HDIM), lambda h, i: (0, h)),
+            pl.BlockSpec((length, HDIM), lambda h, i: (0, h)),
+        ],
+        out_specs=[
+            pl.BlockSpec((tile, HDIM), lambda h, i: (i, h)),
+            pl.BlockSpec((1, 1, tile), lambda h, i: (h, 0, i)),
+        ],
+        out_shape=[
+            jax.ShapeDtypeStruct(q.shape, jnp.bfloat16),
+            jax.ShapeDtypeStruct((heads, 1, length), jnp.float32),
+        ],
+        cost_estimate=pl.CostEstimate(
+            flops=2 * heads * length * length * HDIM,
+            bytes_accessed=8 * length * heads * HDIM,
+            transcendentals=heads * length * length // 2,
+        ),
+        compiler_params=pltpu.CompilerParams(vmem_limit_bytes=32 << 20),
+    )(q, k, v)
+
+
+def turn_back(gradient, cos, sin):
+    return gradient * cos + pltpu.roll(gradient, HDIM // 2, 1) * sin
+
+
+def attend_back_kernel(
+    q_ref, k_ref, v_ref, go_ref, lse_ref, dots_ref, cos_ref, sin_ref, dq_ref, dk_ref, dv_ref, acc_ref
+):
+    j = pl.program_id(1)
+    tile = k_ref.shape[0]
+    length = q_ref.shape[0]
+    scale = 1.0 / math.sqrt(HDIM)
+    factor = log2e * scale
+    k = k_ref[...]
+    v = v_ref[...]
+
+    @pl.when(j == 0)
+    def _():
+        acc_ref[...] = jnp.zeros_like(acc_ref)
+
+    def fold(i, carry, diagonal):
+        dk, dv = carry
+        at = pl.ds(pl.multiple_of(i * tile, tile), tile)
+        q = q_ref[at, :]
+        go = go_ref[at, :]
+        scores = dot_nt(k, q)
+        weight = jnp.exp2(scores * factor - lse_ref[0, :, at])
+        if diagonal:
+            weight = jnp.where(causal(scores, 0, 0), weight, 0.0)
+        grad_weight = dot_nt(v, go)
+        grad_scores = (weight * (grad_weight - dots_ref[0, :, at])).astype(jnp.bfloat16)
+        dv = dv + dot_nn(weight.astype(jnp.bfloat16), go)
+        dk = dk + dot_nn(grad_scores, q)
+        acc_ref[at, :] += dot_tn(grad_scores, k)
+        return (dk, dv)
+
+    zero = jnp.zeros((tile, HDIM), jnp.float32)
+    carry = fold(j, (zero, zero), True)
+    dk, dv = lax.fori_loop(j + 1, length // tile, lambda i, c: fold(i, c, False), carry)
+    at = pl.ds(pl.multiple_of(j * tile, tile), tile)
+    dk_ref[...] = turn_back(dk * scale, cos_ref[at, :], sin_ref[at, :]).astype(dk_ref.dtype)
+    dv_ref[...] = dv.astype(dv_ref.dtype)
+    dq_ref[...] = turn_back(acc_ref[at, :] * scale, cos_ref[at, :], sin_ref[at, :]).astype(dq_ref.dtype)
+
+
+def attend_back(q, k, v, go, lse, dots, cos, sin):
+    length = q.shape[0]
+    heads = q.shape[1] // HDIM
+    tile = attn_tile
+    whole = pl.BlockSpec((length, HDIM), lambda h, j: (0, h))
+    part = pl.BlockSpec((tile, HDIM), lambda h, j: (j, h))
+    row = pl.BlockSpec((1, 1, length), lambda h, j: (h, 0, 0))
+    table = pl.BlockSpec((length, HDIM), lambda h, j: (0, 0))
+    return pl.pallas_call(
+        attend_back_kernel,
+        grid=(heads, length // tile),
+        in_specs=[whole, part, part, whole, row, row, table, table],
+        out_specs=[part, part, part],
+        out_shape=[jax.ShapeDtypeStruct(q.shape, jnp.bfloat16)] * 3,
+        scratch_shapes=[pltpu.VMEM((length, HDIM), jnp.float32)],
+        cost_estimate=pl.CostEstimate(
+            flops=5 * heads * length * length * HDIM,
+            bytes_accessed=14 * length * heads * HDIM,
+            transcendentals=heads * length * length // 2,
+        ),
+        compiler_params=pltpu.CompilerParams(vmem_limit_bytes=32 << 20),
+    )(q, k, v, go, lse, dots, cos, sin)
+
+
+mesh_ids = pl.DeviceIdType.MESH
+
+
+def remote(src, dst, send, recv, target):
+    return pltpu.make_async_remote_copy(
+        src_ref=src, dst_ref=dst, send_sem=send, recv_sem=recv, device_id=target, device_id_type=mesh_ids
+    )
+
+
+def meet(partners):
+    barrier = pltpu.get_barrier_semaphore()
+    for condition, device in partners:
+        if condition is None:
+            pl.semaphore_signal(barrier, inc=1, device_id=device, device_id_type=mesh_ids)
+        else:
+
+            @pl.when(condition)
+            def _():
+                pl.semaphore_signal(barrier, inc=1, device_id=device, device_id_type=mesh_ids)
+
+    count = 0
+    for condition, device in partners:
+        count = count + (1 if condition is None else condition.astype(jnp.int32))
+    pl.semaphore_wait(barrier, count)
+
+
+def flip(index, bit):
+    return index + bit - 2 * bit * ((index // bit) % 2)
+
+
+def places():
+    s = lax.axis_index("seq")
+    z = lax.axis_index("mp")
+    return s, z
+
+
+class Gather:
+    def __init__(self, blocks, s, z, send, recv, half):
+        self.at = blocks
+        self.s = s
+        self.z = z
+        self.send = send
+        self.recv = recv
+        self.half = half
+
+    def rows(self, part):
+        return pl.ds(part * self.half, self.half)
+
+    def copy(self, index, span, part, target):
+        ref = self.at.at[span] if part is None else self.at.at[span, self.rows(part)]
+        return remote(ref, ref, self.send.at[index], self.recv.at[index], (target, self.z))
+
+    def begin(self):
+        s, x, y, other = self.s, flip(self.s, 2), flip(self.s, 4), flip(self.s, 1)
+        self.copies = [
+            self.copy(0, s, 0, x),
+            self.copy(1, s, 1, y),
+            self.copy(2, s, 1, x),
+            self.copy(3, s, 0, y),
+            self.copy(6, s, None, other),
+        ]
+        for one in self.copies:
+            one.start()
+
+    def arrive_first(self):
+        s, x, y = self.s, flip(self.s, 2), flip(self.s, 4)
+        self.copy(0, x, 0, x).wait_recv()
+        one = self.copy(4, x, 0, y)
+        one.start()
+        self.copy(1, y, 1, y).wait_recv()
+        two = self.copy(5, y, 1, x)
+        two.start()
+        self.copies += [one, two]
+
+    def arrive_neighbours(self):
+        s, x, y, other = self.s, flip(self.s, 2), flip(self.s, 4), flip(self.s, 1)
+        self.copy(2, x, 1, x).wait_recv()
+        one = self.copy(7, x, None, other)
+        one.start()
+        self.copy(3, y, 0, y).wait_recv()
+        two = self.copy(8, y, None, other)
+        two.start()
+        self.copies += [one, two]
+
+    def arrive_diagonal(self):
+        s, other = self.s, flip(self.s, 1)
+        diagonal = flip(flip(s, 2), 4)
+        self.copy(4, diagonal, 0, other).wait_recv()
+        self.copy(5, diagonal, 1, other).wait_recv()
+        one = self.copy(9, diagonal, None, other)
+        one.start()
+        self.copies += [one]
+
+    def arrive_core(self, index):
+        s = self.s
+        other = flip(s, 1)
+        span = (other, flip(other, 2), flip(other, 4), flip(flip(other, 2), 4))[index]
+        self.copy(6 + index, span, None, other).wait_recv()
+        return span
+
+    def end(self):
+        for one in self.copies:
+            one.wait_send()
+
+
+gather_sems = 10
+
+
+def spend(microseconds):
+    return pl.CostEstimate(flops=microseconds * 10**9, bytes_accessed=10**6, transcendentals=0)
+
+
+class Line:
+    def __init__(self, blocks, core, s, z, send, recv):
+        self.at = blocks
+        self.core = core
+        self.s = s
+        self.z = z
+        self.send = send
+        self.recv = recv
+
+    def ref(self, j):
+        return self.at.at[j, self.core]
+
+    def up(self, hop, j):
+        ref = self.ref(j)
+        return remote(ref, ref, self.send.at[hop], self.recv.at[hop], (self.s, self.z + 1))
+
+    def down(self, hop, j):
+        ref = self.ref(j)
+        return remote(ref, ref, self.send.at[3 + hop], self.recv.at[3 + hop], (self.s, self.z - 1))
+
+    def across(self, index, j):
+        ref = self.ref(j)
+        return remote(ref, ref, self.send.at[6 + index], self.recv.at[6 + index], (flip(self.s, 1), self.z))
+
+    def begin(self):
+        z = self.z
+
+        @pl.when(z < 3)
+        def _():
+            self.up(0, z).start()
+
+        @pl.when(z > 0)
+        def _():
+            self.down(0, z).start()
+
+        self.across(0, z).start()
+
+    def hop(self, t):
+        z = self.z
+
+        @pl.when(z >= t)
+        def _():
+            self.up(t - 1, z - t).wait_recv()
+            self.across(t, z - t).start()
+            if t < 3:
+
+                @pl.when(z < 3)
+                def _():
+                    self.up(t, z - t).start()
+
+        @pl.when(z + t <= 3)
+        def _():
+            self.down(t - 1, z + t).wait_recv()
+            self.across(3 + t, z + t).start()
+            if t < 3:
+
+                @pl.when(z > 0)
+                def _():
+                    self.down(t, z + t).start()
+
+    def arrive_core(self):
+        z = self.z
+        other = 1 - self.core
+
+        def wait(index, j):
+            ref = self.at.at[j, other]
+            remote(ref, ref, self.send.at[6 + index], self.recv.at[6 + index], (flip(self.s, 1), z)).wait_recv()
+
+        wait(0, z)
+        for t in (1, 2, 3):
+
+            @pl.when(z >= t)
+            def _():
+                wait(t, z - t)
+
+            @pl.when(z + t <= 3)
+            def _():
+                wait(3 + t, z + t)
+
+    def end(self):
+        z = self.z
+
+        @pl.when(z < 3)
+        def _():
+            self.up(0, z).wait_send()
+
+        @pl.when(z > 0)
+        def _():
+            self.down(0, z).wait_send()
+
+        self.across(0, z).wait_send()
+        for t in (1, 2, 3):
+
+            @pl.when(z >= t)
+            def _():
+                self.across(t, z - t).wait_send()
+                if t < 3:
+
+                    @pl.when(z < 3)
+                    def _():
+                        self.up(t, z - t).wait_send()
+
+            @pl.when(z + t <= 3)
+            def _():
+                self.across(3 + t, z + t).wait_send()
+                if t < 3:
+
+                    @pl.when(z > 0)
+                    def _():
+                        self.down(t, z + t).wait_send()
+
+
+line_sems = 13
+
+
+def norm_rows(values):
+    centred = values - jnp.mean(values, axis=-1, keepdims=True)
+    inverse = lax.rsqrt(jnp.mean(centred * centred, axis=-1, keepdims=True) + norm_eps)
+    return (centred * inverse, inverse)
+
+
+def start_kernel(
+    x_ref, w_ref, o_ref, cos_ref, sin_ref, a_ref, set_ref,
+    x_own_ref, n_own_ref, u_out, w_all, o_all, q_ref, k_ref, v_ref, low_ref, b_sel_ref, a_sel_ref,
+    u_ref, w_buf, w_big, a2a_send, a2a_recv, ag_send, ag_recv, w_send, w_recv, o_send, o_recv, local_sem,
+):
+    s, z = places()
+    core = s % 2
+    other = flip(s, 1)
+    zs = [flip(z, 1), flip(z, 2), 3 - z]
+    meet([(None, (other, z)), (None, (flip(s, 2), z)), (None, (flip(s, 4), z))] + [(None, (s, j)) for j in zs])
+
+    swaps = [
+        remote(x_ref.at[j], x_own_ref.at[z], a2a_send.at[d], a2a_recv.at[d], (s, j)) for d, j in enumerate(zs)
+    ]
+    for one in swaps:
+        one.start()
+    x_own_ref[z] = x_ref[z]
+    w_buf[z, core] = w_ref[...]
+    own_o = pltpu.make_async_copy(o_ref, o_all.at[z, core], local_sem.at[8])
+    own_o.start()
+    for d, j in enumerate(zs):
+        remote(x_ref.at[j], x_own_ref.at[j], a2a_send.at[d], a2a_recv.at[d], (s, j)).wait_recv()
+    line = Line(w_buf, core, s, z, w_send, w_recv)
+    line.begin()
+    for part in range(4):
+        normed, _ = norm_rows(x_own_ref[part].astype(jnp.float32))
+        normed = normed.astype(jnp.bfloat16)
+        n_own_ref[pl.ds(part * 64, 64), :] = normed
+        u_ref[s, pl.ds(part * 64, 64), :] = normed
+    gather = Gather(u_ref, s, z, ag_send, ag_recv, 128)
+    gather.begin()
+    gather.arrive_first()
+    line.hop(1)
+    gather.arrive_neighbours()
+    line.hop(2)
+    gather.arrive_diagonal()
+    for index in range(4):
+        gather.arrive_core(index)
+    stores = [pltpu.make_async_copy(u_ref.at[t], u_out.at[t], local_sem.at[t]) for t in range(8)]
+    for one in stores:
+        one.start()
+    a48 = a_ref[...]
+
+    def lows(t, _):
+        low_ref[t] = (adapt_scale * dot_nt(u_ref[t], a48)).astype(jnp.bfloat16)
+        return 0
+
+    lax.fori_loop(0, 8, lows, 0)
+    line.hop(3)
+    own_o.wait()
+    o_line = Line(o_all, core, s, z, o_send, o_recv)
+    o_line.begin()
+    line.arrive_core()
+    keep = pltpu.make_async_copy(w_buf, w_all, local_sem.at[9])
+    keep.start()
+    mine = set_ref[0]
+    for j in range(4):
+        table = w_buf[j, 0, 3072:, :]
+        picked = jnp.zeros((48, HDIM), jnp.bfloat16)
+        picked_a = jnp.zeros((16, HDIM), jnp.bfloat16)
+        for member in range(4):
+            picked = jnp.where(mine == member, table[48 * member : 48 * member + 48], picked)
+            picked_a = jnp.where(mine == member, table[192 + 16 * member : 208 + 16 * member], picked_a)
+        b_sel_ref[j] = picked
+        a_sel_ref[j] = picked_a
+    for part in range(3):
+        for head in range(2):
+            columns = pl.ds((2 * part + head) * HDIM, HDIM)
+            for side in range(2):
+                w_big[pl.ds(side * 1024, 1024), columns] = w_buf[
+                    2 * core + head, side, pl.ds(part * 1024, 1024), :
+                ]
+    b_two = [
+        jnp.concatenate(
+            [b_sel_ref[2 * core, 16 * part : 16 * part + 16], b_sel_ref[2 * core + 1, 16 * part : 16 * part + 16]],
+            axis=1,
+        )
+        for part in range(3)
+    ]
+
+    def project(t, _):
+        u = u_ref[t]
+        low = low_ref[t]
+        cos = cos_ref[pl.ds(pl.multiple_of(t * 256, 256), 256), :]
+        sin = sin_ref[pl.ds(pl.multiple_of(t * 256, 256), 256), :]
+        for part, out in enumerate((q_ref, k_ref, v_ref)):
+            raw = dot_nn(u, w_big[:, 256 * part : 256 * part + 256]) + dot_nn(
+                low[:, 16 * part : 16 * part + 16], b_two[part]
+            )
+            for head in range(2):
+                piece = raw[:, HDIM * head : HDIM * head + HDIM]
+                if part < 2:
+                    piece = piece * cos - pltpu.roll(piece, HDIM // 2, 1) * sin
+                out[t, :, pl.ds(HDIM * head, HDIM)] = piece.astype(jnp.bfloat16)
+        return 0
+
+    lax.fori_loop(0, 3, project, 0)
+    o_line.hop(1)
+    lax.fori_loop(3, 6, project, 0)
+    o_line.hop(2)
+    lax.fori_loop(6, 8, project, 0)
+    o_line.hop(3)
+    o_line.arrive_core()
+    for one in stores:
+        one.wait()
+    keep.wait()
+    for one in swaps:
+        one.wait_send()
+    line.end()
+    o_line.end()
+    gather.end()
+
+
+def start_layer(x, w_pack, o_pack, cos, sin, a48, my_set):
+    bf16 = jnp.bfloat16
+    vmem = pl.BlockSpec(memory_space=pltpu.VMEM)
+    anywhere = pl.BlockSpec(memory_space=pl.ANY)
+    width = x.shape[2]
+    rows = w_pack.shape[0]
+    shape = jax.ShapeDtypeStruct
+    dma = pltpu.SemaphoreType.DMA
+    return pl.pallas_call(
+        start_kernel,
+        in_specs=[vmem, vmem, anywhere, vmem, vmem, vmem, pl.BlockSpec(memory_space=pltpu.SMEM)],
+        out_specs=[vmem, vmem, anywhere, anywhere, anywhere, vmem, vmem, vmem, vmem, vmem, vmem],
+        out_shape=[
+            shape((4, 64, width), bf16),
+            shape((256, width), bf16),
+            shape((8, 256, width), bf16),
+            shape((4, 2, rows, HDIM), bf16),
+            shape((4, 2, HDIM, width // 2), bf16),
+            shape((8, 256, 256), bf16),
+            shape((8, 256, 256), bf16),
+            shape((8, 256, 256), bf16),
+            shape((8, 256, 48), bf16),
+            shape((4, 48, HDIM), bf16),
+            shape((4, 16, HDIM), bf16),
+        ],
+        scratch_shapes=[
+            pltpu.VMEM((8, 256, width), bf16),
+            pltpu.VMEM((4, 2, rows, HDIM), bf16),
+            pltpu.VMEM((width, 768), bf16),
+            dma((3,)),
+            dma((3,)),
+            dma((gather_sems,)),
+            dma((gather_sems,)),
+            dma((line_sems,)),
+            dma((line_sems,)),
+            dma((line_sems,)),
+            dma((line_sems,)),
+            dma((10,)),
+        ],
+        cost_estimate=spend(80),
+        compiler_params=pltpu.CompilerParams(
+            collective_id=1, has_side_effects=True, vmem_limit_bytes=56 << 20
+        ),
+    )(x, w_pack, o_pack, cos, sin, a48, my_set)
+
+
+class Reduce:
+    def __init__(self, product, s, z, out, inn, send, recv):
+        self.product = product
+        self.s = s
+        self.z = z
+        self.out = out
+        self.inn = inn
+        self.send = send
+        self.recv = recv
+        chip = s // 2
+        self.chip = chip
+        self.cx = flip(chip, 1)
+        self.cy = flip(chip, 2)
+        self.cd = flip(self.cx, 2)
+
+    def copy(self, index):
+        target = flip(self.s, 2) if index in (0, 2, 5) else flip(self.s, 4)
+        return remote(
+            self.out.at[index], self.inn.at[index], self.send.at[index], self.recv.at[index], (target, self.z)
+        )
+
+    def give(self, index, chip, half, extra=None):
+        value = self.product(chip, half)
+        if extra is not None:
+            self.copy(extra).wait_recv()
+            value = value + self.inn[extra].astype(jnp.float32)
+        self.out[index] = value.astype(jnp.bfloat16)
+        self.copy(index).start()
+
+    def begin(self):
+        self.give(0, self.cd, 0)
+        self.give(1, self.cd, 1)
+        self.give(2, self.cx, 0)
+        self.give(3, self.cy, 1)
+
+    def middle(self):
+        self.give(4, self.cy, 0, 0)
+        self.give(5, self.cx, 1, 1)
+
+    def finish(self, half):
+        indices = (2, 4) if half == 0 else (3, 5)
+        total = self.product(self.chip, half)
+        for index in indices:
+            self.copy(index).wait_recv()
+            total = total + self.inn[index].astype(jnp.float32)
+        return total
+
+    def end(self):
+        for index in range(6):
+            self.copy(index).wait_send()
+
+
+def out_kernel(
+    mixed_ref, o_all, a_sel_ref, b_ref, w_all, a48_ref, b_sel_ref, x_own_ref,
+    residual_ref, m_own_ref, o_eff_ref, w_cat_ref,
+    sib_ref, out_buf, in_buf, o_big, w_buf, sib_send, sib_recv, send, recv, local_sem,
+):
+    s, z = places()
+    core = s % 2
+    other = flip(s, 1)
+    meet([(None, (other, z)), (None, (flip(s, 2), z)), (None, (flip(s, 4), z))])
+    swaps = [
+        remote(
+            mixed_ref.at[2 * c + 1 - core], sib_ref.at[c], sib_send.at[c], sib_recv.at[c], (other, z)
+        )
+        for c in range(4)
+    ]
+    for one in swaps:
+        one.start()
+    load_w = pltpu.make_async_copy(w_all, w_buf, local_sem.at[0])
+    load_w.start()
+    for j in range(4):
+        head = (2 * core + j) % 4
+        merged = adapt_scale * dot_tn(a_sel_ref[head], b_ref[...])
+        for side in range(2):
+            o_big[pl.ds(j * HDIM, HDIM), pl.ds(side * 1024, 1024)] = (
+                o_all[head, side].astype(jnp.float32) + merged[:, side * 1024 : side * 1024 + 1024]
+            ).astype(jnp.bfloat16)
+    o_eff_ref[...] = o_big[0 : 2 * HDIM, :]
+    for one in swaps:
+        one.wait_recv()
+
+    def product(chip, half):
+        rows = pl.ds(half * 128, 128)
+        both = jnp.concatenate([mixed_ref[2 * chip + core, rows, :], sib_ref[chip, rows, :]], axis=1)
+        return dot_nn(both, o_big[...])
+
+    reduce = Reduce(product, s, z, out_buf, in_buf, send, recv)
+    reduce.begin()
+    load_w.wait()
+
+    def merge(index, _):
+        j = index // 3
+        part = index % 3
+        head = (2 * core + j) % 4
+        b_part = b_sel_ref[head, pl.ds(pl.multiple_of(part * 16, 16), 16), :]
+        a_part = a48_ref[pl.ds(pl.multiple_of(part * 16, 16), 16), :]
+        column = pl.multiple_of(((j // 2) * 6 + part * 2 + j % 2) * HDIM, HDIM)
+        for side in range(2):
+            merged = adapt_scale * dot_tn(a_part[:, side * 1024 : side * 1024 + 1024], b_part)
+            w_cat_ref[pl.ds(side * 1024, 1024), pl.ds(column, HDIM)] = (
+                w_buf[head, side, pl.ds(pl.multiple_of(part * 1024, 1024), 1024), :].astype(jnp.float32)
+                + merged
+            ).astype(jnp.bfloat16)
+        return 0
+
+    lax.fori_loop(0, 4, merge, 0)
+    reduce.middle()
+    lax.fori_loop(4, 12, merge, 0)
+    for half in range(2):
+        total = reduce.finish(half)
+        x = x_own_ref[2 * half : 2 * half + 2].reshape(128, -1).astype(jnp.float32)
+        residual = x + total
+        residual_ref[pl.ds(half * 128, 128), :] = residual
+        normed, _ = norm_rows(residual)
+        m_own_ref[pl.ds(half * 128, 128), :] = normed.astype(jnp.bfloat16)
+    for one in swaps:
+        one.wait_send()
+    reduce.end()
+
+
+def out_layer(mixed, o_all, a_sel, b_row, w_all, a48, b_sel, x_own):
+    bf16 = jnp.bfloat16
+    vmem = pl.BlockSpec(memory_space=pltpu.VMEM)
+    width = x_own.shape[2]
+    shape = jax.ShapeDtypeStruct
+    dma = pltpu.SemaphoreType.DMA
+    return pl.pallas_call(
+        out_kernel,
+        in_specs=[vmem, vmem, vmem, vmem, pl.BlockSpec(memory_space=pl.ANY), vmem, vmem, vmem],
+        out_specs=[vmem, vmem, vmem, vmem],
+        out_shape=[
+            shape((256, width), jnp.float32),
+            shape((256, width), bf16),
+            shape((256, width), bf16),
+            shape((width, 1536), bf16),
+        ],
+        scratch_shapes=[
+            pltpu.VMEM((4, 256, 256), bf16),
+            pltpu.VMEM((6, 128, width), bf16),
+            pltpu.VMEM((6, 128, width), bf16),
+            pltpu.VMEM((512, width), bf16),
+            pltpu.VMEM(w_all.shape, bf16),
+            dma((4,)),
+            dma((4,)),
+            dma((6,)),
+            dma((6,)),
+            dma((1,)),
+        ],
+        cost_estimate=spend(45),
+        compiler_params=pltpu.CompilerParams(
+            collective_id=2, has_side_effects=True, vmem_limit_bytes=56 << 20
+        ),
+    )(mixed, o_all, a_sel, b_row, w_all, a48, b_sel, x_own)
+
+
+def spread_kernel(
+    g_ref, o_eff_ref, mixed_ref, b_ref, g_out, gm_ref, dots_ref, rank_ref, g_buf, send, recv, local_sem
+):
+    s, z = places()
+    meet([(None, (flip(s, 1), z)), (None, (flip(s, 2), z)), (None, (flip(s, 4), z))])
+    g_buf[s] = g_ref[...]
+    gather = Gather(g_buf, s, z, send, recv, 128)
+    gather.begin()
+
+    def store(t):
+        return pltpu.make_async_copy(g_buf.at[t], g_out.at[t], local_sem.at[0])
+
+    def work(t):
+        g = g_buf[t]
+        store(t).start()
+        back = dot_nt(g, o_eff_ref[...]).astype(jnp.bfloat16)
+        gm_ref[t] = back
+        product = back.astype(jnp.float32) * mixed_ref[t].astype(jnp.float32)
+        for head in range(2):
+            turned = jnp.transpose(product[:, HDIM * head : HDIM * head + HDIM])
+            dots_ref[head, t] = jnp.sum(turned, axis=0, keepdims=True)
+        rank_ref[t] = (adapt_scale * dot_nt(g, b_ref[...])).astype(jnp.bfloat16)
+        store(t).wait()
+
+    work(s)
+    gather.arrive_first()
+    work(gather.arrive_core(0))
+    gather.arrive_neighbours()
+    work(flip(s, 2))
+    work(flip(s, 4))
+    work(gather.arrive_core(1))
+    work(gather.arrive_core(2))
+    gather.arrive_diagonal()
+    work(flip(flip(s, 2), 4))
+    work(gather.arrive_core(3))
+    gather.end()
+
+
+def spread_layer(g_own, o_eff, mixed, b_row):
+    bf16 = jnp.bfloat16
+    vmem = pl.BlockSpec(memory_space=pltpu.VMEM)
+    width = g_own.shape[1]
+    shape = jax.ShapeDtypeStruct
+    dma = pltpu.SemaphoreType.DMA
+    return pl.pallas_call(
+        spread_kernel,
+        in_specs=[vmem, vmem, vmem, vmem],
+        out_specs=[pl.BlockSpec(memory_space=pl.ANY), vmem, vmem, vmem],
+        out_shape=[
+            shape((8, 256, width), bf16),
+            shape((8, 256, 256), bf16),
+            shape((2, 8, 1, 256), jnp.float32),
+            shape((8, 256, 16), bf16),
+        ],
+        scratch_shapes=[
+            pltpu.VMEM((8, 256, width), bf16),
+            dma((gather_sems,)),
+            dma((gather_sems,)),
+            dma((1,)),
+        ],
+        cost_estimate=spend(40),
+        compiler_params=pltpu.CompilerParams(
+            collective_id=3, has_side_effects=True, vmem_limit_bytes=48 << 20
+        ),
+    )(g_own, o_eff, mixed, b_row)
+
+
+def in_kernel(
+    dq_ref, dk_ref, dv_ref, w_ref, x_own_ref, residual_ref,
+    grad_ref, own_ref, sib_q, sib_k, sib_v, out_buf, in_buf, a2a_send, a2a_recv, sib_send, sib_recv, send, recv,
+):
+    s, z = places()
+    core = s % 2
+    other = flip(s, 1)
+    zs = [flip(z, 1), flip(z, 2), 3 - z]
+    meet([(None, (other, z)), (None, (flip(s, 2), z)), (None, (flip(s, 4), z))] + [(None, (s, j)) for j in zs])
+    mine = (dq_ref, dk_ref, dv_ref)
+    theirs = (sib_q, sib_k, sib_v)
+    swaps = [
+        remote(
+            mine[p].at[2 * c + 1 - core], theirs[p].at[c], sib_send.at[4 * p + c], sib_recv.at[4 * p + c], (other, z)
+        )
+        for c in range(4)
+        for p in range(3)
+    ]
+    for one in swaps:
+        one.start()
+    for one in swaps:
+        one.wait_recv()
+
+    def product(chip, half):
+        rows = pl.ds(half * 128, 128)
+        both = jnp.concatenate(
+            [ref[2 * chip + core, rows, :] for ref in mine] + [ref[chip, rows, :] for ref in theirs], axis=1
+        )
+        return dot_nt(both, w_ref[...])
+
+    reduce = Reduce(product, s, z, out_buf, in_buf, send, recv)
+    reduce.begin()
+    reduce.middle()
+    for half in range(2):
+        total = reduce.finish(half)
+        x = x_own_ref[2 * half : 2 * half + 2].reshape(128, -1).astype(jnp.float32)
+        normed, inverse = norm_rows(x)
+        value = residual_ref[pl.ds(half * 128, 128), :] + norm_back(total, normed, inverse)
+        own_ref[2 * half : 2 * half + 2] = value.astype(jnp.bfloat16).reshape(2, 64, -1)
+    backs = [
+        remote(own_ref.at[j], grad_ref.at[z], a2a_send.at[d], a2a_recv.at[d], (s, j)) for d, j in enumerate(zs)
+    ]
+    for one in backs:
+        one.start()
+    grad_ref[z] = own_ref[z]
+    for one in swaps:
+        one.wait_send()
+    reduce.end()
+    for d, j in enumerate(zs):
+        remote(own_ref.at[j], grad_ref.at[j], a2a_send.at[d], a2a_recv.at[d], (s, j)).wait_recv()
+    for one in backs:
+        one.wait_send()
+
+
+def in_layer(dq, dk, dv, w_cat, x_own, grad_residual):
+    bf16 = jnp.bfloat16
+    vmem = pl.BlockSpec(memory_space=pltpu.VMEM)
+    width = x_own.shape[2]
+    dma = pltpu.SemaphoreType.DMA
+
+    return pl.pallas_call(
+        in_kernel,
+        in_specs=[vmem] * 6,
+        out_specs=vmem,
+        out_shape=jax.ShapeDtypeStruct((4, 64, width), bf16),
+        scratch_shapes=[
+            pltpu.VMEM((4, 64, width), bf16),
+            pltpu.VMEM((4, 256, 256), bf16),
+            pltpu.VMEM((4, 256, 256), bf16),
+            pltpu.VMEM((4, 256, 256), bf16),
+            pltpu.VMEM((6, 128, width), bf16),
+            pltpu.VMEM((6, 128, width), bf16),
+            dma((3,)),
+            dma((3,)),
+            dma((12,)),
+            dma((12,)),
+            dma((6,)),
+            dma((6,)),
+        ],
+        cost_estimate=spend(80),
+        compiler_params=pltpu.CompilerParams(
+            collective_id=4, has_side_effects=True, vmem_limit_bytes=48 << 20
+        ),
+    )(dq, dk, dv, w_cat, x_own, grad_residual)
+
+
+def mlp_line_kernel(
+    m_ref, residual_ref, cot0_ref, cot1_ref, cot2_ref, cot3_ref, w_gu_ref, w_d_ref, a_ref, b_ref, ad_ref, bd_ref,
+    g_ref, grad_res_ref, down0_ref, down1_ref, down2_ref, down3_ref, grad_b_ref, grad_ad_ref, grad_a_ref, grad_bd_ref,
+    m_buf, wg, wu, wd, cot_buf, back_acc, down_acc, ranks, slots, r1, r2, r3, r4, r5, stage,
+    up_send, up_recv, dn_send, dn_recv, send1, recv1, send4, recv4, send5, recv5, send23, recv23,
+    weight_sem, cot_sem, stage_sem,
+):
+    s, z = places()
+    tiles = wg.shape[0]
+    tile = wg.shape[2]
+    f32 = jnp.float32
+    bf16 = jnp.bfloat16
+    middle = z * (3 - z) == 2
+    at_end = z * (3 - z) == 0
+    pair = flip(z, 1)
+    opposite = 3 - z
+    inner = 1 + z // 2
+    high = z // 2
+    ids = [z, pair, 2 - high, 3 - 3 * high]
+    far = 3 - 3 * high
+
+    loads = []
+    for h in range(tiles):
+        columns = pl.ds(h * tile, tile)
+        loads.append(
+            [
+                pltpu.make_async_copy(w_gu_ref.at[0, :, columns], wg.at[h], weight_sem.at[3 * h]),
+                pltpu.make_async_copy(w_gu_ref.at[1, :, columns], wu.at[h], weight_sem.at[3 * h + 1]),
+                pltpu.make_async_copy(w_d_ref.at[columns, :], wd.at[h], weight_sem.at[3 * h + 2]),
+            ]
+        )
+        for one in loads[-1]:
+            one.start()
+
+    others = [z, pair, flip(z, 2), opposite]
+    cot_refs = (cot0_ref, cot1_ref, cot2_ref, cot3_ref)
+    down_refs = (down0_ref, down1_ref, down2_ref, down3_ref)
+
+    def load_cot(seq):
+        return [
+            pltpu.make_async_copy(cot_refs[d].at[seq], cot_buf.at[others[d]], cot_sem.at[d]) for d in range(4)
+        ]
+
+    for one in load_cot(z):
+        one.start()
+
+    meet([(z < 3, (s, z + 1)), (z > 0, (s, z - 1)), (None, (s, flip(z, 2)))])
+    m_buf[z] = m_ref[...]
+
+    def up(hop, j):
+        return remote(m_buf.at[j], m_buf.at[j], up_send.at[hop], up_recv.at[hop], (s, z + 1))
+
+    def down(hop, j):
+        return remote(m_buf.at[j], m_buf.at[j], dn_send.at[hop], dn_recv.at[hop], (s, z - 1))
+
+    def begin():
+        @pl.when(z < 3)
+        def _():
+            up(0, z).start()
+
+        @pl.when(z > 0)
+        def _():
+            down(0, z).start()
+
+    def hop(t):
+        @pl.when(z >= t)
+        def _():
+            up(t - 1, z - t).wait_recv()
+            if t < 3:
+
+                @pl.when(z < 3)
+                def _():
+                    up(t, z - t).start()
+
+        @pl.when(z + t <= 3)
+        def _():
+            down(t - 1, z + t).wait_recv()
+            if t < 3:
+
+                @pl.when(z > 0)
+                def _():
+                    down(t, z + t).start()
+
+    def hop_end():
+        @pl.when(z < 3)
+        def _():
+            up(0, z).wait_send()
+
+        @pl.when(z > 0)
+        def _():
+            down(0, z).wait_send()
+
+        for t in (1, 2):
+
+            @pl.when((z >= t) & (z < 3))
+            def _():
+                up(t, z - t).wait_send()
+
+            @pl.when((z + t <= 3) & (z > 0))
+            def _():
+                down(t, z + t).wait_send()
+
+    def piece(p):
+        return pl.ds(p * 64, 64)
+
+    def copy1():
+        return remote(slots.at[1], r1, send1.at[0], recv1.at[0], (s, pair))
+
+    def copy2():
+        return remote(slots.at[2], r2, send23.at[0], recv23.at[0], (s, opposite))
+
+    def copy3():
+        return remote(slots.at[2], r3, send23.at[1], recv23.at[1], (s, inner))
+
+    def copy4(p):
+        return remote(slots.at[3, piece(p)], r4.at[piece(p)], send4.at[p], recv4.at[p], (s, far))
+
+    def copy5(p):
+        return remote(slots.at[3, piece(p)], r5.at[piece(p)], send5.at[p], recv5.at[p], (s, inner))
+
+    def stage_copies(seq):
+        return [
+            pltpu.make_async_copy(stage.at[others[d]], down_refs[d].at[seq], stage_sem.at[d]) for d in range(4)
+        ]
+
+    def compute(slot):
+        seq = ids[slot]
+        rows = m_buf[seq]
+        for one in load_cot(seq):
+            one.wait()
+        ranks[:, 0:32] = adapt_scale * dot_nt(rows, a_ref[seq])
+        cot = cot_buf[...].reshape(256, -1)
+        ranks[:, 32:48] = adapt_scale * dot_nt(cot, bd_ref[seq])
+        ranks[:, 48:96] = jnp.zeros((256, 48), f32)
+        back_acc[...] = jnp.zeros_like(back_acc)
+        down_acc[...] = jnp.zeros_like(down_acc)
+
+        def step(h, _):
+            columns = pl.ds(pl.multiple_of(h * tile, tile), tile)
+            low = ranks[...].astype(bf16)
+            low_gate = low[:, 0:16]
+            low_up = low[:, 16:32]
+            low_cot = low[:, 32:48]
+            bg = b_ref[seq, 0, :, columns]
+            bu = b_ref[seq, 1, :, columns]
+            ad = ad_ref[seq, :, columns]
+            rows = m_buf[seq]
+            cot = cot_buf[...].reshape(256, -1)
+            gate = dot_nn(rows, wg[h]) + dot_nn(low_gate, bg)
+            up_value = dot_nn(rows, wu[h]) + dot_nn(low_up, bu)
+            grad_act = dot_nt(cot, wd[h]) + dot_nn(low_cot, ad)
+            sig = jax.nn.sigmoid(gate)
+            act = (gate * sig * up_value).astype(bf16)
+            grad_up = (grad_act * gate * sig).astype(bf16)
+            grad_gate = (grad_act * up_value * sig * (1.0 + gate * (1.0 - sig))).astype(bf16)
+            for part in range(4):
+                wide = pl.ds(part * 512, 512)
+                back_acc[:, wide] += dot_nt(grad_gate, wg[h, wide, :]) + dot_nt(grad_up, wu[h, wide, :])
+                down_acc[:, wide] += dot_nn(act, wd[h, :, wide])
+            ranks[:, 48:64] += dot_nt(act, ad)
+            ranks[:, 64:80] += dot_nt(grad_gate, bg)
+            ranks[:, 80:96] += dot_nt(grad_up, bu)
+            grad_b_ref[seq, 0, :, columns] = dot_tn(low_gate, grad_gate)
+            grad_b_ref[seq, 1, :, columns] = dot_tn(low_up, grad_up)
+            grad_ad_ref[seq, :, columns] = dot_tn(low_cot, act)
+            return 0
+
+        if slot == 0:
+            for h in range(tiles):
+                for one in loads[h]:
+                    one.wait()
+        lax.fori_loop(0, tiles, step, 0)
+        back_rank = (adapt_scale * ranks[:, 64:96]).astype(bf16)
+        slots[slot] = (back_acc[...] + dot_nn(back_rank, a_ref[seq])).astype(bf16)
+
+    def rest(slot):
+        seq = ids[slot]
+        back_rank = (adapt_scale * ranks[:, 64:96]).astype(bf16)
+        low_down = (adapt_scale * ranks[:, 48:64]).astype(bf16)
+        grad_a_ref[seq] = dot_tn(back_rank, m_buf[seq])
+        grad_bd_ref[seq] = dot_tn(low_down, cot_buf[...].reshape(256, -1))
+        if slot > 0:
+            for one in stage_copies(ids[slot - 1]):
+                one.wait()
+        value = down_acc[...] + dot_nn(low_down, bd_ref[seq])
+        if slot == 0:
+            value = value + residual_ref[...]
+        stage[...] = value.astype(bf16).reshape(4, 64, -1)
+        for one in stage_copies(seq):
+            one.start()
+        following = ids[slot + 1] if slot < 3 else z
+        for one in load_cot(following):
+            one.start()
+
+    def add(slot, p, extra):
+        slots[slot, piece(p), :] = (
+            slots[slot, piece(p), :].astype(f32) + extra[piece(p), :].astype(f32)
+        ).astype(bf16)
+
+    begin()
+    compute(0)
+    rest(0)
+    hop(1)
+    compute(1)
+
+    @pl.when(at_end)
+    def _():
+        copy1().start()
+
+    rest(1)
+    hop(2)
+    compute(2)
+
+    @pl.when(at_end)
+    def _():
+        copy3().start()
+
+    @pl.when(middle)
+    def _():
+        copy1().start()
+
+    rest(2)
+    hop(3)
+    compute(3)
+
+    @pl.when(at_end)
+    def _():
+        copy5(0).start()
+        copy5(1).start()
+
+    @pl.when(middle)
+    def _():
+        copy3().wait_recv()
+        for p in range(4):
+            add(2, p, r3)
+        copy2().start()
+
+    rest(3)
+
+    @pl.when(at_end)
+    def _():
+        for p in (2, 3):
+            copy5(p - 2).wait_send()
+            copy5(p).start()
+
+    @pl.when(middle)
+    def _():
+        for p in range(4):
+            copy5(p).wait_recv()
+            add(3, p, r5)
+            copy4(p).start()
+
+    copy1().wait_recv()
+    for p in range(4):
+        add(0, p, r1)
+
+    @pl.when(middle)
+    def _():
+        copy2().wait_recv()
+        for p in range(4):
+            add(0, p, r2)
+
+    for one in load_cot(z):
+        one.wait()
+    for p in range(4):
+
+        @pl.when(at_end)
+        def _():
+            copy4(p).wait_recv()
+            add(0, p, r4)
+
+        grad = slots[0, piece(p), :].astype(f32)
+        normed, inverse = norm_rows(residual_ref[piece(p), :])
+        value = cot_buf[p].astype(f32) + norm_back(grad, normed, inverse)
+        grad_res_ref[piece(p), :] = value
+        g_ref[piece(p), :] = value.astype(bf16)
+    for one in stage_copies(ids[3]):
+        one.wait()
+    hop_end()
+    copy1().wait_send()
+
+    @pl.when(at_end)
+    def _():
+        copy3().wait_send()
+        for p in (2, 3):
+            copy5(p).wait_send()
+
+    @pl.when(middle)
+    def _():
+        copy2().wait_send()
+        for p in range(4):
+            copy4(p).wait_send()
+
+
+def mlp_line(m_own, residual, cots, w_gate_up, w_down, a_sel, b_sel, ad_sel, bd_sel):
+    bf16 = jnp.bfloat16
+    f32 = jnp.float32
+    vmem = pl.BlockSpec(memory_space=pltpu.VMEM)
+    anywhere = pl.BlockSpec(memory_space=pl.ANY)
+    width = m_own.shape[1]
+    hidden = w_down.shape[0]
+    tile = hidden_tile
+    tiles = hidden // tile
+    shape = jax.ShapeDtypeStruct
+    dma = pltpu.SemaphoreType.DMA
+    vm = pltpu.VMEM
+    return pl.pallas_call(
+        mlp_line_kernel,
+        in_specs=[vmem, vmem] + [anywhere] * 6 + [vmem] * 4,
+        out_specs=[vmem, vmem] + [anywhere] * 4 + [vmem, vmem, vmem, vmem],
+        out_shape=[
+            shape((256, width), bf16),
+            shape((256, width), f32),
+        ]
+        + [shape((4, 64, width), bf16)] * 4
+        + [
+            shape((4, 2, 16, hidden), f32),
+            shape((4, 16, hidden), f32),
+            shape((4, 32, width), f32),
+            shape((4, 16, width), f32),
+        ],
+        scratch_shapes=[
+            vm((4, 256, width), bf16),
+            vm((tiles, width, tile), bf16),
+            vm((tiles, width, tile), bf16),
+            vm((tiles, tile, width), bf16),
+            vm((4, 64, width), bf16),
+            vm((256, width), f32),
+            vm((256, width), f32),
+            vm((256, 96), f32),
+            vm((4, 256, width), bf16),
+            vm((256, width), bf16),
+            vm((256, width), bf16),
+            vm((256, width), bf16),
+            vm((256, width), bf16),
+            vm((256, width), bf16),
+            vm((4, 64, width), bf16),
+        ]
+        + [dma((3,))] * 4
+        + [dma((4,))] * 6
+        + [dma((2,))] * 2
+        + [dma((3 * tiles,)), dma((4,)), dma((4,))],
+        cost_estimate=spend(110),
+        compiler_params=pltpu.CompilerParams(
+            collective_id=5, has_side_effects=True, vmem_limit_bytes=60 << 20
+        ),
+    )(m_own, residual, *cots, w_gate_up, w_down, a_sel, b_sel, ad_sel, bd_sel)
+
+
+def swap_mp(values, d):
+    pairs = [(s * 4 + z, s * 4 + (z ^ d)) for s in range(lax.axis_size("seq")) for z in range(4)]
+    return lax.ppermute(values, ("seq", "mp"), pairs)
+
+
+def full_tables(positions):
+    half_dim = HDIM // 2
+    frequency = jnp.exp(
+        jnp.arange(half_dim, dtype=jnp.float32) * (-2.0 * math.log(rope_base) / HDIM)
+    )
+    angles = positions.astype(jnp.float32)[:, None] * frequency
+    cos = jnp.cos(angles)
+    sin = jnp.sin(angles)
+    return (jnp.concatenate([cos, cos], axis=1), jnp.concatenate([sin, -sin], axis=1))
+
+
+def by_sets(set_ids, grads, sets):
+    return jnp.stack(
+        [
+            sum(jnp.where(one == member, grad, 0.0) for one, grad in zip(set_ids, grads))
+            for member in range(sets)
+        ]
+    )
+
+
+def pick(values, index, axis=0):
+    return lax.dynamic_index_in_dim(values, index, axis, keepdims=False)
+
+
+def per_device_layers(
+    layer_in, w_qkv, w_out, w_gate_up, w_down, a_in, b_qkv, b_gate_up, a_out, a_down, b_out_down,
+    set_index, positions, cotangent,
+):
+    bf16 = jnp.bfloat16
+    f32 = jnp.float32
+    s = lax.axis_index("seq")
+    z = lax.axis_index("mp")
+    chip = s // 2
+    core = s % 2
+    sets = a_in.shape[0]
+    width = layer_in.shape[2]
+    rank = a_in.shape[2]
+    length = 8 * 256
+
+    my_set = pick(set_index, z)
+    a48 = pick(a_in, my_set)[:3].reshape(3 * rank, width)
+    bo_set = pick(b_out_down, my_set)
+    a_sel = jnp.stack([pick(a_in, set_index[q])[3:].reshape(2 * rank, width) for q in range(4)])
+    b_sel_mlp = jnp.stack([pick(b_gate_up, set_index[q]) for q in range(4)])
+    ad_sel = jnp.stack([pick(a_down, set_index[q]) for q in range(4)])
+    bd_sel = jnp.stack([pick(b_out_down, set_index[q])[1] for q in range(4)])
+    half = width // 2
+    w_half = lax.dynamic_slice(w_qkv, (0, core * half, chip * HDIM), (3, half, HDIM)).reshape(-1, HDIM)
+    b_own = lax.dynamic_slice_in_dim(b_qkv, chip * HDIM, HDIM, 3).reshape(-1, HDIM)
+    a_own = lax.dynamic_slice_in_dim(a_out, chip * HDIM, HDIM, 2).reshape(-1, HDIM)
+    w_pack = jnp.concatenate([w_half, b_own, a_own], axis=0)
+    o_pack = lax.dynamic_slice(w_out, (chip * HDIM, core * half), (HDIM, half))
+    positions_z = lax.all_gather(pick(positions, z), "seq", axis=0, tiled=True)
+    cos, sin = full_tables(positions_z)
+
+    (x_own, n_own, u, w_all, o_all, q, k, v, low, b_sel, a_out_sel) = start_layer(
+        layer_in, w_pack, o_pack, cos, sin, a48, my_set[None]
+    )
+    del n_own
+    cot_late, _ = lax.optimization_barrier((cotangent, x_own))
+    cots = [cot_late] + [swap_mp(cot_late, d) for d in (1, 2, 3)]
+
+    def flat(values):
+        return values.reshape(length, values.shape[-1])
+
+    mixed, lse = attend(flat(q), flat(k), flat(v))
+    residual, m_own, o_eff, w_cat = out_layer(
+        mixed.reshape(8, 256, 256), o_all, a_out_sel, bo_set[0], w_all, a48, b_sel, x_own
+    )
+    g_own, grad_residual, down0, down1, down2, down3, grad_b_mlp, grad_ad, grad_a_mlp, grad_bd = mlp_line(
+        m_own, residual, cots, w_gate_up, w_down, a_sel, b_sel_mlp, ad_sel, bd_sel
+    )
+    result = down0.astype(f32)
+    for d, part in ((1, down1), (2, down2), (3, down3)):
+        result = result + swap_mp(part, d).astype(f32)
+    result = result.astype(bf16)
+
+    set_ids = [set_index[q_] for q_ in range(4)]
+    sum_b_gate_up = by_sets(set_ids, [grad_b_mlp[q_] for q_ in range(4)], sets).astype(bf16)
+    sum_a_down = by_sets(set_ids, [grad_ad[q_] for q_ in range(4)], sets).astype(bf16)
+    sum_a_mlp = by_sets(set_ids, [grad_a_mlp[q_].reshape(2, rank, width) for q_ in range(4)], sets).astype(bf16)
+    sum_b_down = by_sets(set_ids, [grad_bd[q_] for q_ in range(4)], sets).astype(bf16)
+    sum_b_gate_up, sum_a_down = lax.psum((sum_b_gate_up, sum_a_down), "seq")
+    sum_a_mlp, sum_b_down = lax.psum((sum_a_mlp, sum_b_down), ("seq", "mp"))
+
+    g, grad_mixed, dots, out_rank = spread_layer(g_own, o_eff, mixed.reshape(8, 256, 256), bo_set[0])
+    dq, dk, dv = attend_back(
+        flat(q), flat(k), flat(v), flat(grad_mixed), lse, dots.reshape(2, 1, length), cos, sin
+    )
+
+    def spans(values):
+        return values.reshape(8, 256, 256)
+
+    grad_in = in_layer(spans(dq), spans(dk), spans(dv), w_cat, x_own, grad_residual)
+
+    my_b = lax.dynamic_slice_in_dim(b_sel.reshape(4, 3, rank, HDIM), 2 * core, 2, 0)
+    my_a = lax.dynamic_slice_in_dim(a_out_sel, 2 * core, 2, 0)
+    d_parts = [d.reshape(length, 2, HDIM) for d in (dq, dk, dv)]
+    back_rank = jnp.concatenate(
+        [
+            adapt_scale * jnp.einsum("thk,hrk->tr", d_parts[p], my_b[:, p], preferred_element_type=f32)
+            for p in range(3)
+        ],
+        axis=1,
+    ).astype(bf16)
+    grad_a_qkv = dot_tn(back_rank, flat(u)).reshape(3, rank, width)
+    low = flat(low)
+    grad_b_qkv = jnp.stack(
+        [dot_tn(low[:, rank * p : rank * p + rank], d) for p, d in enumerate((dq, dk, dv))]
+    )
+    grad_a_out = dot_tn(flat(out_rank), mixed)
+    out_low = (
+        adapt_scale
+        * jnp.einsum("thk,hrk->tr", mixed.reshape(length, 2, HDIM), my_a, preferred_element_type=f32)
+    ).astype(bf16)
+    grad_b_out = dot_tn(out_low, flat(g))
+
+    def in_set(values):
+        return jnp.stack([jnp.where(my_set == member, values, 0.0) for member in range(sets)]).astype(bf16)
+
+    def in_heads(values):
+        pairs = values.reshape(values.shape[:-1] + (2, HDIM))
+        out = jnp.zeros(values.shape[:-1] + (4, 4 * HDIM), values.dtype)
+        start = (0,) * (values.ndim - 1) + (2 * core, chip * HDIM)
+        return lax.dynamic_update_slice(out, pairs, start)
+
+    grad_b_out, _ = lax.optimization_barrier((grad_b_out, sum_b_down))
+    sum_a_qkv, sum_b_out, sum_b_qkv, sum_a_out = lax.psum(
+        (in_set(grad_a_qkv), in_set(grad_b_out), in_set(in_heads(grad_b_qkv)), in_set(in_heads(grad_a_out))),
+        ("seq", "mp"),
+    )
+    return (
+        result,
+        grad_in,
+        jnp.concatenate([sum_a_qkv, sum_a_mlp], axis=1).astype(f32),
+        pick(sum_b_qkv, z, 3).astype(f32),
+        sum_b_gate_up.astype(f32),
+        pick(sum_a_out, z, 2).astype(f32),
+        sum_a_down.astype(f32),
+        jnp.stack([sum_b_out, sum_b_down], axis=1).astype(f32),
+    )
+
+
 def solution(mesh):
+    by_layers = mesh.shape["seq"] == 8 and mesh.shape["mp"] == 4
+    body = per_device_layers if by_layers else per_device
     placed = (
         P(None, ("seq", "mp"), None),
         P(None, None, "mp"),
@@ -437,7 +1789,7 @@
         P(None, ("seq", "mp"), None),
     )
     return jax.shard_map(
-        per_device,
+        body,
         mesh=mesh,
         in_specs=placed,
         out_specs=(

time: 1440 us -> 867 us (0.60)
  waiting for transfers between devices: 847 us -> 251 us
  Pallas kernels: 0 us -> 461 us
  matrix products: 415 us -> 17.6 us
  local copies, waits for them, and re-layouts: 77.3 us -> 23 us
  other arithmetic: 65.1 us -> 43.1 us
  between operations: 15.4 us -> 37.3 us
    pallas_call x0 -> x7, Pallas kernels: none -> 461 us  [the longest x1 143 us: mlp_line(): pl.pallas_call(mlp_line_kernel, in_specs=[vmem, vmem] + [anywhere] * 6 +...]
    dot_general x89 -> x9, matrix products: 415 us -> 17.6 us  [the longest x6 14.5 us: dot_tn(): lax.dot_general(a, b, (((0,), (0,)), ((), ())), preferred_element_type=jn...]
    reduce_scatter x5 -> x0, waiting for transfers between devices: 371 us -> none  [the longest x4 315 us: scatter_rows(): lax.psum_scatter(values.astype(jnp.bfloat16), 'mp', scatter_dimension=1,...]
    all_gather x6 -> x0, waiting for transfers between devices: 332 us -> none  [the longest x4 284 us: gather_rows(): return lax.all_gather(values, 'mp', axis=1, tiled=True)]
    psum x2 -> x3, waiting for transfers between devices: 143 us -> 251 us  [the longest x2 251 us: per_device_layers(): sum_a_mlp, sum_b_down = lax.psum((sum_a_mlp, sum_b_down), ('seq', 'mp'))]
    unnamed x176 -> x108, local copies, waits for them, and re-layouts: 33.8 us -> 11.1 us
    reduce_sum x10 -> x0, other arithmetic: 18.8 us -> none  [the longest x3 5.12 us: compute(): running_sum = running_sum * factor + jnp.sum(exponent, axis=-1)]
    another operation x4 -> x22, other arithmetic: 2.89 us -> 20.8 us
  transfers between devices with their start and end apart: 13 -> 9, of which waited for: 12 -> 2; matrix products, arithmetic and copies ran while one was open for 16% -> 5% of each run, Pallas kernels for 0% -> 17%
where the time goes in v1:
time: 867 us; the launch traced here: 857 us
  Pallas kernels  461 us (53%)
  waiting for transfers between devices  251 us (29%)
  other arithmetic  43.1 us (5%)
  between operations  37.3 us (4%)
  local copies, waits for them, and re-layouts  23 us (3%)
  matrix products  17.6 us (2%)
  starting transfers between devices  14.8 us (2%)
  blocking collectives  9.34 us (1%)
    psum x2, waiting for transfers between devices, per_device_layers(): sum_a_mlp, sum_b_down = lax.psum((sum_a_mlp, sum_b_down), ('seq', 'mp'))  251 us
    pallas_call x1, Pallas kernels, mlp_line(): pl.pallas_call(mlp_line_kernel, in_specs=[vmem, vmem] + [anywhere] * 6 +...  143 us
    pallas_call x1, Pallas kernels, start_layer(): pl.pallas_call(start_kernel, in_specs=[vmem, vmem, anywhere, vmem, vmem,...  104 us
    pallas_call x1, Pallas kernels, in_layer(): pl.pallas_call(in_kernel, in_specs=[vmem] * 6, out_specs=vmem, out_shape=...  86.4 us
    pallas_call x1, Pallas kernels, out_layer(): pl.pallas_call(out_kernel, in_specs=[vmem, vmem, vmem, vmem, pl.BlockSpec...  47.4 us
    pallas_call x1, Pallas kernels, spread_layer(): pl.pallas_call(spread_kernel, in_specs=[vmem, vmem, vmem, vmem], out_spec...  42 us
    pallas_call x1, Pallas kernels, attend_back(): pl.pallas_call(attend_back_kernel, grid=(heads, length // tile), in_specs...  21.8 us
  transfers between devices with their start and end apart: 9, of which 2 were waited for; matrix products, arithmetic and copies ran while one was open for 5% of the time, Pallas kernels for 17%

profile of v1, /device:TPU:13, one launch (start us, length us, event | category | flops | bytes accessed | tf_op | source)
XLA Modules:
  0.0 857.4 jit_solution(1404764893894349187)
XLA Ops:
  7.3 1.5 fusion.51
  10.8 2.1 constant_dynamic-slice_fusion.16
  12.9 1.7 dynamic_slice.94.o_ref
  15.3 9.3 %all-gather = s32[1,2048]{1,0:T(1,128)S(1)} all-gather(s32[1,256]{1,0:T(1,128)S(1)} %constant_dynamic-slice_fusion.13), channel_id=2, replica_groups=mesh['seq'=8,'mp'=4] {'seq'}, dimensions={1}, use_global_device_ids=true | all-gather | bytes 9216 | tf_op jit(solution)/shard_map/all_gather | solution.py:1681
  24.6 3.7 multiply_sine_fusion
  29.0 1.6 constant_dynamic-slice_fusion.12
  30.6 2.1 pad_maximum_fusion.2.w_ref
  32.7 1.9 pad_maximum_fusion
  34.6 104.5 %shard_map.197 = (bf16[4,64,2048]{2,1,0:T(8,128)(2,1)}, bf16[256,2048]{1,0:T(8,128)(2,1)}, bf16[8,256,2048]{2,1,0:T(8,128)(2,1)}, bf16[4,2,3328,128]{3,2,1,0:T(8...) custom-call(bf16[4,64,2048]{2,1,0:T(8,128)(2,1)} %x_ref.1, ...), custom_call_target="tpu_custom_call" | custom-call | flops 80000000000 | bytes 1000000 | tf_op jit(solution)/shard_map/pallas_call | solution.py:928
  139.1 6.5 collective-permute-start
  145.6 1.3 collective-permute-start.1
  155.0 1.1 constant_dynamic-slice_fusion.11
  156.8 1.2 copy-done.12
  158.0 1.2 copy-done.14
  159.2 1.2 copy-done.16
  160.5 15.8 %shard_map.198 = (bf16[2048,256]{1,0:T(8,128)(2,1)S(1)}, f32[2,1,2048]{2,1,0:T(1,128)S(1)}) custom-call(bf16[2048,256]{1,0:T(8,128)(2,1)S(1)} %bitcast.190, bf16[2048,256]{1,0:T(8,128)(2,1)S(1)} %bitcast.192, bf16[2048,256]{1,0:T(8,128)(2,1)S(1)} %bitcast.194), custom_call_target="tpu_custom_call" | custom-call | flops 2147483648 | bytes 4194304 | tf_op jit(solution)/shard_map/pallas_call | solution.py:481
  176.2 1.0 copy-done.2
  177.2 47.4 %shard_map.199 = (f32[256,2048]{1,0:T(8,128)}, bf16[256,2048]{1,0:T(8,128)(2,1)}, bf16[256,2048]{1,0:T(8,128)(2,1)}, bf16[2048,1536]{1,0:T(8,128)(2,1)}) custom-call(bf16[8,256,256]{2,1,0:T(8,128)(2,1)} %bitcast.183, bf16[4,2,128,1024]{3,2,1,0:T(8,128)(2,1)} %get-tuple-element.47.o_all, bf16[4,16,128]{2,1,0:T(8,128)(2,1)} %get-tuple-element.48.a_sel_ref, ...), custom_call_target="tpu_custom_call" | custom-call | flops 44999999488 | bytes 1000000 | tf_op jit(solution)/shard_map/pallas_call | solution.py:1093
  237.7 1.6 copy.41
  242.0 143.2 %shard_map.200 = (bf16[256,2048]{1,0:T(8,128)(2,1)}, f32[256,2048]{1,0:T(8,128)}, bf16[4,64,2048]{2,1,0:T(8,128)(2,1)}, bf16[4,64,2048]{2,1,0:T(8,128)(2,1)}, bf...) custom-call(bf16[256,2048]{1,0:T(8,128)(2,1)} %get-tuple-element.52., ...), custom_call_target="tpu_custom_call" | custom-call | flops 109999996928 | bytes 1000000 | tf_op jit(solution)/shard_map/pallas_call | solution.py:1581
  385.2 1.2 copy-done.19
  386.4 42.0 %shard_map.201 = (bf16[8,256,2048]{2,1,0:T(8,128)(2,1)}, bf16[8,256,256]{2,1,0:T(8,128)(2,1)S(1)}, f32[2,8,1,256]{3,2,1,0:T(1,128)S(1)}, bf16[8,256,16]{2,1,0:T(8,128)(2,1)S(1)}) custom-call(bf16[256,2048]{1,0:T(8,128)(2,1)S(1)} %copy-done.19, bf16[256,2048]{1,0:T(8,128)(2,1)S(1)} %copy-done.18, bf16[8,256,256]{2,1,0:T(8,128)(2,1)S(1)} %bitcast.185, ...), custom_call_target="tpu_custom_call" | custom-call | flops 40000000000 | bytes 1000000 | tf_op jit(solution)/shard_map/pallas_call | solution.py:1166
  429.3 21.8 %shard_map.202 = (bf16[2048,256]{1,0:T(8,128)(2,1)S(1)}, bf16[2048,256]{1,0:T(8,128)(2,1)S(1)}, bf16[2048,256]{1,0:T(8,128)(2,1)S(1)}) custom-call(bf16[2048,256]{1,0:T(8,128)(2,1)S(1)} %bitcast.191, bf16[2048,256]{1,0:T(8,128)(2,1)S(1)} %bitcast.193, bf16[2048,256]{1,0:T(8,128)(2,1)S(1)} %bitcast.195, bf16[2048,256]{1,0:T(8,128)(2,1)S(1)} %bitcast.196, ...), custom_call_target="tpu_custom_call" | custom-call | flops 5368709120 | bytes 7340032 | tf_op jit(solution)/shard_map/pallas_call | solution.py:558
  451.1 1.0 fusion.5
  452.1 1.0 fusion.4
  460.3 1.5 collective-permute-start.5
  461.8 4.9 collective-permute-start.4
  467.3 1.0 fusion.6
  468.4 1.8 convolution_dynamic-update-slice_fusion
  471.9 5.5 fusion.8
  477.4 1.6 pad_maximum_fusion.13
  480.1 5.8 fusion.26
  487.8 2.0 pad_maximum_fusion.7
  489.8 1.9 pad_maximum_fusion.3
  491.7 1.0 pad_maximum_fusion.4
  493.5 140.9 %all-reduce.6.cloned.1.call-done = bf16[4,16,2048]{2,1,0:T(8,128)(2,1)} async-done(((bf16[4,16,2048]{2,1,0:T(8,128)(2,1)}), bf16[4,16,2048]{2,1,0:T(8,128)(2,1)}) %all-reduce.6.cloned.1.call-update) | async-done | bytes 262160 | tf_op jit(solution)/shard_map/psum | solution.py:1712
  636.0 1.2 copy-done.20
  637.2 86.4 %shard_map.203 = bf16[4,64,2048]{2,1,0:T(8,128)(2,1)S(1)} custom-call(bf16[8,256,256]{2,1,0:T(8,128)(2,1)S(1)} %bitcast.186, bf16[8,256,256]{2,1,0:T(8,128)(2,1)S(1)} %bitcast.187, bf16[8,256,256]{2,1,0:T(8,128)(2,1)S(1)} %bitcast.188, bf16[2048,1536]{1,0:T(8,128)(2,1)} %get-tuple-element.67.w_ref, bf16[4,64,2048]{2,1,0:T(8,128)(2,1)S(1)} %copy-done.20, ...), custom_call_target="tpu_custom_call" | custom-call | flops 80000000000 | bytes 1000000 | tf_op jit(solution)/shard_map/pallas_call | solution.py:1249
  724.6 2.2 convert_element_type.63
  726.8 1.8 convert_element_type.66
  728.6 3.6 add_convert_fusion
  732.2 110.4 %all-reduce.8.cloned.1.call-done = (bf16[4,2,16,2048]{3,2,1,0:T(8,128)(2,1)}, bf16[4,3,16,2048]{3,2,1,0:T(8,128)(2,1)}, bf16[4,3,16,4,512]{4,2,1,0,3:T(8,128)(2,...) async-done(((bf16[4,2,16,2048]{3,2,1,0:T(8,128)(2,1)}, bf16[4,3,16,2048]{3,2,1,0:T(8,128)(2,1)}, bf16[4,3,16,4,512]{4,2,1,0,3:T(8,128)(2,1)}, ...) | async-done | bytes 2621456 | tf_op jit(solution)/shard_map/psum | solution.py:1712
  842.6 1.8 bitcast_convert_fusion
  844.4 1.5 bitcast_convert_fusion.1
  846.0 1.0 maximum_convert_fusion.1
  847.0 1.1 copy.37
  848.1 1.7 maximum_convert_fusion
  849.7 1.0 copy.78
  (154 shorter events, 21.6 us)
Async XLA Ops:
  7.2 3.6 copy-start
  7.2 627.2 %all-reduce.6.cloned.1.call-start = ((), (), s32[]{:S(2)}) async-start(), calls=%async_computation | async-start | bytes 524288 | tf_op jit(solution)/shard_map/psum | solution.py:1712
  34.6 121.5 %copy-start.50 = (bf16[4,2,16,2048]{3,2,1,0:T(8,128)(2,1)S(1)}, bf16[4,2,16,2048]{3,2,1,0:T(8,128)(2,1)}, u32[]{:S(2)}) copy-start(bf16[4,2,16,2048]{3,2,1,0:T(8,128)(2,1)} %param.24) | copy-start | bytes 1572868
  139.1 102.9 %collective-permute-start = (bf16[4,64,2048]{2,1,0:T(8,128)(2,1)}, bf16[4,64,2048]{2,1,0:T(8,128)(2,1)}, u32[]{:S(2)}, u32[]{:S(2)}) collective-permute-start(bf16[4,64,2048]{2,1,0:T(8,128)(2,1)} %cot0_ref), channel_id=1, source_target_pairs={{0,1},{1,0},{2,3},{3,2},{4,5},{5,4},{6,7},{7,6},{8,9},{9,8},{10,11... | collective-permute-start | bytes 3145736 | tf_op jit(solution)/shard_map/ppermute | solution.py:1626
  145.6 96.4 %collective-permute-start.1 = (bf16[4,64,2048]{2,1,0:T(8,128)(2,1)}, bf16[4,64,2048]{2,1,0:T(8,128)(2,1)}, u32[]{:S(2)}, u32[]{:S(2)}) collective-permute-start(bf16[4,64,2048]{2,1,0:T(8,128)(2,1)} %cot0_ref), channel_id=1, source_target_pairs={{0,2},{1,3},{2,0},{3,1},{4,6},{5,7},{6,4},{7,5},{8,10},{9,11},{10,... | collective-permute-start | bytes 3145736 | tf_op jit(solution)/shard_map/ppermute | solution.py:1626
  146.9 95.1 %collective-permute-start.2 = (bf16[4,64,2048]{2,1,0:T(8,128)(2,1)}, bf16[4,64,2048]{2,1,0:T(8,128)(2,1)}, u32[]{:S(2)}, u32[]{:S(2)}) collective-permute-start(bf16[4,64,2048]{2,1,0:T(8,128)(2,1)} %cot0_ref), channel_id=1, source_target_pairs={{0,3},{1,2},{2,1},{3,0},{4,7},{5,6},{6,5},{7,4},{8,11},{9,10},{10,... | collective-permute-start | bytes 3145736 | tf_op jit(solution)/shard_map/ppermute | solution.py:1626
  177.2 47.4 %copy-start.37 = (bf16[4,16,2048]{2,1,0:T(8,128)(2,1)S(1)}, bf16[4,16,2048]{2,1,0:T(8,128)(2,1)}, u32[]{:S(2)}) copy-start(bf16[4,16,2048]{2,1,0:T(8,128)(2,1)} %param.23) | copy-start | bytes 786436
  177.2 60.5 %copy-start.3 = (bf16[2048,256]{1,0:T(8,128)(2,1)S(1)}, bf16[2048,256]{1,0:T(8,128)(2,1)}, u32[]{:S(2)}) copy-start(bf16[2048,256]{1,0:T(8,128)(2,1)} %copy-done.2) | copy-start | bytes 3145732
  224.6 14.7 %copy-start.32 = (bf16[4,2,16,2048]{3,2,1,0:T(8,128)(2,1)S(1)}, bf16[4,2,16,2048]{3,2,1,0:T(8,128)(2,1)}, u32[]{:S(2)}) copy-start(bf16[4,2,16,2048]{3,2,1,0:T(8,128)(2,1)} %param.21) | copy-start | bytes 1572868
  242.0 143.2 %copy-start.11 = (bf16[16,2048]{1,0:T(8,128)(2,1)S(1)}, bf16[16,2048]{1,0:T(8,128)(2,1)}, u32[]{:S(2)}) copy-start(bf16[16,2048]{1,0:T(8,128)(2,1)} %get-tuple-element.115.b_ref) | copy-start | bytes 196612
  242.0 143.2 %copy-start.18 = (bf16[256,2048]{1,0:T(8,128)(2,1)S(1)}, bf16[256,2048]{1,0:T(8,128)(2,1)}, u32[]{:S(2)}) copy-start(bf16[256,2048]{1,0:T(8,128)(2,1)} %get-tuple-element.60.o_eff_ref) | copy-start | bytes 3145732
  386.4 42.8 %copy-start.4 = (f32[2048,128]{1,0:T(8,128)S(1)}, f32[2048,128]{1,0:T(8,128)}, u32[]{:S(2)}) copy-start(f32[2048,128]{1,0:T(8,128)} %get-tuple-element.150.cos_ref) | copy-start | bytes 3145732
  386.4 42.8 %copy-start.5 = (f32[2048,128]{1,0:T(8,128)S(1)}, f32[2048,128]{1,0:T(8,128)}, u32[]{:S(2)}) copy-start(f32[2048,128]{1,0:T(8,128)} %get-tuple-element.151.sin_ref) | copy-start | bytes 3145732
  386.4 42.8 %copy-start.13 = (bf16[8,256,256]{2,1,0:T(8,128)(2,1)S(1)}, bf16[8,256,256]{2,1,0:T(8,128)(2,1)}, u32[]{:S(2)}) copy-start(bf16[8,256,256]{2,1,0:T(8,128)(2,1)} %get-tuple-element.43) | copy-start | bytes 3145732
  386.4 42.8 %copy-start.15 = (bf16[8,256,256]{2,1,0:T(8,128)(2,1)S(1)}, bf16[8,256,256]{2,1,0:T(8,128)(2,1)}, u32[]{:S(2)}) copy-start(bf16[8,256,256]{2,1,0:T(8,128)(2,1)} %get-tuple-element.44) | copy-start | bytes 3145732
  386.4 42.8 %copy-start.17 = (bf16[8,256,256]{2,1,0:T(8,128)(2,1)S(1)}, bf16[8,256,256]{2,1,0:T(8,128)(2,1)}, u32[]{:S(2)}) copy-start(bf16[8,256,256]{2,1,0:T(8,128)(2,1)} %get-tuple-element.45) | copy-start | bytes 3145732
  429.3 21.9 %copy-start.52 = (bf16[4,48,128]{2,1,0:T(8,128)(2,1)S(1)}, bf16[4,48,128]{2,1,0:T(8,128)(2,1)}, u32[]{:S(2)}) copy-start(bf16[4,48,128]{2,1,0:T(8,128)(2,1)} %get-tuple-element.50.b_sel_ref) | copy-start | bytes 147460
  451.1 16.2 %copy-start.6 = (bf16[2048,256]{1,0:T(8,128)(2,1)}, bf16[2048,256]{1,0:T(8,128)(2,1)S(1)}, u32[]{:S(2)}) copy-start(bf16[2048,256]{1,0:T(8,128)(2,1)S(1)} %get-tuple-element.66) | copy-start | bytes 3145732
  455.6 3.2 copy-start.24
  460.3 268.3 %collective-permute-start.5 = (bf16[4,64,2048]{2,1,0:T(8,128)(2,1)}, bf16[4,64,2048]{2,1,0:T(8,128)(2,1)}, u32[]{:S(2)}, u32[]{:S(2)}) collective-permute-start(bf16[4,64,2048]{2,1,0:T(8,128)(2,1)} %get-tuple-element.58), channel_id=1, source_target_pairs={{0,3},{1,2},{2,1},{3,0},{4,7},{5,6},{6,5},{7,4},{8,11},{9,10},{10,... | collective-permute-start | bytes 3145736 | tf_op jit(solution)/shard_map/ppermute | solution.py:1626
  461.8 266.8 %collective-permute-start.4 = (bf16[4,64,2048]{2,1,0:T(8,128)(2,1)}, bf16[4,64,2048]{2,1,0:T(8,128)(2,1)}, u32[]{:S(2)}, u32[]{:S(2)}) collective-permute-start(bf16[4,64,2048]{2,1,0:T(8,128)(2,1)} %get-tuple-element.57), channel_id=1, source_target_pairs={{0,2},{1,3},{2,0},{3,1},{4,6},{5,7},{6,4},{7,5},{8,10},{9,11},{10,... | collective-permute-start | bytes 3145736 | tf_op jit(solution)/shard_map/ppermute | solution.py:1626
  466.7 261.9 %collective-permute-start.3 = (bf16[4,64,2048]{2,1,0:T(8,128)(2,1)}, bf16[4,64,2048]{2,1,0:T(8,128)(2,1)}, u32[]{:S(2)}, u32[]{:S(2)}) collective-permute-start(bf16[4,64,2048]{2,1,0:T(8,128)(2,1)} %get-tuple-element.56), channel_id=1, source_target_pairs={{0,1},{1,0},{2,3},{3,2},{4,5},{5,4},{6,7},{7,6},{8,9},{9,8},{10,11... | collective-permute-start | bytes 3145736 | tf_op jit(solution)/shard_map/ppermute | solution.py:1626
  467.3 4.6 copy-start.51
  471.9 5.5 copy-start.43
  471.9 5.5 copy-start.44
  471.9 5.5 copy-start.45
  479.0 245.6 %all-reduce.10.cloned.1.call-start = ((), (), s32[]{:S(2)}) async-start(), calls=%async_computation.2 | async-start | bytes 1572864 | tf_op jit(solution)/shard_map/psum | solution.py:1711
  480.0 5.9 copy-start.33
  480.0 5.9 copy-start.34
  480.0 5.8 copy-start.35
  480.0 5.8 copy-start.36
  480.0 6.7 copy-start.39
  480.0 6.7 copy-start.40
  480.1 6.7 copy-start.41
  480.1 6.7 copy-start.42
  486.7 5.0 copy-start.27
  486.7 5.0 copy-start.28
  486.7 5.0 copy-start.29
  487.5 355.1 %all-reduce.8.cloned.1.call-start = ((), (), s32[]{:S(2)}) async-start(), calls=%async_computation.1 | async-start | bytes 5242880 | tf_op jit(solution)/shard_map/psum | solution.py:1712
  487.8 4.9 copy-start.46
  487.8 4.9 copy-start.47
  487.8 4.9 copy-start.48
  487.8 4.9 copy-start.49
  492.7 143.3 %copy-start.7 = (bf16[2048,256]{1,0:T(8,128)(2,1)S(1)}, bf16[2048,256]{1,0:T(8,128)(2,1)}, u32[]{:S(2)}) copy-start(bf16[2048,256]{1,0:T(8,128)(2,1)} %copy-done.6) | copy-start | bytes 3145732
  724.6 4.0 copy-start.26
  728.6 117.3 %copy-start.38 = (bf16[4,16,2048]{2,1,0:T(8,128)(2,1)S(1)}, bf16[4,16,2048]{2,1,0:T(8,128)(2,1)}, u32[]{:S(2)}) copy-start(bf16[4,16,2048]{2,1,0:T(8,128)(2,1)} %all-reduce.6.cloned.1.call-done) | copy-start | bytes 786436
  842.6 5.4 copy-start.30
  842.6 5.4 copy-start.31
  (14 other events, 22.0 us)
Sparse Core Ops, SparseCore 0:
  479.1 155.1 all-reduce.5
  638.1 56.6 all-reduce.9
  701.6 140.9 all-reduce.7

commit v2 on v1

--- a/solution.py
+++ b/solution.py
@@ -1120,10 +1120,20 @@
 
 
 def spread_kernel(
-    g_ref, o_eff_ref, mixed_ref, b_ref, g_out, gm_ref, dots_ref, rank_ref, g_buf, send, recv, local_sem
+    g_ref, o_eff_ref, mixed_ref, b_ref, down1_ref, down2_ref,
+    g_out, gm_ref, dots_ref, rank_ref, got1_ref, got2_ref, g_buf, send, recv, local_sem, down_send, down_recv,
 ):
     s, z = places()
-    meet([(None, (flip(s, 1), z)), (None, (flip(s, 2), z)), (None, (flip(s, 4), z))])
+    meet(
+        [(None, (flip(s, 1), z)), (None, (flip(s, 2), z)), (None, (flip(s, 4), z))]
+        + [(None, (s, flip(z, 1))), (None, (s, flip(z, 2)))]
+    )
+    results = [
+        remote(down1_ref, got1_ref, down_send.at[0], down_recv.at[0], (s, flip(z, 1))),
+        remote(down2_ref, got2_ref, down_send.at[1], down_recv.at[1], (s, flip(z, 2))),
+    ]
+    for one in results:
+        one.start()
     g_buf[s] = g_ref[...]
     gather = Gather(g_buf, s, z, send, recv, 128)
     gather.begin()
@@ -1155,121 +1165,42 @@
     work(flip(flip(s, 2), 4))
     work(gather.arrive_core(3))
     gather.end()
-
-
-def spread_layer(g_own, o_eff, mixed, b_row):
+    for one in results:
+        one.wait()
+
+
+def spread_layer(g_own, o_eff, mixed, b_row, down1, down2):
     bf16 = jnp.bfloat16
     vmem = pl.BlockSpec(memory_space=pltpu.VMEM)
+    anywhere = pl.BlockSpec(memory_space=pl.ANY)
     width = g_own.shape[1]
     shape = jax.ShapeDtypeStruct
     dma = pltpu.SemaphoreType.DMA
     return pl.pallas_call(
         spread_kernel,
-        in_specs=[vmem, vmem, vmem, vmem],
-        out_specs=[pl.BlockSpec(memory_space=pl.ANY), vmem, vmem, vmem],
+        in_specs=[vmem] * 4 + [anywhere] * 2,
+        out_specs=[anywhere, vmem, vmem, vmem, anywhere, anywhere],
         out_shape=[
             shape((8, 256, width), bf16),
             shape((8, 256, 256), bf16),
             shape((2, 8, 1, 256), jnp.float32),
             shape((8, 256, 16), bf16),
+            shape(down1.shape, bf16),
+            shape(down2.shape, bf16),
         ],
         scratch_shapes=[
             pltpu.VMEM((8, 256, width), bf16),
             dma((gather_sems,)),
             dma((gather_sems,)),
             dma((1,)),
+            dma((2,)),
+            dma((2,)),
         ],
         cost_estimate=spend(40),
         compiler_params=pltpu.CompilerParams(
             collective_id=3, has_side_effects=True, vmem_limit_bytes=48 << 20
         ),
-    )(g_own, o_eff, mixed, b_row)
-
-
-def in_kernel(
-    dq_ref, dk_ref, dv_ref, w_ref, x_own_ref, residual_ref,
-    grad_ref, own_ref, sib_q, sib_k, sib_v, out_buf, in_buf, a2a_send, a2a_recv, sib_send, sib_recv, send, recv,
-):
-    s, z = places()
-    core = s % 2
-    other = flip(s, 1)
-    zs = [flip(z, 1), flip(z, 2), 3 - z]
-    meet([(None, (other, z)), (None, (flip(s, 2), z)), (None, (flip(s, 4), z))] + [(None, (s, j)) for j in zs])
-    mine = (dq_ref, dk_ref, dv_ref)
-    theirs = (sib_q, sib_k, sib_v)
-    swaps = [
-        remote(
-            mine[p].at[2 * c + 1 - core], theirs[p].at[c], sib_send.at[4 * p + c], sib_recv.at[4 * p + c], (other, z)
-        )
-        for c in range(4)
-        for p in range(3)
-    ]
-    for one in swaps:
-        one.start()
-    for one in swaps:
-        one.wait_recv()
-
-    def product(chip, half):
-        rows = pl.ds(half * 128, 128)
-        both = jnp.concatenate(
-            [ref[2 * chip + core, rows, :] for ref in mine] + [ref[chip, rows, :] for ref in theirs], axis=1
-        )
-        return dot_nt(both, w_ref[...])
-
-    reduce = Reduce(product, s, z, out_buf, in_buf, send, recv)
-    reduce.begin()
-    reduce.middle()
-    for half in range(2):
-        total = reduce.finish(half)
-        x = x_own_ref[2 * half : 2 * half + 2].reshape(128, -1).astype(jnp.float32)
-        normed, inverse = norm_rows(x)
-        value = residual_ref[pl.ds(half * 128, 128), :] + norm_back(total, normed, inverse)
-        own_ref[2 * half : 2 * half + 2] = value.astype(jnp.bfloat16).reshape(2, 64, -1)
-    backs = [
-        remote(own_ref.at[j], grad_ref.at[z], a2a_send.at[d], a2a_recv.at[d], (s, j)) for d, j in enumerate(zs)
-    ]
-    for one in backs:
-        one.start()
-    grad_ref[z] = own_ref[z]
-    for one in swaps:
-        one.wait_send()
-    reduce.end()
-    for d, j in enumerate(zs):
-        remote(own_ref.at[j], grad_ref.at[j], a2a_send.at[d], a2a_recv.at[d], (s, j)).wait_recv()
-    for one in backs:
-        one.wait_send()
-
-
-def in_layer(dq, dk, dv, w_cat, x_own, grad_residual):
-    bf16 = jnp.bfloat16
-    vmem = pl.BlockSpec(memory_space=pltpu.VMEM)
-    width = x_own.shape[2]
-    dma = pltpu.SemaphoreType.DMA
-
-    return pl.pallas_call(
-        in_kernel,
-        in_specs=[vmem] * 6,
-        out_specs=vmem,
-        out_shape=jax.ShapeDtypeStruct((4, 64, width), bf16),
-        scratch_shapes=[
-            pltpu.VMEM((4, 64, width), bf16),
-            pltpu.VMEM((4, 256, 256), bf16),
-            pltpu.VMEM((4, 256, 256), bf16),
-            pltpu.VMEM((4, 256, 256), bf16),
-            pltpu.VMEM((6, 128, width), bf16),
-            pltpu.VMEM((6, 128, width), bf16),
-            dma((3,)),
-            dma((3,)),
-            dma((12,)),
-            dma((12,)),
-            dma((6,)),
-            dma((6,)),
-        ],
-        cost_estimate=spend(80),
-        compiler_params=pltpu.CompilerParams(
-            collective_id=4, has_side_effects=True, vmem_limit_bytes=48 << 20
-        ),
-    )(dq, dk, dv, w_cat, x_own, grad_residual)
+    )(g_own, o_eff, mixed, b_row, down1, down2)
 
 
 def mlp_line_kernel(
@@ -1621,6 +1552,316 @@
     )(m_own, residual, *cots, w_gate_up, w_down, a_sel, b_sel, ad_sel, bd_sel)
 
 
+def finish_kernel(
+    dq_ref, dk_ref, dv_ref, w_ref, x_own_ref, residual_ref, u_ref, g_ref, low_ref, rank_ref, mixed_ref,
+    b_sel_ref, a_sel_ref, grad_b_ref, grad_ad_ref, grad_a_ref, grad_bd_ref, down0_ref, got1_ref, got2_ref, down3_ref,
+    set_ref,
+    result_ref, grad_ref, pool_ref, heads_ref, got3_ref,
+    own_ref, sib_q, sib_k, sib_v, out_buf, in_buf, u_buf, g_buf, a_acc, b_acc, chunk_src, chunk_sib, chunk_sum,
+    chunk_in, z_src, z_in, head_src, head_in,
+    a2a_send, a2a_recv, sib_send, sib_recv, send, recv, load_sem, cs_send, cs_recv, cx_send, cx_recv,
+    cz_send, cz_recv, cg_send, cg_recv, hz_send, hz_recv, hg_send, hg_recv, down_send, down_recv,
+):
+    f32 = jnp.float32
+    bf16 = jnp.bfloat16
+    s, z = places()
+    core = s % 2
+    chip = s // 2
+    other = flip(s, 1)
+    sx = flip(s, 2)
+    sy = flip(s, 4)
+    sd = flip(sx, 4)
+    zs = [flip(z, 1), flip(z, 2), 3 - z]
+    meet([(None, (t, z)) for t in (other, sx, sy, sd)] + [(None, (s, j)) for j in zs])
+    last_down = remote(down3_ref, got3_ref, down_send.at[0], down_recv.at[0], (s, 3 - z))
+    last_down.start()
+    mine = (dq_ref, dk_ref, dv_ref)
+    theirs = (sib_q, sib_k, sib_v)
+    swaps = [
+        remote(
+            mine[p].at[2 * c + 1 - core], theirs[p].at[c], sib_send.at[4 * p + c], sib_recv.at[4 * p + c], (other, z)
+        )
+        for c in range(4)
+        for p in range(3)
+    ]
+    for one in swaps:
+        one.start()
+
+    def load(t):
+        return [
+            pltpu.make_async_copy(u_ref.at[t], u_buf.at[t % 2], load_sem.at[t % 2]),
+            pltpu.make_async_copy(g_ref.at[t], g_buf.at[t % 2], load_sem.at[2 + t % 2]),
+        ]
+
+    for one in load(0):
+        one.start()
+    for one in swaps:
+        one.wait_recv()
+
+    def product(c, half):
+        rows = pl.ds(half * 128, 128)
+        both = jnp.concatenate(
+            [ref[2 * c + core, rows, :] for ref in mine] + [ref[c, rows, :] for ref in theirs], axis=1
+        )
+        return dot_nt(both, w_ref[...])
+
+    reduce = Reduce(product, s, z, out_buf, in_buf, send, recv)
+    reduce.begin()
+
+    b_two = [
+        jnp.concatenate(
+            [b_sel_ref[2 * core, 16 * p : 16 * p + 16], b_sel_ref[2 * core + 1, 16 * p : 16 * p + 16]], axis=1
+        )
+        for p in range(3)
+    ]
+    a_two = jnp.concatenate([a_sel_ref[2 * core], a_sel_ref[2 * core + 1]], axis=1)
+
+    def adapt(t, first):
+        for one in load(t):
+            one.wait()
+        if t < 7:
+            for one in load(t + 1):
+                one.start()
+        back = jnp.concatenate([dot_nt(mine[p][t], b_two[p]) for p in range(3)], axis=1)
+        back = (adapt_scale * back).astype(bf16)
+        a_part = dot_tn(back, u_buf[t % 2])
+        lows = (adapt_scale * dot_nt(mixed_ref[t], a_two)).astype(bf16)
+        b_part = dot_tn(lows, g_buf[t % 2])
+        if first:
+            a_acc[...] = a_part
+            b_acc[...] = b_part
+        else:
+            a_acc[...] += a_part
+            b_acc[...] += b_part
+
+    for t in range(3):
+        adapt(t, t == 0)
+    reduce.middle()
+    for t in range(3, 8):
+        adapt(t, False)
+    per_head = [
+        dot_tn(low_ref[...].reshape(2048, 48)[:, 16 * p : 16 * p + 16], mine[p][...].reshape(2048, 256))
+        for p in range(3)
+    ] + [dot_tn(rank_ref[...].reshape(2048, 16), mixed_ref[...].reshape(2048, 256))]
+    for head in range(2):
+        columns = slice(HDIM * head, HDIM * head + HDIM)
+        head_src[head] = jnp.concatenate([part[:, columns] for part in per_head], axis=0).astype(bf16)
+
+    keeper = (z // 2) == core
+
+    def head_copy(head):
+        return remote(head_src.at[head], head_in.at[z], hz_send.at[head], hz_recv.at[z], (s, 2 * core + head))
+
+    for head in range(2):
+
+        @pl.when(2 * core + head != z)
+        def _():
+            head_copy(head).start()
+
+        @pl.when(2 * core + head == z)
+        def _():
+            head_in[z] = head_src[head]
+
+    for member in range(4):
+        whole = jnp.zeros((48, a_acc.shape[1]), f32)
+        split = jnp.zeros((48, a_acc.shape[1]), f32)
+        for seq in range(4):
+            used = (set_ref[seq] == member).astype(f32)
+            whole += used * jnp.concatenate([grad_a_ref[seq], grad_bd_ref[seq]], axis=0)
+            split += used * jnp.concatenate([grad_b_ref[seq, 0], grad_b_ref[seq, 1], grad_ad_ref[seq]], axis=0)
+        for part in range(2):
+            i = 2 * member + part
+            sequence = a_acc[8 * i : 8 * i + 8] if i < 6 else b_acc[8 * i - 48 : 8 * i - 40]
+            chunk_src[i] = jnp.concatenate(
+                [
+                    whole[24 * part : 24 * part + 24],
+                    sequence,
+                    split[24 * part : 24 * part + 24],
+                    jnp.zeros((8, a_acc.shape[1]), f32),
+                ],
+                axis=0,
+            ).astype(bf16)
+    crosses = [
+        remote(chunk_src.at[2 * c + 1 - core], chunk_sib.at[c], cs_send.at[c], cs_recv.at[c], (other, z))
+        for c in range(4)
+    ]
+    for one in crosses:
+        one.start()
+    for one in crosses:
+        one.wait_recv()
+    for c in range(4):
+        chunk_sum[c] = (chunk_src[2 * c + core].astype(f32) + chunk_sib[c].astype(f32)).astype(bf16)
+    around = [
+        remote(chunk_sum.at[t // 2], chunk_in.at[d], cx_send.at[d], cx_recv.at[d], (t, z))
+        for d, t in enumerate((sx, sy, sd))
+    ]
+    for one in around:
+        one.start()
+
+    for half in range(2):
+        total = reduce.finish(half)
+        x = x_own_ref[2 * half : 2 * half + 2].reshape(128, -1).astype(f32)
+        normed, inverse = norm_rows(x)
+        value = residual_ref[pl.ds(half * 128, 128), :] + norm_back(total, normed, inverse)
+        own_ref[2 * half : 2 * half + 2] = value.astype(bf16).reshape(2, 64, -1)
+    backs = [
+        remote(own_ref.at[j], grad_ref.at[z], a2a_send.at[d], a2a_recv.at[d], (s, j)) for d, j in enumerate(zs)
+    ]
+    for one in backs:
+        one.start()
+    grad_ref[z] = own_ref[z]
+
+    last_down.wait_recv()
+    for part in range(4):
+        result_ref[part] = (
+            down0_ref[part].astype(f32)
+            + got1_ref[part].astype(f32)
+            + got2_ref[part].astype(f32)
+            + got3_ref[part].astype(f32)
+        ).astype(bf16)
+    for one in around:
+        one.wait_recv()
+    chunk = chunk_sum[chip].astype(f32)
+    for d in range(3):
+        chunk += chunk_in[d].astype(f32)
+    z_src[...] = chunk[0:32].astype(bf16)
+    along = [remote(z_src, z_in.at[d], cz_send.at[d], cz_recv.at[d], (s, j)) for d, j in enumerate(zs)]
+    for one in along:
+        one.start()
+
+    def head_spread(target, index):
+        return remote(heads_ref.at[chip], heads_ref.at[chip], hg_send.at[index], hg_recv.at[index], (target, z))
+
+    def head_pass(t, index):
+        c = t // 2
+        return remote(heads_ref.at[c], heads_ref.at[c], hg_send.at[index], hg_recv.at[index], (other, z))
+
+    @pl.when(keeper)
+    def _():
+        for j in range(4):
+
+            @pl.when(z != j)
+            def _():
+                remote(head_src.at[0], head_in.at[j], hz_send.at[0], hz_recv.at[j], (s, j)).wait_recv()
+
+        for member in range(4):
+            total = jnp.zeros((64, HDIM), f32)
+            for seq in range(4):
+                total += (set_ref[seq] == member).astype(f32) * head_in[seq].astype(f32)
+            heads_ref[chip, pl.ds(64 * member, 64)] = total.astype(bf16)
+        for index, target in enumerate((sx, sy, sd, other)):
+            head_spread(target, index).start()
+
+    for one in along:
+        one.wait_recv()
+    whole = chunk[0:24]
+    places_z = [z] + zs
+    parts = [chunk[24:32]] + [z_in[d, 24:32].astype(f32) for d in range(3)]
+    for d in range(3):
+        whole += z_in[d, 0:24].astype(f32)
+    by_member = [
+        sum((set_ref[places_z[d]] == member).astype(f32) * parts[d] for d in range(4)) for member in range(4)
+    ]
+    pool_ref[s] = jnp.concatenate([whole] + by_member + [chunk[32:56]], axis=0).astype(bf16)
+
+    def pool_copy(t, index, target):
+        return remote(pool_ref.at[t], pool_ref.at[t], cg_send.at[index], cg_recv.at[index], (target, z))
+
+    gives = [pool_copy(s, index, target) for index, target in enumerate((sx, sy, sd, other))]
+    for one in gives:
+        one.start()
+
+    @pl.when(keeper)
+    def _():
+        for index, t in enumerate((sx, sy, sd)):
+            head_pass(t, index).wait_recv()
+            head_pass(t, 4 + index).start()
+
+    for index, t in enumerate((sx, sy, sd)):
+        pool_copy(t, index, other).wait_recv()
+        pool_copy(t, 4 + index, other).start()
+    pool_copy(other, 3, other).wait_recv()
+    for index, t in enumerate((sx, sy, sd)):
+        pool_copy(flip(t, 1), 4 + index, other).wait_recv()
+
+    @pl.when(z // 2 != core)
+    def _():
+        head_spread(other, 3).wait_recv()
+        for index, t in enumerate((sx, sy, sd)):
+            head_pass(t, 4 + index).wait_recv()
+
+    for d, j in enumerate(zs):
+        remote(own_ref.at[j], grad_ref.at[j], a2a_send.at[d], a2a_recv.at[d], (s, j)).wait_recv()
+    for one in swaps + crosses + around + backs + along + gives + [last_down]:
+        one.wait_send()
+    for index, t in enumerate((sx, sy, sd)):
+        pool_copy(t, 4 + index, other).wait_send()
+    reduce.end()
+    for head in range(2):
+
+        @pl.when(2 * core + head != z)
+        def _():
+            head_copy(head).wait_send()
+
+    @pl.when(keeper)
+    def _():
+        for index, target in enumerate((sx, sy, sd, other)):
+            head_spread(target, index).wait_send()
+        for index, t in enumerate((sx, sy, sd)):
+            head_pass(t, 4 + index).wait_send()
+
+
+def finish_layer(*operands):
+    bf16 = jnp.bfloat16
+    f32 = jnp.float32
+    vmem = pl.BlockSpec(memory_space=pltpu.VMEM)
+    anywhere = pl.BlockSpec(memory_space=pl.ANY)
+    width = operands[4].shape[2]
+    dma = pltpu.SemaphoreType.DMA
+    vm = pltpu.VMEM
+    shape = jax.ShapeDtypeStruct
+    return pl.pallas_call(
+        finish_kernel,
+        in_specs=[vmem] * 6 + [anywhere] * 2 + [vmem] * 13 + [pl.BlockSpec(memory_space=pltpu.SMEM)],
+        out_specs=[vmem] * 5,
+        out_shape=[
+            shape((4, 64, width), bf16),
+            shape((4, 64, width), bf16),
+            shape((8, 80, width), bf16),
+            shape((4, 256, HDIM), bf16),
+            shape((4, 64, width), bf16),
+        ],
+        scratch_shapes=[
+            vm((4, 64, width), bf16),
+            vm((4, 256, 256), bf16),
+            vm((4, 256, 256), bf16),
+            vm((4, 256, 256), bf16),
+            vm((6, 128, width), bf16),
+            vm((6, 128, width), bf16),
+            vm((2, 256, width), bf16),
+            vm((2, 256, width), bf16),
+            vm((48, width), f32),
+            vm((16, width), f32),
+            vm((8, 64, width), bf16),
+            vm((4, 64, width), bf16),
+            vm((4, 64, width), bf16),
+            vm((3, 64, width), bf16),
+            vm((32, width), bf16),
+            vm((3, 32, width), bf16),
+            vm((2, 64, HDIM), bf16),
+            vm((4, 64, HDIM), bf16),
+        ]
+        + [
+            dma((count,))
+            for count in (3, 3, 12, 12, 6, 6, 4, 4, 4, 3, 3, 3, 3, 7, 7, 2, 4, 7, 7, 1, 1)
+        ],
+        cost_estimate=spend(80),
+        compiler_params=pltpu.CompilerParams(
+            collective_id=4, has_side_effects=True, vmem_limit_bytes=58 << 20
+        ),
+    )(*operands)
+
+
 def swap_mp(values, d):
     pairs = [(s * 4 + z, s * 4 + (z ^ d)) for s in range(lax.axis_size("seq")) for z in range(4)]
     return lax.ppermute(values, ("seq", "mp"), pairs)
@@ -1635,15 +1876,6 @@
     cos = jnp.cos(angles)
     sin = jnp.sin(angles)
     return (jnp.concatenate([cos, cos], axis=1), jnp.concatenate([sin, -sin], axis=1))
-
-
-def by_sets(set_ids, grads, sets):
-    return jnp.stack(
-        [
-            sum(jnp.where(one == member, grad, 0.0) for one, grad in zip(set_ids, grads))
-            for member in range(sets)
-        ]
-    )
 
 
 def pick(values, index, axis=0):
@@ -1698,20 +1930,9 @@
     g_own, grad_residual, down0, down1, down2, down3, grad_b_mlp, grad_ad, grad_a_mlp, grad_bd = mlp_line(
         m_own, residual, cots, w_gate_up, w_down, a_sel, b_sel_mlp, ad_sel, bd_sel
     )
-    result = down0.astype(f32)
-    for d, part in ((1, down1), (2, down2), (3, down3)):
-        result = result + swap_mp(part, d).astype(f32)
-    result = result.astype(bf16)
-
-    set_ids = [set_index[q_] for q_ in range(4)]
-    sum_b_gate_up = by_sets(set_ids, [grad_b_mlp[q_] for q_ in range(4)], sets).astype(bf16)
-    sum_a_down = by_sets(set_ids, [grad_ad[q_] for q_ in range(4)], sets).astype(bf16)
-    sum_a_mlp = by_sets(set_ids, [grad_a_mlp[q_].reshape(2, rank, width) for q_ in range(4)], sets).astype(bf16)
-    sum_b_down = by_sets(set_ids, [grad_bd[q_] for q_ in range(4)], sets).astype(bf16)
-    sum_b_gate_up, sum_a_down = lax.psum((sum_b_gate_up, sum_a_down), "seq")
-    sum_a_mlp, sum_b_down = lax.psum((sum_a_mlp, sum_b_down), ("seq", "mp"))
-
-    g, grad_mixed, dots, out_rank = spread_layer(g_own, o_eff, mixed.reshape(8, 256, 256), bo_set[0])
+    g, grad_mixed, dots, out_rank, got1, got2 = spread_layer(
+        g_own, o_eff, mixed.reshape(8, 256, 256), bo_set[0], down1, down2
+    )
     dq, dk, dv = attend_back(
         flat(q), flat(k), flat(v), flat(grad_mixed), lse, dots.reshape(2, 1, length), cos, sin
     )
@@ -1719,53 +1940,25 @@
     def spans(values):
         return values.reshape(8, 256, 256)
 
-    grad_in = in_layer(spans(dq), spans(dk), spans(dv), w_cat, x_own, grad_residual)
-
-    my_b = lax.dynamic_slice_in_dim(b_sel.reshape(4, 3, rank, HDIM), 2 * core, 2, 0)
-    my_a = lax.dynamic_slice_in_dim(a_out_sel, 2 * core, 2, 0)
-    d_parts = [d.reshape(length, 2, HDIM) for d in (dq, dk, dv)]
-    back_rank = jnp.concatenate(
-        [
-            adapt_scale * jnp.einsum("thk,hrk->tr", d_parts[p], my_b[:, p], preferred_element_type=f32)
-            for p in range(3)
-        ],
-        axis=1,
-    ).astype(bf16)
-    grad_a_qkv = dot_tn(back_rank, flat(u)).reshape(3, rank, width)
-    low = flat(low)
-    grad_b_qkv = jnp.stack(
-        [dot_tn(low[:, rank * p : rank * p + rank], d) for p, d in enumerate((dq, dk, dv))]
-    )
-    grad_a_out = dot_tn(flat(out_rank), mixed)
-    out_low = (
-        adapt_scale
-        * jnp.einsum("thk,hrk->tr", mixed.reshape(length, 2, HDIM), my_a, preferred_element_type=f32)
-    ).astype(bf16)
-    grad_b_out = dot_tn(out_low, flat(g))
-
-    def in_set(values):
-        return jnp.stack([jnp.where(my_set == member, values, 0.0) for member in range(sets)]).astype(bf16)
-
-    def in_heads(values):
-        pairs = values.reshape(values.shape[:-1] + (2, HDIM))
-        out = jnp.zeros(values.shape[:-1] + (4, 4 * HDIM), values.dtype)
-        start = (0,) * (values.ndim - 1) + (2 * core, chip * HDIM)
-        return lax.dynamic_update_slice(out, pairs, start)
-
-    grad_b_out, _ = lax.optimization_barrier((grad_b_out, sum_b_down))
-    sum_a_qkv, sum_b_out, sum_b_qkv, sum_a_out = lax.psum(
-        (in_set(grad_a_qkv), in_set(grad_b_out), in_set(in_heads(grad_b_qkv)), in_set(in_heads(grad_a_out))),
-        ("seq", "mp"),
-    )
+    result, grad_in, pool, heads, _ = finish_layer(
+        spans(dq), spans(dk), spans(dv), w_cat, x_own, grad_residual, u, g, low, out_rank, spans(mixed),
+        b_sel, a_out_sel, grad_b_mlp, grad_ad, grad_a_mlp, grad_bd, down0, got1, got2, down3, set_index,
+    )
+    pool = pool.astype(f32)
+    whole = pool[:, 0:24].reshape(sets, 48, width)
+    sequence = jnp.transpose(pool[:, 24:56].reshape(8, sets, 8, width), (1, 0, 2, 3)).reshape(sets, 64, width)
+    split = pool[:, 56:80].reshape(sets, 48, width)
+    heads = heads.astype(f32).reshape(4, sets, 64, HDIM)
+    heads = jnp.transpose(heads, (1, 2, 0, 3)).reshape(sets, 4, rank, 4 * HDIM)
     return (
         result,
         grad_in,
-        jnp.concatenate([sum_a_qkv, sum_a_mlp], axis=1).astype(f32),
-        pick(sum_b_qkv, z, 3).astype(f32),
-        sum_b_gate_up.astype(f32),
-        pick(sum_a_out, z, 2).astype(f32),
-        sum_a_down.astype(f32),
-        jnp.stack([sum_b_out, sum_b_down], axis=1).astype(f32),
+        jnp.concatenate([sequence[:, :48], whole[:, :32]], axis=1).reshape(sets, 5, rank, width),
+        heads[:, :3],
+        split[:, :32].reshape(sets, 2, rank, width),
+        heads[:, 3],
+        split[:, 32:],
+        jnp.stack([sequence[:, 48:], whole[:, 32:]], axis=1),
     )
 
 

time: 867 us -> 574 us (0.66)
  waiting for transfers between devices: 251 us -> 0.98 us
  Pallas kernels: 461 us -> 498 us
  other arithmetic: 43.1 us -> 12.7 us
  between operations: 37.3 us -> 11.1 us
  matrix products: 17.6 us -> 0 us
    psum x3 -> x0, waiting for transfers between devices: 251 us -> none  [the longest x2 251 us: per_device_layers(): sum_a_mlp, sum_b_down = lax.psum((sum_a_mlp, sum_b_down), ('seq', 'mp'))]
    pallas_call x2, Pallas kernels: 128 us -> 172 us  [the longest x1 116 us: finish_layer(): pl.pallas_call(finish_kernel, in_specs=[vmem] * 6 + [anywhere] * 2 + [vme...]
    dot_general x9 -> x0, matrix products: 17.6 us -> none  [the longest x6 14.5 us: dot_tn(): lax.dot_general(a, b, (((0,), (0,)), ((), ())), preferred_element_type=jn...]
    another operation x19 -> x1, other arithmetic: 18.3 us -> 1.04 us  [per_device_layers(): jnp.stack([sequence[:, 48:], whole[:, 32:]], axis=1)]
    convert_element_type x7 -> x1, other arithmetic: 13.6 us -> 0.67 us  [per_device_layers(): pool = pool.astype(f32)]
  transfers between devices with their start and end apart: 9 -> 3, of which waited for: 2 -> 1; matrix products, arithmetic and copies ran while one was open for 5% -> 1% of each run, Pallas kernels for 17% -> 11%
where the time goes in v2:
time: 574 us; the launch traced here: 567 us
  Pallas kernels  498 us (87%)
  local copies, waits for them, and re-layouts  26.1 us (5%)
  other arithmetic  12.7 us (2%)
  between operations  11.1 us (2%)
  blocking collectives  9.34 us (2%)
  starting transfers between devices  8.92 us (2%)
    pallas_call x1, Pallas kernels, mlp_line(): pl.pallas_call(mlp_line_kernel, in_specs=[vmem, vmem] + [anywhere] * 6 +...  137 us
    pallas_call x1, Pallas kernels, finish_layer(): pl.pallas_call(finish_kernel, in_specs=[vmem] * 6 + [anywhere] * 2 + [vme...  116 us
    pallas_call x1, Pallas kernels, start_layer(): pl.pallas_call(start_kernel, in_specs=[vmem, vmem, anywhere, vmem, vmem,...  105 us
    pallas_call x1, Pallas kernels, spread_layer(): pl.pallas_call(spread_kernel, in_specs=[vmem] * 4 + [anywhere] * 2, out_s...  56.7 us
    pallas_call x1, Pallas kernels, out_layer(): pl.pallas_call(out_kernel, in_specs=[vmem, vmem, vmem, vmem, pl.BlockSpec...  47 us
    pallas_call x1, Pallas kernels, attend_back(): pl.pallas_call(attend_back_kernel, grid=(heads, length // tile), in_specs...  22 us
    pallas_call x1, Pallas kernels, attend(): pl.pallas_call(attend_kernel, grid=(heads, length // tile), in_specs=[pl....  15.8 us
  transfers between devices with their start and end apart: 3, of which 1 were waited for; matrix products, arithmetic and copies ran while one was open for 1% of the time, Pallas kernels for 11%

profile of v2, /device:TPU:13, one launch (start us, length us, event | category | flops | bytes accessed | tf_op | source)
XLA Modules:
  0.0 567.4 jit_solution(17060417716656128003)
XLA Ops:
  0.7 1.5 fusion.2
  3.5 0.7 constant_dynamic-slice_fusion.13
  4.2 9.3 %all-gather = s32[1,2048]{1,0:T(1,128)S(1)} all-gather(s32[1,256]{1,0:T(1,128)S(1)} %constant_dynamic-slice_fusion.13), channel_id=2, replica_groups=mesh['seq'=8,'mp'=4] {'seq'}, dimensions={1}, use_global_device_ids=true | all-gather | bytes 9216 | tf_op jit(solution)/shard_map/all_gather | solution.py:1913
  13.6 0.7 constant_dynamic-slice_fusion.14
  14.3 1.7 dynamic_slice.80.o_ref
  16.0 1.2 constant_dynamic-slice_fusion.16
  17.9 0.7 constant_dynamic-slice_fusion.12
  18.6 3.7 multiply_sine_fusion
  22.3 1.0 pad_maximum_fusion.4.w_ref
  23.2 1.9 pad_maximum_fusion.1
  25.2 104.5 %shard_map.197 = (bf16[4,64,2048]{2,1,0:T(8,128)(2,1)}, bf16[256,2048]{1,0:T(8,128)(2,1)}, bf16[8,256,2048]{2,1,0:T(8,128)(2,1)}, bf16[4,2,3328,128]{3,2,1,0:T(8...) custom-call(bf16[4,64,2048]{2,1,0:T(8,128)(2,1)} %x_ref.1, ...), custom_call_target="tpu_custom_call" | custom-call | flops 80000000000 | bytes 1000000 | tf_op jit(solution)/shard_map/pallas_call | solution.py:928
  129.7 1.6 collective-permute-start.2
  131.3 7.0 %collective-permute-start.1 = (bf16[4,64,2048]{2,1,0:T(8,128)(2,1)S(1)}, bf16[4,64,2048]{2,1,0:T(8,128)(2,1)}, u32[]{:S(2)}, u32[]{:S(2)}) collective-permute-start(bf16[4,64,2048]{2,1,0:T(8,128)(2,1)S(1)} %copy-done.27), channel_id=1, source_target_pairs={{0,2},{1,3},{2,0},{3,1},{4,6},{5,7},{6,4},{7,5},{8,10},{9,11},{10,... | collective-permute-start | bytes 3145736 | tf_op jit(solution)/shard_map/ppermute | solution.py:1867
  138.3 0.4 collective-permute-start
  146.6 0.7 dynamic-slice_bitcast_fusion.3
  147.3 1.2 copy-done.5
  148.5 1.2 copy-done.7
  149.7 1.2 copy-done.9
  150.9 15.8 %shard_map.198 = (bf16[2048,256]{1,0:T(8,128)(2,1)S(1)}, f32[2,1,2048]{2,1,0:T(1,128)S(1)}) custom-call(bf16[2048,256]{1,0:T(8,128)(2,1)S(1)} %bitcast.55, bf16[2048,256]{1,0:T(8,128)(2,1)S(1)} %bitcast.57, bf16[2048,256]{1,0:T(8,128)(2,1)S(1)} %bitcast.59), custom_call_target="tpu_custom_call" | custom-call | flops 2147483648 | bytes 4194304 | tf_op jit(solution)/shard_map/pallas_call | solution.py:481
  166.7 1.0 copy-done.11
  167.7 47.0 %shard_map.199 = (f32[256,2048]{1,0:T(8,128)}, bf16[256,2048]{1,0:T(8,128)(2,1)}, bf16[256,2048]{1,0:T(8,128)(2,1)}, bf16[2048,1536]{1,0:T(8,128)(2,1)}) custom-call(bf16[8,256,256]{2,1,0:T(8,128)(2,1)} %bitcast.61, bf16[4,2,128,1024]{3,2,1,0:T(8,128)(2,1)} %get-tuple-element.52.o_all, bf16[4,16,128]{2,1,0:T(8,128)(2,1)} %get-tuple-element.53.a_sel_ref, ...), custom_call_target="tpu_custom_call" | custom-call | flops 44999999488 | bytes 1000000 | tf_op jit(solution)/shard_map/pallas_call | solution.py:1093
  214.8 0.9 pad_maximum_fusion.5.a_ref
  215.7 0.9 pad_maximum_fusion.6.b_ref
  216.5 0.9 pad_maximum_fusion.7
  217.4 1.0 collective-permute-done.1.cot2_ref
  218.4 136.7 %shard_map.200 = (bf16[256,2048]{1,0:T(8,128)(2,1)}, f32[256,2048]{1,0:T(8,128)}, bf16[4,64,2048]{2,1,0:T(8,128)(2,1)}, bf16[4,64,2048]{2,1,0:T(8,128)(2,1)}, bf...) custom-call(bf16[256,2048]{1,0:T(8,128)(2,1)} %get-tuple-element.57., ...), custom_call_target="tpu_custom_call" | custom-call | flops 109999996928 | bytes 1000000 | tf_op jit(solution)/shard_map/pallas_call | solution.py:1512
  355.1 1.2 copy-done.18
  356.4 56.7 %shard_map.201 = (bf16[8,256,2048]{2,1,0:T(8,128)(2,1)}, bf16[8,256,256]{2,1,0:T(8,128)(2,1)S(1)}, f32[2,8,1,256]{3,2,1,0:T(1,128)S(1)}, bf16[8,256,16]{2,1,0:T(...) custom-call(bf16[256,2048]{1,0:T(8,128)(2,1)S(1)} %copy-done.18, ...), custom_call_target="tpu_custom_call" | custom-call | flops 40000000000 | bytes 1000000 | tf_op jit(solution)/shard_map/pallas_call | solution.py:1179
  413.2 22.0 %shard_map.202 = (bf16[2048,256]{1,0:T(8,128)(2,1)S(1)}, bf16[2048,256]{1,0:T(8,128)(2,1)S(1)}, bf16[2048,256]{1,0:T(8,128)(2,1)S(1)}) custom-call(bf16[2048,256]{1,0:T(8,128)(2,1)S(1)} %bitcast.56, bf16[2048,256]{1,0:T(8,128)(2,1)S(1)} %bitcast.58, bf16[2048,256]{1,0:T(8,128)(2,1)S(1)} %bitcast.60, bf16[2048,256]{1,0:T(8,128)(2,1)S(1)} %bitcast.67, ...), custom_call_target="tpu_custom_call" | custom-call | flops 5368709120 | bytes 7340032 | tf_op jit(solution)/shard_map/pallas_call | solution.py:558
  435.2 1.0 copy-done.12
  436.2 1.0 copy-done.13
  437.2 1.0 copy-done.14
  438.1 115.5 %shard_map.203 = (bf16[4,64,2048]{2,1,0:T(8,128)(2,1)}, bf16[4,64,2048]{2,1,0:T(8,128)(2,1)}, bf16[8,80,2048]{2,1,0:T(8,128)(2,1)}, bf16[4,256,128]{2,1,0:T(8,128)(2,1)}, bf16[4,64,2048]{2,1,0:T(8,128)(2,1)}) custom-call(bf16[8,256,256]{2,1,0:T(8,128)(2,1)} %bitcast.64, bf16[8,256,256]{2,1,0:T(8,128)(2,1)} %bitcast.65, bf16[8,256,256]{2,1,0:T(8,128)(2,1)} %bitcast.66, ...), custom_call_target="tpu_custom_call" | custom-call | flops 80000000000 | bytes 1000000 | tf_op jit(solution)/shard_map/pallas_call | solution.py:1823
  553.7 2.1 copy.28
  555.8 1.3 reshape.133
  557.0 0.7 slice_bitcast_fusion.3
  557.7 0.8 slice.139
  558.5 0.4 fusion.1
  559.0 0.8 slice.143
  559.8 1.0 slice.141
  560.9 0.7 convert_element_type.8
  561.5 0.1 copy_bitcast_fusion
  561.7 0.1 slice.136
  561.8 1.8 pad_maximum_fusion
  563.6 1.0 pad_maximum_fusion.3
  564.7 0.6 copy-done.22
  565.2 1.0 copy.31
  566.2 1.0 copy.32
  (58 shorter events, 0.4 us)
Async XLA Ops:
  0.6 13.7 %copy-start = (bf16[4,3,16,512]{3,2,1,0:T(8,128)(2,1)S(1)}, bf16[4,3,16,512]{3,2,1,0:T(8,128)(2,1)}, u32[]{:S(2)}) copy-start(bf16[4,3,16,512]{3,2,1,0:T(8,128)(2,1)} %param.20) | copy-start | bytes 589828
  0.6 17.2 %copy-start.24 = (bf16[4,5,16,2048]{3,2,1,0:T(8,128)(2,1)S(1)}, bf16[4,5,16,2048]{3,2,1,0:T(8,128)(2,1)}, u32[]{:S(2)}) copy-start(bf16[4,5,16,2048]{3,2,1,0:T(8,128)(2,1)} %param.19) | copy-start | bytes 3932164
  25.2 104.5 %copy-start.27 = (bf16[4,64,2048]{2,1,0:T(8,128)(2,1)S(1)}, bf16[4,64,2048]{2,1,0:T(8,128)(2,1)}, u32[]{:S(2)}) copy-start(bf16[4,64,2048]{2,1,0:T(8,128)(2,1)} %cot0_ref) | copy-start | bytes 3145732
  25.2 121.4 %copy-start.26 = (bf16[4,2,16,2048]{3,2,1,0:T(8,128)(2,1)S(1)}, bf16[4,2,16,2048]{3,2,1,0:T(8,128)(2,1)}, u32[]{:S(2)}) copy-start(bf16[4,2,16,2048]{3,2,1,0:T(8,128)(2,1)} %param.24) | copy-start | bytes 1572868
  129.7 87.7 %collective-permute-start.2 = (bf16[4,64,2048]{2,1,0:T(8,128)(2,1)S(1)}, bf16[4,64,2048]{2,1,0:T(8,128)(2,1)}, u32[]{:S(2)}, u32[]{:S(2)}) collective-permute-start(bf16[4,64,2048]{2,1,0:T(8,128)(2,1)S(1)} %copy-done.27), channel_id=1, source_target_pairs={{0,3},{1,2},{2,1},{3,0},{4,7},{5,6},{6,5},{7,4},{8,11},{9,10},{10,... | collective-permute-start | bytes 3145736 | tf_op jit(solution)/shard_map/ppermute | solution.py:1867
  131.3 87.1 %collective-permute-start.1 = (bf16[4,64,2048]{2,1,0:T(8,128)(2,1)S(1)}, bf16[4,64,2048]{2,1,0:T(8,128)(2,1)}, u32[]{:S(2)}, u32[]{:S(2)}) collective-permute-start(bf16[4,64,2048]{2,1,0:T(8,128)(2,1)S(1)} %copy-done.27), channel_id=1, source_target_pairs={{0,2},{1,3},{2,0},{3,1},{4,6},{5,7},{6,4},{7,5},{8,10},{9,11},{10,... | collective-permute-start | bytes 3145736 | tf_op jit(solution)/shard_map/ppermute | solution.py:1867
  138.3 80.1 %collective-permute-start = (bf16[4,64,2048]{2,1,0:T(8,128)(2,1)S(1)}, bf16[4,64,2048]{2,1,0:T(8,128)(2,1)}, u32[]{:S(2)}, u32[]{:S(2)}) collective-permute-start(bf16[4,64,2048]{2,1,0:T(8,128)(2,1)S(1)} %copy-done.27), channel_id=1, source_target_pairs={{0,1},{1,0},{2,3},{3,2},{4,5},{5,4},{6,7},{7,6},{8,9},{9,8},{10,11... | collective-permute-start | bytes 3145736 | tf_op jit(solution)/shard_map/ppermute | solution.py:1867
  147.3 1.2 copy-start.5
  148.5 1.2 copy-start.7
  149.7 1.2 copy-start.9
  166.7 1.0 copy-start.11
  167.7 47.0 %copy-start.25 = (bf16[4,16,2048]{2,1,0:T(8,128)(2,1)S(1)}, bf16[4,16,2048]{2,1,0:T(8,128)(2,1)}, u32[]{:S(2)}) copy-start(bf16[4,16,2048]{2,1,0:T(8,128)(2,1)} %param.23) | copy-start | bytes 786436
  167.7 47.1 %copy-start.23 = (bf16[4,2,16,2048]{3,2,1,0:T(8,128)(2,1)S(1)}, bf16[4,2,16,2048]{3,2,1,0:T(8,128)(2,1)}, u32[]{:S(2)}) copy-start(bf16[4,2,16,2048]{3,2,1,0:T(8,128)(2,1)} %param.21) | copy-start | bytes 1572868
  218.4 136.7 %copy-start.4 = (bf16[16,2048]{1,0:T(8,128)(2,1)S(1)}, bf16[16,2048]{1,0:T(8,128)(2,1)}, u32[]{:S(2)}) copy-start(bf16[16,2048]{1,0:T(8,128)(2,1)} %get-tuple-element.104.b_ref) | copy-start | bytes 196612
  218.4 136.7 %copy-start.15 = (bf16[256,2048]{1,0:T(8,128)(2,1)S(1)}, bf16[256,2048]{1,0:T(8,128)(2,1)}, u32[]{:S(2)}) copy-start(bf16[256,2048]{1,0:T(8,128)(2,1)} %get-tuple-element.61.o_eff_ref) | copy-start | bytes 3145732
  355.1 1.2 copy-start.18
  356.3 56.8 %copy-start.2 = (f32[2048,128]{1,0:T(8,128)S(1)}, f32[2048,128]{1,0:T(8,128)}, u32[]{:S(2)}) copy-start(f32[2048,128]{1,0:T(8,128)} %get-tuple-element.123.cos_ref) | copy-start | bytes 3145732
  356.3 56.8 %copy-start.3 = (f32[2048,128]{1,0:T(8,128)S(1)}, f32[2048,128]{1,0:T(8,128)}, u32[]{:S(2)}) copy-start(f32[2048,128]{1,0:T(8,128)} %get-tuple-element.124.sin_ref) | copy-start | bytes 3145732
  356.4 56.8 %copy-start.6 = (bf16[8,256,256]{2,1,0:T(8,128)(2,1)S(1)}, bf16[8,256,256]{2,1,0:T(8,128)(2,1)}, u32[]{:S(2)}) copy-start(bf16[8,256,256]{2,1,0:T(8,128)(2,1)} %get-tuple-element.48) | copy-start | bytes 3145732
  356.4 56.8 %copy-start.8 = (bf16[8,256,256]{2,1,0:T(8,128)(2,1)S(1)}, bf16[8,256,256]{2,1,0:T(8,128)(2,1)}, u32[]{:S(2)}) copy-start(bf16[8,256,256]{2,1,0:T(8,128)(2,1)} %get-tuple-element.49) | copy-start | bytes 3145732
  356.4 56.8 %copy-start.10 = (bf16[8,256,256]{2,1,0:T(8,128)(2,1)S(1)}, bf16[8,256,256]{2,1,0:T(8,128)(2,1)}, u32[]{:S(2)}) copy-start(bf16[8,256,256]{2,1,0:T(8,128)(2,1)} %get-tuple-element.50) | copy-start | bytes 3145732
  413.1 22.1 %copy-start.16 = (bf16[4,64,2048]{2,1,0:T(8,128)(2,1)}, bf16[4,64,2048]{2,1,0:T(8,128)(2,1)S(1)}, u32[]{:S(2)}) copy-start(bf16[4,64,2048]{2,1,0:T(8,128)(2,1)S(1)} %get-tuple-element.81.got1_ref) | copy-start | bytes 3145732
  413.1 22.1 %copy-start.17 = (bf16[4,64,2048]{2,1,0:T(8,128)(2,1)}, bf16[4,64,2048]{2,1,0:T(8,128)(2,1)S(1)}, u32[]{:S(2)}) copy-start(bf16[4,64,2048]{2,1,0:T(8,128)(2,1)S(1)} %get-tuple-element.82.got2_ref) | copy-start | bytes 3145732
  413.1 22.1 %copy-start.19 = (bf16[8,256,16]{2,1,0:T(8,128)(2,1)}, bf16[8,256,16]{2,1,0:T(8,128)(2,1)S(1)}, u32[]{:S(2)}) copy-start(bf16[8,256,16]{2,1,0:T(8,128)(2,1)S(1)} %get-tuple-element.75.rank_ref) | copy-start | bytes 196612
  435.2 1.0 copy-start.12
  436.2 1.0 copy-start.13
  437.2 1.0 copy-start.14
  553.7 4.8 copy-start.20
  563.6 1.6 copy-start.22
  563.6 2.6 copy-start.21
  564.7 2.5 copy-start.1

commit v3 on v2

--- a/solution.py
+++ b/solution.py
@@ -444,71 +444,16 @@
     return rows <= cols
 
 
-def attend_kernel(q_ref, k_ref, v_ref, o_ref, lse_ref):
-    i = pl.program_id(1)
-    tile = q_ref.shape[0]
-    factor = log2e / math.sqrt(HDIM)
-    q = q_ref[...]
-
-    def fold(j, carry, diagonal):
-        top, total, acc = carry
-        at = pl.ds(pl.multiple_of(j * tile, tile), tile)
-        scores = dot_nt(k_ref[at, :], q)
-        if diagonal:
-            scores = jnp.where(causal(scores, 0, 0), scores, far_below)
-        new_top = jnp.maximum(top, jnp.max(scores, axis=0, keepdims=True))
-        weight = jnp.exp2(scores * factor - new_top * factor)
-        keep = jnp.exp2((top - new_top) * factor)
-        total = total * keep + jnp.sum(weight, axis=0, keepdims=True)
-        acc = acc * keep + dot_tn(v_ref[at, :], weight.astype(jnp.bfloat16))
-        return (new_top, total, acc)
-
-    carry = (
-        jnp.full((1, tile), far_below, jnp.float32),
-        jnp.zeros((1, tile), jnp.float32),
-        jnp.zeros((HDIM, tile), jnp.float32),
-    )
-    carry = lax.fori_loop(0, i, lambda j, c: fold(j, c, False), carry)
-    top, total, acc = fold(i, carry, True)
-    o_ref[...] = jnp.transpose(acc / total).astype(o_ref.dtype)
-    lse_ref[0] = top * factor + jnp.log2(total)
-
-
-def attend(q, k, v):
-    length = q.shape[0]
-    heads = q.shape[1] // HDIM
-    tile = attn_tile
-    return pl.pallas_call(
-        attend_kernel,
-        grid=(heads, length // tile),
-        in_specs=[
-            pl.BlockSpec((tile, HDIM), lambda h, i: (i, h)),
-            pl.BlockSpec((length, HDIM), lambda h, i: (0, h)),
-            pl.BlockSpec((length, HDIM), lambda h, i: (0, h)),
-        ],
-        out_specs=[
-            pl.BlockSpec((tile, HDIM), lambda h, i: (i, h)),
-            pl.BlockSpec((1, 1, tile), lambda h, i: (h, 0, i)),
-        ],
-        out_shape=[
-            jax.ShapeDtypeStruct(q.shape, jnp.bfloat16),
-            jax.ShapeDtypeStruct((heads, 1, length), jnp.float32),
-        ],
-        cost_estimate=pl.CostEstimate(
-            flops=2 * heads * length * length * HDIM,
-            bytes_accessed=8 * length * heads * HDIM,
-            transcendentals=heads * length * length // 2,
-        ),
-        compiler_params=pltpu.CompilerParams(vmem_limit_bytes=32 << 20),
-    )(q, k, v)
-
-
-def turn_back(gradient, cos, sin):
+def turn_back(gradient, packed):
+    left = lax.broadcasted_iota(jnp.int32, packed.shape, 1) < HDIM // 2
+    turned = pltpu.roll(packed, HDIM // 2, 1)
+    cos = jnp.where(left, packed, turned)
+    sin = jnp.where(left, turned, -packed)
     return gradient * cos + pltpu.roll(gradient, HDIM // 2, 1) * sin
 
 
 def attend_back_kernel(
-    q_ref, k_ref, v_ref, go_ref, lse_ref, dots_ref, cos_ref, sin_ref, dq_ref, dk_ref, dv_ref, acc_ref
+    q_ref, k_ref, v_ref, go_ref, lse_ref, dots_ref, table_ref, dq_ref, dk_ref, dv_ref, acc_ref
 ):
     j = pl.program_id(1)
     tile = k_ref.shape[0]
@@ -542,23 +487,23 @@
     carry = fold(j, (zero, zero), True)
     dk, dv = lax.fori_loop(j + 1, length // tile, lambda i, c: fold(i, c, False), carry)
     at = pl.ds(pl.multiple_of(j * tile, tile), tile)
-    dk_ref[...] = turn_back(dk * scale, cos_ref[at, :], sin_ref[at, :]).astype(dk_ref.dtype)
+    dk_ref[...] = turn_back(dk * scale, table_ref[at, :]).astype(dk_ref.dtype)
     dv_ref[...] = dv.astype(dv_ref.dtype)
-    dq_ref[...] = turn_back(acc_ref[at, :] * scale, cos_ref[at, :], sin_ref[at, :]).astype(dq_ref.dtype)
-
-
-def attend_back(q, k, v, go, lse, dots, cos, sin):
+    dq_ref[...] = turn_back(acc_ref[at, :] * scale, table_ref[at, :]).astype(dq_ref.dtype)
+
+
+def attend_back(q, k, v, go, lse, dots, table):
     length = q.shape[0]
     heads = q.shape[1] // HDIM
     tile = attn_tile
     whole = pl.BlockSpec((length, HDIM), lambda h, j: (0, h))
     part = pl.BlockSpec((tile, HDIM), lambda h, j: (j, h))
     row = pl.BlockSpec((1, 1, length), lambda h, j: (h, 0, 0))
-    table = pl.BlockSpec((length, HDIM), lambda h, j: (0, 0))
+    rope = pl.BlockSpec((length, HDIM), lambda h, j: (0, 0))
     return pl.pallas_call(
         attend_back_kernel,
         grid=(heads, length // tile),
-        in_specs=[whole, part, part, whole, row, row, table, table],
+        in_specs=[whole, part, part, whole, row, row, rope],
         out_specs=[part, part, part],
         out_shape=[jax.ShapeDtypeStruct(q.shape, jnp.bfloat16)] * 3,
         scratch_shapes=[pltpu.VMEM((length, HDIM), jnp.float32)],
@@ -568,7 +513,7 @@
             transcendentals=heads * length * length // 2,
         ),
         compiler_params=pltpu.CompilerParams(vmem_limit_bytes=32 << 20),
-    )(q, k, v, go, lse, dots, cos, sin)
+    )(q, k, v, go, lse, dots, table)
 
 
 mesh_ids = pl.DeviceIdType.MESH
@@ -693,7 +638,7 @@
         self.recv = recv
 
     def ref(self, j):
-        return self.at.at[j, self.core]
+        return self.at.at[j] if self.core is None else self.at.at[j, self.core]
 
     def up(self, hop, j):
         ref = self.ref(j)
@@ -718,7 +663,8 @@
         def _():
             self.down(0, z).start()
 
-        self.across(0, z).start()
+        if self.core is not None:
+            self.across(0, z).start()
 
     def hop(self, t):
         z = self.z
@@ -726,7 +672,8 @@
         @pl.when(z >= t)
         def _():
             self.up(t - 1, z - t).wait_recv()
-            self.across(t, z - t).start()
+            if self.core is not None:
+                self.across(t, z - t).start()
             if t < 3:
 
                 @pl.when(z < 3)
@@ -736,7 +683,8 @@
         @pl.when(z + t <= 3)
         def _():
             self.down(t - 1, z + t).wait_recv()
-            self.across(3 + t, z + t).start()
+            if self.core is not None:
+                self.across(3 + t, z + t).start()
             if t < 3:
 
                 @pl.when(z > 0)
@@ -773,12 +721,14 @@
         def _():
             self.down(0, z).wait_send()
 
-        self.across(0, z).wait_send()
+        if self.core is not None:
+            self.across(0, z).wait_send()
         for t in (1, 2, 3):
 
             @pl.when(z >= t)
             def _():
-                self.across(t, z - t).wait_send()
+                if self.core is not None:
+                    self.across(t, z - t).wait_send()
                 if t < 3:
 
                     @pl.when(z < 3)
@@ -787,7 +737,8 @@
 
             @pl.when(z + t <= 3)
             def _():
-                self.across(3 + t, z + t).wait_send()
+                if self.core is not None:
+                    self.across(3 + t, z + t).wait_send()
                 if t < 3:
 
                     @pl.when(z > 0)
@@ -802,165 +753,6 @@
     centred = values - jnp.mean(values, axis=-1, keepdims=True)
     inverse = lax.rsqrt(jnp.mean(centred * centred, axis=-1, keepdims=True) + norm_eps)
     return (centred * inverse, inverse)
-
-
-def start_kernel(
-    x_ref, w_ref, o_ref, cos_ref, sin_ref, a_ref, set_ref,
-    x_own_ref, n_own_ref, u_out, w_all, o_all, q_ref, k_ref, v_ref, low_ref, b_sel_ref, a_sel_ref,
-    u_ref, w_buf, w_big, a2a_send, a2a_recv, ag_send, ag_recv, w_send, w_recv, o_send, o_recv, local_sem,
-):
-    s, z = places()
-    core = s % 2
-    other = flip(s, 1)
-    zs = [flip(z, 1), flip(z, 2), 3 - z]
-    meet([(None, (other, z)), (None, (flip(s, 2), z)), (None, (flip(s, 4), z))] + [(None, (s, j)) for j in zs])
-
-    swaps = [
-        remote(x_ref.at[j], x_own_ref.at[z], a2a_send.at[d], a2a_recv.at[d], (s, j)) for d, j in enumerate(zs)
-    ]
-    for one in swaps:
-        one.start()
-    x_own_ref[z] = x_ref[z]
-    w_buf[z, core] = w_ref[...]
-    own_o = pltpu.make_async_copy(o_ref, o_all.at[z, core], local_sem.at[8])
-    own_o.start()
-    for d, j in enumerate(zs):
-        remote(x_ref.at[j], x_own_ref.at[j], a2a_send.at[d], a2a_recv.at[d], (s, j)).wait_recv()
-    line = Line(w_buf, core, s, z, w_send, w_recv)
-    line.begin()
-    for part in range(4):
-        normed, _ = norm_rows(x_own_ref[part].astype(jnp.float32))
-        normed = normed.astype(jnp.bfloat16)
-        n_own_ref[pl.ds(part * 64, 64), :] = normed
-        u_ref[s, pl.ds(part * 64, 64), :] = normed
-    gather = Gather(u_ref, s, z, ag_send, ag_recv, 128)
-    gather.begin()
-    gather.arrive_first()
-    line.hop(1)
-    gather.arrive_neighbours()
-    line.hop(2)
-    gather.arrive_diagonal()
-    for index in range(4):
-        gather.arrive_core(index)
-    stores = [pltpu.make_async_copy(u_ref.at[t], u_out.at[t], local_sem.at[t]) for t in range(8)]
-    for one in stores:
-        one.start()
-    a48 = a_ref[...]
-
-    def lows(t, _):
-        low_ref[t] = (adapt_scale * dot_nt(u_ref[t], a48)).astype(jnp.bfloat16)
-        return 0
-
-    lax.fori_loop(0, 8, lows, 0)
-    line.hop(3)
-    own_o.wait()
-    o_line = Line(o_all, core, s, z, o_send, o_recv)
-    o_line.begin()
-    line.arrive_core()
-    keep = pltpu.make_async_copy(w_buf, w_all, local_sem.at[9])
-    keep.start()
-    mine = set_ref[0]
-    for j in range(4):
-        table = w_buf[j, 0, 3072:, :]
-        picked = jnp.zeros((48, HDIM), jnp.bfloat16)
-        picked_a = jnp.zeros((16, HDIM), jnp.bfloat16)
-        for member in range(4):
-            picked = jnp.where(mine == member, table[48 * member : 48 * member + 48], picked)
-            picked_a = jnp.where(mine == member, table[192 + 16 * member : 208 + 16 * member], picked_a)
-        b_sel_ref[j] = picked
-        a_sel_ref[j] = picked_a
-    for part in range(3):
-        for head in range(2):
-            columns = pl.ds((2 * part + head) * HDIM, HDIM)
-            for side in range(2):
-                w_big[pl.ds(side * 1024, 1024), columns] = w_buf[
-                    2 * core + head, side, pl.ds(part * 1024, 1024), :
-                ]
-    b_two = [
-        jnp.concatenate(
-            [b_sel_ref[2 * core, 16 * part : 16 * part + 16], b_sel_ref[2 * core + 1, 16 * part : 16 * part + 16]],
-            axis=1,
-        )
-        for part in range(3)
-    ]
-
-    def project(t, _):
-        u = u_ref[t]
-        low = low_ref[t]
-        cos = cos_ref[pl.ds(pl.multiple_of(t * 256, 256), 256), :]
-        sin = sin_ref[pl.ds(pl.multiple_of(t * 256, 256), 256), :]
-        for part, out in enumerate((q_ref, k_ref, v_ref)):
-            raw = dot_nn(u, w_big[:, 256 * part : 256 * part + 256]) + dot_nn(
-                low[:, 16 * part : 16 * part + 16], b_two[part]
-            )
-            for head in range(2):
-                piece = raw[:, HDIM * head : HDIM * head + HDIM]
-                if part < 2:
-                    piece = piece * cos - pltpu.roll(piece, HDIM // 2, 1) * sin
-                out[t, :, pl.ds(HDIM * head, HDIM)] = piece.astype(jnp.bfloat16)
-        return 0
-
-    lax.fori_loop(0, 3, project, 0)
-    o_line.hop(1)
-    lax.fori_loop(3, 6, project, 0)
-    o_line.hop(2)
-    lax.fori_loop(6, 8, project, 0)
-    o_line.hop(3)
-    o_line.arrive_core()
-    for one in stores:
-        one.wait()
-    keep.wait()
-    for one in swaps:
-        one.wait_send()
-    line.end()
-    o_line.end()
-    gather.end()
-
-
-def start_layer(x, w_pack, o_pack, cos, sin, a48, my_set):
-    bf16 = jnp.bfloat16
-    vmem = pl.BlockSpec(memory_space=pltpu.VMEM)
-    anywhere = pl.BlockSpec(memory_space=pl.ANY)
-    width = x.shape[2]
-    rows = w_pack.shape[0]
-    shape = jax.ShapeDtypeStruct
-    dma = pltpu.SemaphoreType.DMA
-    return pl.pallas_call(
-        start_kernel,
-        in_specs=[vmem, vmem, anywhere, vmem, vmem, vmem, pl.BlockSpec(memory_space=pltpu.SMEM)],
-        out_specs=[vmem, vmem, anywhere, anywhere, anywhere, vmem, vmem, vmem, vmem, vmem, vmem],
-        out_shape=[
-            shape((4, 64, width), bf16),
-            shape((256, width), bf16),
-            shape((8, 256, width), bf16),
-            shape((4, 2, rows, HDIM), bf16),
-            shape((4, 2, HDIM, width // 2), bf16),
-            shape((8, 256, 256), bf16),
-            shape((8, 256, 256), bf16),
-            shape((8, 256, 256), bf16),
-            shape((8, 256, 48), bf16),
-            shape((4, 48, HDIM), bf16),
-            shape((4, 16, HDIM), bf16),
-        ],
-        scratch_shapes=[
-            pltpu.VMEM((8, 256, width), bf16),
-            pltpu.VMEM((4, 2, rows, HDIM), bf16),
-            pltpu.VMEM((width, 768), bf16),
-            dma((3,)),
-            dma((3,)),
-            dma((gather_sems,)),
-            dma((gather_sems,)),
-            dma((line_sems,)),
-            dma((line_sems,)),
-            dma((line_sems,)),
-            dma((line_sems,)),
-            dma((10,)),
-        ],
-        cost_estimate=spend(80),
-        compiler_params=pltpu.CompilerParams(
-            collective_id=1, has_side_effects=True, vmem_limit_bytes=56 << 20
-        ),
-    )(x, w_pack, o_pack, cos, sin, a48, my_set)
 
 
 class Reduce:
@@ -1015,112 +807,301 @@
             self.copy(index).wait_send()
 
 
-def out_kernel(
-    mixed_ref, o_all, a_sel_ref, b_ref, w_all, a48_ref, b_sel_ref, x_own_ref,
-    residual_ref, m_own_ref, o_eff_ref, w_cat_ref,
-    sib_ref, out_buf, in_buf, o_big, w_buf, sib_send, sib_recv, send, recv, local_sem,
+def front_kernel(
+    x_ref, w_qkv_ref, w_out_ref, b_qkv_ref, a_out_ref, a_in_ref, b_od_ref, table_ref, cot_ref, set_ref,
+    x_own_ref, m_own_ref, residual_ref, o_eff_ref, b_sel_ref, a_sel_ref, lse_ref,
+    u_out, q_out, k_out, v_out, low_out, table_out, mixed_out, w_cat_out, cots_ref,
+    u_ref, w_buf, w_cat, q_buf, k_buf, v_buf, low_buf, tables, mixed, o_all, o_big, sib, out_buf, in_buf,
+    b_small, a_small,
+    a2a_send, a2a_recv, tab_send, tab_recv, ag_send, ag_recv, w_send, w_recv, o_send, o_recv, cot_send, cot_recv,
+    small_send, small_recv, sib_send, sib_recv, red_send, red_recv, local_sem, store_sem,
 ):
+    f32 = jnp.float32
+    bf16 = jnp.bfloat16
     s, z = places()
     core = s % 2
+    chip = s // 2
     other = flip(s, 1)
-    meet([(None, (other, z)), (None, (flip(s, 2), z)), (None, (flip(s, 4), z))])
+    zs = [flip(z, 1), flip(z, 2), 3 - z]
+    columns = pl.ds(pl.multiple_of(chip * HDIM, HDIM), HDIM)
+    half_rows = pl.ds(pl.multiple_of(core * 1024, 1024), 1024)
+    owns = [
+        pltpu.make_async_copy(w_qkv_ref.at[:, half_rows, columns], w_buf.at[z, core], local_sem.at[0]),
+        pltpu.make_async_copy(w_out_ref.at[columns, half_rows], o_all.at[z, core], local_sem.at[1]),
+        pltpu.make_async_copy(b_qkv_ref.at[:, :, :, columns], b_small.at[z], local_sem.at[2]),
+        pltpu.make_async_copy(a_out_ref.at[:, :, columns], a_small.at[z], local_sem.at[3]),
+        pltpu.make_async_copy(cot_ref, cots_ref.at[z], local_sem.at[4]),
+    ]
+    for one in owns:
+        one.start()
+    tables[s] = table_ref[...]
+    meet([(None, (other, z)), (None, (flip(s, 2), z)), (None, (flip(s, 4), z))] + [(None, (s, j)) for j in zs])
+
     swaps = [
-        remote(
-            mixed_ref.at[2 * c + 1 - core], sib_ref.at[c], sib_send.at[c], sib_recv.at[c], (other, z)
-        )
-        for c in range(4)
+        remote(x_ref.at[j], x_own_ref.at[z], a2a_send.at[d], a2a_recv.at[d], (s, j)) for d, j in enumerate(zs)
     ]
     for one in swaps:
         one.start()
-    load_w = pltpu.make_async_copy(w_all, w_buf, local_sem.at[0])
-    load_w.start()
+    table_gather = Gather(tables, s, z, tab_send, tab_recv, 128)
+    table_gather.begin()
+    x_own_ref[z] = x_ref[z]
+    table_gather.arrive_first()
+    table_gather.arrive_neighbours()
+    table_gather.arrive_diagonal()
+    for one in owns:
+        one.wait()
+    for d, j in enumerate(zs):
+        remote(x_ref.at[j], x_own_ref.at[j], a2a_send.at[d], a2a_recv.at[d], (s, j)).wait_recv()
+    line = Line(w_buf, core, s, z, w_send, w_recv)
+    line.begin()
+    smalls = []
+    for d, j in enumerate(zs):
+        smalls.append(remote(b_small.at[z], b_small.at[z], small_send.at[d], small_recv.at[d], (s, j)))
+        smalls.append(remote(a_small.at[z], a_small.at[z], small_send.at[3 + d], small_recv.at[3 + d], (s, j)))
+    for one in smalls:
+        one.start()
+    for part in range(4):
+        normed, _ = norm_rows(x_own_ref[part].astype(f32))
+        u_ref[s, pl.ds(part * 64, 64), :] = normed.astype(bf16)
+    gather = Gather(u_ref, s, z, ag_send, ag_recv, 128)
+    gather.begin()
+    gather.arrive_first()
+    line.hop(1)
+    gather.arrive_neighbours()
+    line.hop(2)
+    gather.arrive_diagonal()
+    for index in range(4):
+        gather.arrive_core(index)
+        table_gather.arrive_core(index)
+    stores = [pltpu.make_async_copy(u_ref, u_out, store_sem.at[0])]
+    stores[0].start()
+    mine = set_ref[z]
+    a48 = a_in_ref[mine, 0:3].reshape(48, -1)
+
+    def lows(t, _):
+        low_buf[t] = (adapt_scale * dot_nt(u_ref[t], a48)).astype(bf16)
+        return 0
+
+    lax.fori_loop(0, 8, lows, 0)
+    for d, j in enumerate(zs):
+        remote(b_small.at[j], b_small.at[j], small_send.at[d], small_recv.at[d], (s, j)).wait_recv()
+        remote(a_small.at[j], a_small.at[j], small_send.at[3 + d], small_recv.at[3 + d], (s, j)).wait_recv()
     for j in range(4):
-        head = (2 * core + j) % 4
-        merged = adapt_scale * dot_tn(a_sel_ref[head], b_ref[...])
-        for side in range(2):
-            o_big[pl.ds(j * HDIM, HDIM), pl.ds(side * 1024, 1024)] = (
-                o_all[head, side].astype(jnp.float32) + merged[:, side * 1024 : side * 1024 + 1024]
-            ).astype(jnp.bfloat16)
-    o_eff_ref[...] = o_big[0 : 2 * HDIM, :]
-    for one in swaps:
-        one.wait_recv()
-
-    def product(chip, half):
-        rows = pl.ds(half * 128, 128)
-        both = jnp.concatenate([mixed_ref[2 * chip + core, rows, :], sib_ref[chip, rows, :]], axis=1)
-        return dot_nn(both, o_big[...])
-
-    reduce = Reduce(product, s, z, out_buf, in_buf, send, recv)
-    reduce.begin()
-    load_w.wait()
+        b_sel_ref[j] = b_small[j, mine].reshape(48, HDIM)
+        a_sel_ref[j] = a_small[j, mine]
 
     def merge(index, _):
         j = index // 3
         part = index % 3
         head = (2 * core + j) % 4
         b_part = b_sel_ref[head, pl.ds(pl.multiple_of(part * 16, 16), 16), :]
-        a_part = a48_ref[pl.ds(pl.multiple_of(part * 16, 16), 16), :]
         column = pl.multiple_of(((j // 2) * 6 + part * 2 + j % 2) * HDIM, HDIM)
         for side in range(2):
-            merged = adapt_scale * dot_tn(a_part[:, side * 1024 : side * 1024 + 1024], b_part)
-            w_cat_ref[pl.ds(side * 1024, 1024), pl.ds(column, HDIM)] = (
-                w_buf[head, side, pl.ds(pl.multiple_of(part * 1024, 1024), 1024), :].astype(jnp.float32)
-                + merged
-            ).astype(jnp.bfloat16)
+            a_part = a_in_ref[mine, part, :, pl.ds(side * 1024, 1024)]
+            merged = adapt_scale * dot_tn(a_part, b_part)
+            w_cat[pl.ds(side * 1024, 1024), pl.ds(column, HDIM)] = (
+                w_buf[head, side, part].astype(f32) + merged
+            ).astype(bf16)
         return 0
 
-    lax.fori_loop(0, 4, merge, 0)
+    line.hop(3)
+    o_line = Line(o_all, core, s, z, o_send, o_recv)
+    o_line.begin()
+    cot_line = Line(cots_ref, None, s, z, cot_send, cot_recv)
+    cot_line.begin()
+    line.arrive_core()
+    lax.fori_loop(0, 6, merge, 0)
+    left = lax.broadcasted_iota(jnp.int32, (256, HDIM), 1) < HDIM // 2
+
+    def project(t, _):
+        u = u_ref[t]
+        packed = tables[t]
+        turned = pltpu.roll(packed, HDIM // 2, 1)
+        cos = jnp.where(left, packed, turned)
+        sin = jnp.where(left, turned, -packed)
+        rows = pl.ds(pl.multiple_of(t * 256, 256), 256)
+        for part, out in enumerate((q_buf, k_buf, v_buf)):
+            raw = dot_nn(u, w_cat[:, 256 * part : 256 * part + 256])
+            for head in range(2):
+                piece = raw[:, HDIM * head : HDIM * head + HDIM]
+                if part < 2:
+                    piece = piece * cos - pltpu.roll(piece, HDIM // 2, 1) * sin
+                out[rows, HDIM * head : HDIM * head + HDIM] = piece.astype(bf16)
+        return 0
+
+    lax.fori_loop(0, 3, project, 0)
+    o_line.hop(1)
+    lax.fori_loop(3, 6, project, 0)
+    o_line.hop(2)
+    lax.fori_loop(6, 8, project, 0)
+    stores += [
+        pltpu.make_async_copy(source, target, store_sem.at[1 + i])
+        for i, (source, target) in enumerate(
+            ((q_buf, q_out), (k_buf, k_out), (v_buf, v_out), (low_buf, low_out), (tables, table_out))
+        )
+    ]
+    for one in stores[1:]:
+        one.start()
+
+    tile = attn_tile
+    factor = log2e / math.sqrt(HDIM)
+
+    def attend(index, _):
+        head = index // 4
+        i = index % 4
+        lanes = pl.ds(pl.multiple_of(head * HDIM, HDIM), HDIM)
+        here = pl.ds(pl.multiple_of(i * tile, tile), tile)
+        q = q_buf[here, lanes]
+
+        def fold(j, carry, diagonal):
+            top, total, acc = carry
+            at = pl.ds(pl.multiple_of(j * tile, tile), tile)
+            scores = dot_nt(k_buf[at, lanes], q)
+            if diagonal:
+                scores = jnp.where(causal(scores, 0, 0), scores, far_below)
+            new_top = jnp.maximum(top, jnp.max(scores, axis=0, keepdims=True))
+            weight = jnp.exp2(scores * factor - new_top * factor)
+            keep = jnp.exp2((top - new_top) * factor)
+            total = total * keep + jnp.sum(weight, axis=0, keepdims=True)
+            acc = acc * keep + dot_tn(v_buf[at, lanes], weight.astype(bf16))
+            return (new_top, total, acc)
+
+        carry = (
+            jnp.full((1, tile), far_below, f32),
+            jnp.zeros((1, tile), f32),
+            jnp.zeros((HDIM, tile), f32),
+        )
+        carry = lax.fori_loop(0, i, lambda j, c: fold(j, c, False), carry)
+        top, total, acc = fold(i, carry, True)
+        mixed[here, lanes] = jnp.transpose(acc / total).astype(bf16)
+        lse_ref[head, i] = top * factor + jnp.log2(total)
+        return 0
+
+    lax.fori_loop(0, 3, attend, 0)
+    o_line.hop(3)
+    lax.fori_loop(3, 8, attend, 0)
+
+    def span_rows(span, first, count):
+        return pl.ds(pl.multiple_of(span * 256 + first, 128), count)
+
+    crosses = [
+        remote(mixed.at[span_rows(2 * c + 1 - core, 0, 256)], sib.at[c], sib_send.at[c], sib_recv.at[c], (other, z))
+        for c in range(4)
+    ]
+    for one in crosses:
+        one.start()
+    stores.append(pltpu.make_async_copy(mixed, mixed_out, store_sem.at[6]))
+    stores[-1].start()
+    o_line.arrive_core()
+    b_row = b_od_ref[mine, 0]
+    for j in range(4):
+        head = (2 * core + j) % 4
+        merged = adapt_scale * dot_tn(a_sel_ref[head], b_row)
+        for side in range(2):
+            o_big[pl.ds(j * HDIM, HDIM), pl.ds(side * 1024, 1024)] = (
+                o_all[head, side].astype(f32) + merged[:, side * 1024 : side * 1024 + 1024]
+            ).astype(bf16)
+    o_eff_ref[...] = o_big[0 : 2 * HDIM, :]
+    for one in crosses:
+        one.wait_recv()
+
+    def product(c, half):
+        both = jnp.concatenate(
+            [mixed[span_rows(2 * c + core, half * 128, 128), :], sib[c, pl.ds(half * 128, 128), :]], axis=1
+        )
+        return dot_nn(both, o_big[...])
+
+    reduce = Reduce(product, s, z, out_buf, in_buf, red_send, red_recv)
+    reduce.begin()
+    cot_line.hop(1)
+    lax.fori_loop(6, 8, merge, 0)
     reduce.middle()
-    lax.fori_loop(4, 12, merge, 0)
+    lax.fori_loop(8, 12, merge, 0)
+    stores.append(pltpu.make_async_copy(w_cat, w_cat_out, store_sem.at[7]))
+    stores[-1].start()
+    cot_line.hop(2)
     for half in range(2):
         total = reduce.finish(half)
-        x = x_own_ref[2 * half : 2 * half + 2].reshape(128, -1).astype(jnp.float32)
+        x = x_own_ref[2 * half : 2 * half + 2].reshape(128, -1).astype(f32)
         residual = x + total
         residual_ref[pl.ds(half * 128, 128), :] = residual
         normed, _ = norm_rows(residual)
-        m_own_ref[pl.ds(half * 128, 128), :] = normed.astype(jnp.bfloat16)
-    for one in swaps:
+        m_own_ref[pl.ds(half * 128, 128), :] = normed.astype(bf16)
+    cot_line.hop(3)
+    for one in stores:
+        one.wait()
+    for one in swaps + smalls + crosses:
         one.wait_send()
+    line.end()
+    o_line.end()
+    cot_line.end()
+    gather.end()
+    table_gather.end()
     reduce.end()
 
 
-def out_layer(mixed, o_all, a_sel, b_row, w_all, a48, b_sel, x_own):
+def front_layer(x, w_qkv, w_out, b_qkv, a_out, a_in, b_out_down, table, cotangent, set_index):
     bf16 = jnp.bfloat16
+    f32 = jnp.float32
     vmem = pl.BlockSpec(memory_space=pltpu.VMEM)
-    width = x_own.shape[2]
+    anywhere = pl.BlockSpec(memory_space=pl.ANY)
+    width = x.shape[2]
     shape = jax.ShapeDtypeStruct
     dma = pltpu.SemaphoreType.DMA
+    vm = pltpu.VMEM
     return pl.pallas_call(
-        out_kernel,
-        in_specs=[vmem, vmem, vmem, vmem, pl.BlockSpec(memory_space=pl.ANY), vmem, vmem, vmem],
-        out_specs=[vmem, vmem, vmem, vmem],
+        front_kernel,
+        in_specs=[vmem] + [anywhere] * 4 + [vmem] * 3 + [anywhere, pl.BlockSpec(memory_space=pltpu.SMEM)],
+        out_specs=[vmem] * 7 + [anywhere] * 9,
         out_shape=[
-            shape((256, width), jnp.float32),
+            shape((4, 64, width), bf16),
             shape((256, width), bf16),
+            shape((256, width), f32),
             shape((256, width), bf16),
+            shape((4, 48, HDIM), bf16),
+            shape((4, 16, HDIM), bf16),
+            shape((2, 4, 1, attn_tile), f32),
+            shape((8, 256, width), bf16),
+            shape((2048, 256), bf16),
+            shape((2048, 256), bf16),
+            shape((2048, 256), bf16),
+            shape((8, 256, 48), bf16),
+            shape((8, 256, HDIM), f32),
+            shape((2048, 256), bf16),
             shape((width, 1536), bf16),
+            shape((4, 4, 64, width), bf16),
         ],
         scratch_shapes=[
-            pltpu.VMEM((4, 256, 256), bf16),
-            pltpu.VMEM((6, 128, width), bf16),
-            pltpu.VMEM((6, 128, width), bf16),
-            pltpu.VMEM((512, width), bf16),
-            pltpu.VMEM(w_all.shape, bf16),
-            dma((4,)),
-            dma((4,)),
-            dma((6,)),
-            dma((6,)),
-            dma((1,)),
+            vm((8, 256, width), bf16),
+            vm((4, 2, 3, 1024, HDIM), bf16),
+            vm((width, 1536), bf16),
+            vm((2048, 256), bf16),
+            vm((2048, 256), bf16),
+            vm((2048, 256), bf16),
+            vm((8, 256, 48), bf16),
+            vm((8, 256, HDIM), f32),
+            vm((2048, 256), bf16),
+            vm((4, 2, HDIM, 1024), bf16),
+            vm((4 * HDIM, width), bf16),
+            vm((4, 256, 256), bf16),
+            vm((6, 128, width), bf16),
+            vm((6, 128, width), bf16),
+            vm((4, 4, 3, 16, HDIM), bf16),
+            vm((4, 4, 16, HDIM), bf16),
+        ]
+        + [
+            dma((count,))
+            for count in (3, 3, 10, 10, 10, 10, 13, 13, 13, 13, 13, 13, 6, 6, 4, 4, 6, 6, 5, 8)
         ],
-        cost_estimate=spend(45),
+        cost_estimate=spend(150),
         compiler_params=pltpu.CompilerParams(
-            collective_id=2, has_side_effects=True, vmem_limit_bytes=56 << 20
+            collective_id=1, has_side_effects=True, vmem_limit_bytes=58 << 20
         ),
-    )(mixed, o_all, a_sel, b_row, w_all, a48, b_sel, x_own)
+    )(x, w_qkv, w_out, b_qkv, a_out, a_in, b_out_down, table, cotangent, set_index)
 
 
 def spread_kernel(
-    g_ref, o_eff_ref, mixed_ref, b_ref, down1_ref, down2_ref,
+    g_ref, o_eff_ref, mixed_ref, b_od_ref, down1_ref, down2_ref, set_ref,
     g_out, gm_ref, dots_ref, rank_ref, got1_ref, got2_ref, g_buf, send, recv, local_sem, down_send, down_recv,
 ):
     s, z = places()
@@ -1150,7 +1131,7 @@
         for head in range(2):
             turned = jnp.transpose(product[:, HDIM * head : HDIM * head + HDIM])
             dots_ref[head, t] = jnp.sum(turned, axis=0, keepdims=True)
-        rank_ref[t] = (adapt_scale * dot_nt(g, b_ref[...])).astype(jnp.bfloat16)
+        rank_ref[t] = (adapt_scale * dot_nt(g, b_od_ref[set_ref[z], 0])).astype(jnp.bfloat16)
         store(t).wait()
 
     work(s)
@@ -1169,7 +1150,7 @@
         one.wait()
 
 
-def spread_layer(g_own, o_eff, mixed, b_row, down1, down2):
+def spread_layer(g_own, o_eff, mixed, b_out_down, down1, down2, set_index):
     bf16 = jnp.bfloat16
     vmem = pl.BlockSpec(memory_space=pltpu.VMEM)
     anywhere = pl.BlockSpec(memory_space=pl.ANY)
@@ -1178,7 +1159,7 @@
     dma = pltpu.SemaphoreType.DMA
     return pl.pallas_call(
         spread_kernel,
-        in_specs=[vmem] * 4 + [anywhere] * 2,
+        in_specs=[vmem] * 4 + [anywhere] * 2 + [pl.BlockSpec(memory_space=pltpu.SMEM)],
         out_specs=[anywhere, vmem, vmem, vmem, anywhere, anywhere],
         out_shape=[
             shape((8, 256, width), bf16),
@@ -1200,11 +1181,11 @@
         compiler_params=pltpu.CompilerParams(
             collective_id=3, has_side_effects=True, vmem_limit_bytes=48 << 20
         ),
-    )(g_own, o_eff, mixed, b_row, down1, down2)
+    )(g_own, o_eff, mixed, b_out_down, down1, down2, set_index)
 
 
 def mlp_line_kernel(
-    m_ref, residual_ref, cot0_ref, cot1_ref, cot2_ref, cot3_ref, w_gu_ref, w_d_ref, a_ref, b_ref, ad_ref, bd_ref,
+    m_ref, residual_ref, cots_ref, w_gu_ref, w_d_ref, a_ref, b_ref, ad_ref, bd_ref, set_ref,
     g_ref, grad_res_ref, down0_ref, down1_ref, down2_ref, down3_ref, grad_b_ref, grad_ad_ref, grad_a_ref, grad_bd_ref,
     m_buf, wg, wu, wd, cot_buf, back_acc, down_acc, ranks, slots, r1, r2, r3, r4, r5, stage,
     up_send, up_recv, dn_send, dn_recv, send1, recv1, send4, recv4, send5, recv5, send23, recv23,
@@ -1238,13 +1219,10 @@
             one.start()
 
     others = [z, pair, flip(z, 2), opposite]
-    cot_refs = (cot0_ref, cot1_ref, cot2_ref, cot3_ref)
     down_refs = (down0_ref, down1_ref, down2_ref, down3_ref)
 
     def load_cot(seq):
-        return [
-            pltpu.make_async_copy(cot_refs[d].at[seq], cot_buf.at[others[d]], cot_sem.at[d]) for d in range(4)
-        ]
+        return [pltpu.make_async_copy(cots_ref.at[j, seq], cot_buf.at[j], cot_sem.at[j]) for j in range(4)]
 
     for one in load_cot(z):
         one.start()
@@ -1328,14 +1306,18 @@
             pltpu.make_async_copy(stage.at[others[d]], down_refs[d].at[seq], stage_sem.at[d]) for d in range(4)
         ]
 
+    def in_maps(seq):
+        return a_ref[set_ref[seq], 3:5].reshape(32, -1)
+
     def compute(slot):
         seq = ids[slot]
+        member = set_ref[seq]
         rows = m_buf[seq]
         for one in load_cot(seq):
             one.wait()
-        ranks[:, 0:32] = adapt_scale * dot_nt(rows, a_ref[seq])
+        ranks[:, 0:32] = adapt_scale * dot_nt(rows, in_maps(seq))
         cot = cot_buf[...].reshape(256, -1)
-        ranks[:, 32:48] = adapt_scale * dot_nt(cot, bd_ref[seq])
+        ranks[:, 32:48] = adapt_scale * dot_nt(cot, bd_ref[member, 1])
         ranks[:, 48:96] = jnp.zeros((256, 48), f32)
         back_acc[...] = jnp.zeros_like(back_acc)
         down_acc[...] = jnp.zeros_like(down_acc)
@@ -1346,9 +1328,9 @@
             low_gate = low[:, 0:16]
             low_up = low[:, 16:32]
             low_cot = low[:, 32:48]
-            bg = b_ref[seq, 0, :, columns]
-            bu = b_ref[seq, 1, :, columns]
-            ad = ad_ref[seq, :, columns]
+            bg = b_ref[member, 0, :, columns]
+            bu = b_ref[member, 1, :, columns]
+            ad = ad_ref[member, :, columns]
             rows = m_buf[seq]
             cot = cot_buf[...].reshape(256, -1)
             gate = dot_nn(rows, wg[h]) + dot_nn(low_gate, bg)
@@ -1376,7 +1358,7 @@
                     one.wait()
         lax.fori_loop(0, tiles, step, 0)
         back_rank = (adapt_scale * ranks[:, 64:96]).astype(bf16)
-        slots[slot] = (back_acc[...] + dot_nn(back_rank, a_ref[seq])).astype(bf16)
+        slots[slot] = (back_acc[...] + dot_nn(back_rank, in_maps(seq))).astype(bf16)
 
     def rest(slot):
         seq = ids[slot]
@@ -1387,7 +1369,7 @@
         if slot > 0:
             for one in stage_copies(ids[slot - 1]):
                 one.wait()
-        value = down_acc[...] + dot_nn(low_down, bd_ref[seq])
+        value = down_acc[...] + dot_nn(low_down, bd_ref[set_ref[seq], 1])
         if slot == 0:
             value = value + residual_ref[...]
         stage[...] = value.astype(bf16).reshape(4, 64, -1)
@@ -1497,7 +1479,7 @@
             copy4(p).wait_send()
 
 
-def mlp_line(m_own, residual, cots, w_gate_up, w_down, a_sel, b_sel, ad_sel, bd_sel):
+def mlp_line(m_own, residual, cots, w_gate_up, w_down, a_in, b_gate_up, a_down, b_out_down, set_index):
     bf16 = jnp.bfloat16
     f32 = jnp.float32
     vmem = pl.BlockSpec(memory_space=pltpu.VMEM)
@@ -1511,7 +1493,10 @@
     vm = pltpu.VMEM
     return pl.pallas_call(
         mlp_line_kernel,
-        in_specs=[vmem, vmem] + [anywhere] * 6 + [vmem] * 4,
+        in_specs=[vmem, vmem]
+        + [anywhere] * 3
+        + [vmem] * 4
+        + [pl.BlockSpec(memory_space=pltpu.SMEM)],
         out_specs=[vmem, vmem] + [anywhere] * 4 + [vmem, vmem, vmem, vmem],
         out_shape=[
             shape((256, width), bf16),
@@ -1549,7 +1534,7 @@
         compiler_params=pltpu.CompilerParams(
             collective_id=5, has_side_effects=True, vmem_limit_bytes=60 << 20
         ),
-    )(m_own, residual, *cots, w_gate_up, w_down, a_sel, b_sel, ad_sel, bd_sel)
+    )(m_own, residual, cots, w_gate_up, w_down, a_in, b_gate_up, a_down, b_out_down, set_index)
 
 
 def finish_kernel(
@@ -1862,87 +1847,53 @@
     )(*operands)
 
 
-def swap_mp(values, d):
-    pairs = [(s * 4 + z, s * 4 + (z ^ d)) for s in range(lax.axis_size("seq")) for z in range(4)]
-    return lax.ppermute(values, ("seq", "mp"), pairs)
-
-
-def full_tables(positions):
+def span_table(positions):
     half_dim = HDIM // 2
     frequency = jnp.exp(
         jnp.arange(half_dim, dtype=jnp.float32) * (-2.0 * math.log(rope_base) / HDIM)
     )
     angles = positions.astype(jnp.float32)[:, None] * frequency
-    cos = jnp.cos(angles)
-    sin = jnp.sin(angles)
-    return (jnp.concatenate([cos, cos], axis=1), jnp.concatenate([sin, -sin], axis=1))
-
-
-def pick(values, index, axis=0):
-    return lax.dynamic_index_in_dim(values, index, axis, keepdims=False)
+    return jnp.concatenate([jnp.cos(angles), jnp.sin(angles)], axis=1)
 
 
 def per_device_layers(
     layer_in, w_qkv, w_out, w_gate_up, w_down, a_in, b_qkv, b_gate_up, a_out, a_down, b_out_down,
     set_index, positions, cotangent,
 ):
-    bf16 = jnp.bfloat16
     f32 = jnp.float32
-    s = lax.axis_index("seq")
     z = lax.axis_index("mp")
-    chip = s // 2
-    core = s % 2
     sets = a_in.shape[0]
     width = layer_in.shape[2]
     rank = a_in.shape[2]
     length = 8 * 256
 
-    my_set = pick(set_index, z)
-    a48 = pick(a_in, my_set)[:3].reshape(3 * rank, width)
-    bo_set = pick(b_out_down, my_set)
-    a_sel = jnp.stack([pick(a_in, set_index[q])[3:].reshape(2 * rank, width) for q in range(4)])
-    b_sel_mlp = jnp.stack([pick(b_gate_up, set_index[q]) for q in range(4)])
-    ad_sel = jnp.stack([pick(a_down, set_index[q]) for q in range(4)])
-    bd_sel = jnp.stack([pick(b_out_down, set_index[q])[1] for q in range(4)])
-    half = width // 2
-    w_half = lax.dynamic_slice(w_qkv, (0, core * half, chip * HDIM), (3, half, HDIM)).reshape(-1, HDIM)
-    b_own = lax.dynamic_slice_in_dim(b_qkv, chip * HDIM, HDIM, 3).reshape(-1, HDIM)
-    a_own = lax.dynamic_slice_in_dim(a_out, chip * HDIM, HDIM, 2).reshape(-1, HDIM)
-    w_pack = jnp.concatenate([w_half, b_own, a_own], axis=0)
-    o_pack = lax.dynamic_slice(w_out, (chip * HDIM, core * half), (HDIM, half))
-    positions_z = lax.all_gather(pick(positions, z), "seq", axis=0, tiled=True)
-    cos, sin = full_tables(positions_z)
-
-    (x_own, n_own, u, w_all, o_all, q, k, v, low, b_sel, a_out_sel) = start_layer(
-        layer_in, w_pack, o_pack, cos, sin, a48, my_set[None]
-    )
-    del n_own
-    cot_late, _ = lax.optimization_barrier((cotangent, x_own))
-    cots = [cot_late] + [swap_mp(cot_late, d) for d in (1, 2, 3)]
-
-    def flat(values):
-        return values.reshape(length, values.shape[-1])
-
-    mixed, lse = attend(flat(q), flat(k), flat(v))
-    residual, m_own, o_eff, w_cat = out_layer(
-        mixed.reshape(8, 256, 256), o_all, a_out_sel, bo_set[0], w_all, a48, b_sel, x_own
-    )
-    g_own, grad_residual, down0, down1, down2, down3, grad_b_mlp, grad_ad, grad_a_mlp, grad_bd = mlp_line(
-        m_own, residual, cots, w_gate_up, w_down, a_sel, b_sel_mlp, ad_sel, bd_sel
-    )
-    g, grad_mixed, dots, out_rank, got1, got2 = spread_layer(
-        g_own, o_eff, mixed.reshape(8, 256, 256), bo_set[0], down1, down2
-    )
-    dq, dk, dv = attend_back(
-        flat(q), flat(k), flat(v), flat(grad_mixed), lse, dots.reshape(2, 1, length), cos, sin
+    table = span_table(lax.dynamic_index_in_dim(positions, z, 0, keepdims=False))
+    (
+        x_own, m_own, residual, o_eff, b_sel, a_sel, lse,
+        u, q, k, v, low, tables, mixed, w_cat, cots,
+    ) = front_layer(
+        layer_in, w_qkv, w_out, b_qkv, a_out, a_in, b_out_down, table, cotangent, set_index
     )
 
     def spans(values):
         return values.reshape(8, 256, 256)
 
+    (
+        g_own, grad_residual, down0, down1, down2, down3,
+        grad_b_mlp, grad_ad, grad_a_mlp, grad_bd,
+    ) = mlp_line(
+        m_own, residual, cots, w_gate_up, w_down, a_in, b_gate_up, a_down, b_out_down, set_index
+    )
+    g, grad_mixed, dots, out_rank, got1, got2 = spread_layer(
+        g_own, o_eff, spans(mixed), b_out_down, down1, down2, set_index
+    )
+    dq, dk, dv = attend_back(
+        q, k, v, grad_mixed.reshape(length, -1), lse.reshape(2, 1, length), dots.reshape(2, 1, length),
+        tables.reshape(length, HDIM),
+    )
     result, grad_in, pool, heads, _ = finish_layer(
         spans(dq), spans(dk), spans(dv), w_cat, x_own, grad_residual, u, g, low, out_rank, spans(mixed),
-        b_sel, a_out_sel, grad_b_mlp, grad_ad, grad_a_mlp, grad_bd, down0, got1, got2, down3, set_index,
+        b_sel, a_sel, grad_b_mlp, grad_ad, grad_a_mlp, grad_bd, down0, got1, got2, down3, set_index,
     )
     pool = pool.astype(f32)
     whole = pool[:, 0:24].reshape(sets, 48, width)

time: 574 us -> 551 us (0.960)
  Pallas kernels: 498 us -> 520 us
  local copies, waits for them, and re-layouts: 26.1 us -> 13.5 us
  between operations: 11.1 us -> 1.35 us
  blocking collectives: 9.34 us -> 0 us
  starting transfers between devices: 8.92 us -> 0 us
  other arithmetic: 12.7 us -> 5.47 us
    pallas_call x5 -> x3, Pallas kernels: 361 us -> 383 us  [the longest x1 188 us: front_layer(): pl.pallas_call(front_kernel, in_specs=[vmem] + [anywhere] * 4 + [vmem] *...]
    all_gather x1 -> x0, blocking collectives: 9.34 us -> none  [per_device_layers(): positions_z = lax.all_gather(pick(positions, z), 'seq', axis=0, tiled=True)]
    ppermute x3 -> x0, starting transfers between devices: 8.92 us -> none  [swap_mp(): return lax.ppermute(values, ('seq', 'mp'), pairs)]
  transfers between devices with their start and end apart: 3 -> 0, of which waited for: 1 -> 0; matrix products, arithmetic and copies ran while one was open for 1% -> 0% of each run, Pallas kernels for 11% -> 0%
where the time goes in v3:
time: 551 us; the launch traced here: 541 us
  Pallas kernels  520 us (94%)
  local copies, waits for them, and re-layouts  13.5 us (2%)
    pallas_call x1, Pallas kernels, front_layer(): pl.pallas_call(front_kernel, in_specs=[vmem] + [anywhere] * 4 + [vmem] *...  188 us
    pallas_call x1, Pallas kernels, mlp_line(): pl.pallas_call(mlp_line_kernel, in_specs=[vmem, vmem] + [anywhere] * 3 +...  140 us
    pallas_call x1, Pallas kernels, finish_layer(): pl.pallas_call(finish_kernel, in_specs=[vmem] * 6 + [anywhere] * 2 + [vme...  114 us
    pallas_call x1, Pallas kernels, spread_layer(): pl.pallas_call(spread_kernel, in_specs=[vmem] * 4 + [anywhere] * 2 + [pl....  55.1 us
    pallas_call x1, Pallas kernels, attend_back(): pl.pallas_call(attend_back_kernel, grid=(heads, length // tile), in_specs...  23.1 us

profile of v3, /device:TPU:13, one launch (start us, length us, event | category | flops | bytes accessed | tf_op | source)
XLA Modules:
  0.0 540.7 jit_solution(5938467943543377964)
XLA Ops:
  0.6 0.7 dynamic-slice_convert_fusion
  1.3 0.5 multiply_cosine_fusion
  1.9 0.8 pad_maximum_fusion.2.table_ref
  2.6 188.5 %shard_map.197 = (bf16[4,64,2048]{2,1,0:T(8,128)(2,1)}, bf16[256,2048]{1,0:T(8,128)(2,1)}, f32[256,2048]{1,0:T(8,128)}, bf16[256,2048]{1,0:T(8,128)(2,1)}, bf16[...) custom-call(bf16[4,64,2048]{2,1,0:T(8,128)(2,1)} %x_ref.1, ...), custom_call_target="tpu_custom_call" | custom-call | flops 149999992832 | bytes 1000000 | tf_op jit(solution)/shard_map/pallas_call | solution.py:1052
  191.1 0.0 copy-start
  191.1 0.0 copy-start.1
  191.1 139.6 %shard_map.198 = (bf16[256,2048]{1,0:T(8,128)(2,1)}, f32[256,2048]{1,0:T(8,128)}, bf16[4,64,2048]{2,1,0:T(8,128)(2,1)}, bf16[4,64,2048]{2,1,0:T(8,128)(2,1)}, bf...) custom-call(bf16[256,2048]{1,0:T(8,128)(2,1)} %get-tuple-element.50., ...), custom_call_target="tpu_custom_call" | custom-call | flops 109999996928 | bytes 1000000 | tf_op jit(solution)/shard_map/pallas_call | solution.py:1494
  330.8 0.0 copy-done
  330.8 0.0 copy-done.1
  330.8 0.0 copy-start.12
  330.8 1.2 copy-done.12
  332.0 0.0 copy-start.9
  332.1 55.1 %shard_map.199 = (bf16[8,256,2048]{2,1,0:T(8,128)(2,1)}, bf16[8,256,256]{2,1,0:T(8,128)(2,1)S(1)}, f32[2,8,1,256]{3,2,1,0:T(1,128)S(1)}, bf16[8,256,16]{2,1,0:T(...) custom-call(bf16[256,2048]{1,0:T(8,128)(2,1)S(1)} %copy-done.12, ...), custom_call_target="tpu_custom_call" | custom-call | flops 40000000000 | bytes 1000000 | tf_op jit(solution)/shard_map/pallas_call | solution.py:1160
  387.2 0.0 copy-start.10
  387.2 0.0 copy-start.11
  387.2 0.0 copy-start.13
  387.2 0.0 copy-done.2
  387.2 0.0 copy-done.6
  387.2 0.0 copy-done.7
  387.3 0.0 copy-done.8
  387.3 0.0 copy-done.9
  387.3 23.1 %shard_map.200 = (bf16[2048,256]{1,0:T(8,128)(2,1)S(1)}, bf16[2048,256]{1,0:T(8,128)(2,1)S(1)}, bf16[2048,256]{1,0:T(8,128)(2,1)S(1)}) custom-call(bf16[2048,256]{1,0:T(8,128)(2,1)S(1)} %copy-done.7, bf16[2048,256]{1,0:T(8,128)(2,1)S(1)} %copy-done.8, bf16[2048,256]{1,0:T(8,128)(2,1)S(1)} %copy-done.9, bf16[2048,256]{1,0:T(8,128)(2,1)S(1)} %bitcast.35, ...), custom_call_target="tpu_custom_call" | custom-call | flops 5368709120 | bytes 7340032 | tf_op jit(solution)/shard_map/pallas_call | solution.py:503
  410.4 0.0 copy-done.10
  410.4 0.0 copy-done.11
  410.4 0.0 copy-done.13
  410.4 0.0 copy-start.3
  410.4 1.0 copy-done.3
  411.4 1.0 copy-done.4
  412.4 1.0 copy-done.5
  413.3 114.1 %shard_map.201 = (bf16[4,64,2048]{2,1,0:T(8,128)(2,1)}, bf16[4,64,2048]{2,1,0:T(8,128)(2,1)}, bf16[8,80,2048]{2,1,0:T(8,128)(2,1)}, bf16[4,256,128]{2,1,0:T(8,128)(2,1)}, bf16[4,64,2048]{2,1,0:T(8,128)(2,1)}) custom-call(bf16[8,256,256]{2,1,0:T(8,128)(2,1)} %bitcast.32, bf16[8,256,256]{2,1,0:T(8,128)(2,1)} %bitcast.33, bf16[8,256,256]{2,1,0:T(8,128)(2,1)} %bitcast.34, ...), custom_call_target="tpu_custom_call" | custom-call | flops 80000000000 | bytes 1000000 | tf_op jit(solution)/shard_map/pallas_call | solution.py:1808
  527.4 0.0 copy-start.14
  527.4 2.1 copy.28
  529.5 1.3 reshape.98
  530.8 0.7 slice_bitcast_fusion.3
  531.4 0.8 slice.48
  532.2 0.0 copy-done.14
  532.2 0.2 fusion
  532.5 0.8 slice.52
  533.3 1.0 slice.50
  534.3 0.1 slice.47
  534.4 0.7 convert_element_type.16
  535.1 0.2 copy_bitcast_fusion
  535.3 0.1 slice_bitcast_fusion.1
  535.4 0.1 slice.45
  535.6 1.7 pad_maximum_fusion
  537.3 1.1 pad_maximum_fusion.1
  538.3 1.0 copy.31
  539.3 1.0 copy.32
  (11 shorter events, 0.0 us)
Async XLA Ops:
  191.1 139.7 %copy-start = (bf16[4,2,16,2048]{3,2,1,0:T(8,128)(2,1)S(1)}, bf16[4,2,16,2048]{3,2,1,0:T(8,128)(2,1)}, u32[]{:S(2)}) copy-start(bf16[4,2,16,2048]{3,2,1,0:T(8,128)(2,1)} %b_od_ref.3) | copy-start | bytes 1572868
  191.1 139.7 %copy-start.1 = (s32[4]{0:T(128)S(1)}, s32[4]{0:T(128)}, u32[]{:S(2)}) copy-start(s32[4]{0:T(128)} %set_ref.7) | copy-start | bytes 52
  330.8 1.2 copy-start.12
  332.0 55.2 %copy-start.2 = (f32[8,256,128]{2,1,0:T(8,128)S(1)}, f32[8,256,128]{2,1,0:T(8,128)}, u32[]{:S(2)}) copy-start(f32[8,256,128]{2,1,0:T(8,128)} %get-tuple-element.61) | copy-start | bytes 3145732
  332.0 55.2 %copy-start.6 = (f32[2,4,1,512]{3,2,1,0:T(1,128)S(1)}, f32[2,4,1,512]{3,2,1,0:T(1,128)}, u32[]{:S(2)}) copy-start(f32[2,4,1,512]{3,2,1,0:T(1,128)} %get-tuple-element.59) | copy-start | bytes 49156
  332.0 55.2 %copy-start.7 = (bf16[2048,256]{1,0:T(8,128)(2,1)S(1)}, bf16[2048,256]{1,0:T(8,128)(2,1)}, u32[]{:S(2)}) copy-start(bf16[2048,256]{1,0:T(8,128)(2,1)} %get-tuple-element.47.q_ref) | copy-start | bytes 3145732
  332.0 55.2 %copy-start.8 = (bf16[2048,256]{1,0:T(8,128)(2,1)S(1)}, bf16[2048,256]{1,0:T(8,128)(2,1)}, u32[]{:S(2)}) copy-start(bf16[2048,256]{1,0:T(8,128)(2,1)} %get-tuple-element.48.k_ref) | copy-start | bytes 3145732
  332.0 55.2 %copy-start.9 = (bf16[2048,256]{1,0:T(8,128)(2,1)S(1)}, bf16[2048,256]{1,0:T(8,128)(2,1)}, u32[]{:S(2)}) copy-start(bf16[2048,256]{1,0:T(8,128)(2,1)} %get-tuple-element.49.v_ref) | copy-start | bytes 3145732
  387.2 23.2 %copy-start.10 = (bf16[4,64,2048]{2,1,0:T(8,128)(2,1)}, bf16[4,64,2048]{2,1,0:T(8,128)(2,1)S(1)}, u32[]{:S(2)}) copy-start(bf16[4,64,2048]{2,1,0:T(8,128)(2,1)S(1)} %get-tuple-element.79.got1_ref) | copy-start | bytes 3145732
  387.2 23.2 %copy-start.11 = (bf16[4,64,2048]{2,1,0:T(8,128)(2,1)}, bf16[4,64,2048]{2,1,0:T(8,128)(2,1)S(1)}, u32[]{:S(2)}) copy-start(bf16[4,64,2048]{2,1,0:T(8,128)(2,1)S(1)} %get-tuple-element.80.got2_ref) | copy-start | bytes 3145732
  387.2 23.2 %copy-start.13 = (bf16[8,256,16]{2,1,0:T(8,128)(2,1)}, bf16[8,256,16]{2,1,0:T(8,128)(2,1)S(1)}, u32[]{:S(2)}) copy-start(bf16[8,256,16]{2,1,0:T(8,128)(2,1)S(1)} %get-tuple-element.71.rank_ref) | copy-start | bytes 196612
  410.4 1.0 copy-start.3
  411.4 1.0 copy-start.4
  412.4 1.0 copy-start.5
  527.4 4.8 copy-start.14
  535.5 2.8 copy-start.16
  537.3 2.0 copy-start.15

commit v4 on v3

--- a/solution.py
+++ b/solution.py
@@ -444,78 +444,6 @@
     return rows <= cols
 
 
-def turn_back(gradient, packed):
-    left = lax.broadcasted_iota(jnp.int32, packed.shape, 1) < HDIM // 2
-    turned = pltpu.roll(packed, HDIM // 2, 1)
-    cos = jnp.where(left, packed, turned)
-    sin = jnp.where(left, turned, -packed)
-    return gradient * cos + pltpu.roll(gradient, HDIM // 2, 1) * sin
-
-
-def attend_back_kernel(
-    q_ref, k_ref, v_ref, go_ref, lse_ref, dots_ref, table_ref, dq_ref, dk_ref, dv_ref, acc_ref
-):
-    j = pl.program_id(1)
-    tile = k_ref.shape[0]
-    length = q_ref.shape[0]
-    scale = 1.0 / math.sqrt(HDIM)
-    factor = log2e * scale
-    k = k_ref[...]
-    v = v_ref[...]
-
-    @pl.when(j == 0)
-    def _():
-        acc_ref[...] = jnp.zeros_like(acc_ref)
-
-    def fold(i, carry, diagonal):
-        dk, dv = carry
-        at = pl.ds(pl.multiple_of(i * tile, tile), tile)
-        q = q_ref[at, :]
-        go = go_ref[at, :]
-        scores = dot_nt(k, q)
-        weight = jnp.exp2(scores * factor - lse_ref[0, :, at])
-        if diagonal:
-            weight = jnp.where(causal(scores, 0, 0), weight, 0.0)
-        grad_weight = dot_nt(v, go)
-        grad_scores = (weight * (grad_weight - dots_ref[0, :, at])).astype(jnp.bfloat16)
-        dv = dv + dot_nn(weight.astype(jnp.bfloat16), go)
-        dk = dk + dot_nn(grad_scores, q)
-        acc_ref[at, :] += dot_tn(grad_scores, k)
-        return (dk, dv)
-
-    zero = jnp.zeros((tile, HDIM), jnp.float32)
-    carry = fold(j, (zero, zero), True)
-    dk, dv = lax.fori_loop(j + 1, length // tile, lambda i, c: fold(i, c, False), carry)
-    at = pl.ds(pl.multiple_of(j * tile, tile), tile)
-    dk_ref[...] = turn_back(dk * scale, table_ref[at, :]).astype(dk_ref.dtype)
-    dv_ref[...] = dv.astype(dv_ref.dtype)
-    dq_ref[...] = turn_back(acc_ref[at, :] * scale, table_ref[at, :]).astype(dq_ref.dtype)
-
-
-def attend_back(q, k, v, go, lse, dots, table):
-    length = q.shape[0]
-    heads = q.shape[1] // HDIM
-    tile = attn_tile
-    whole = pl.BlockSpec((length, HDIM), lambda h, j: (0, h))
-    part = pl.BlockSpec((tile, HDIM), lambda h, j: (j, h))
-    row = pl.BlockSpec((1, 1, length), lambda h, j: (h, 0, 0))
-    rope = pl.BlockSpec((length, HDIM), lambda h, j: (0, 0))
-    return pl.pallas_call(
-        attend_back_kernel,
-        grid=(heads, length // tile),
-        in_specs=[whole, part, part, whole, row, row, rope],
-        out_specs=[part, part, part],
-        out_shape=[jax.ShapeDtypeStruct(q.shape, jnp.bfloat16)] * 3,
-        scratch_shapes=[pltpu.VMEM((length, HDIM), jnp.float32)],
-        cost_estimate=pl.CostEstimate(
-            flops=5 * heads * length * length * HDIM,
-            bytes_accessed=14 * length * heads * HDIM,
-            transcendentals=heads * length * length // 2,
-        ),
-        compiler_params=pltpu.CompilerParams(vmem_limit_bytes=32 << 20),
-    )(q, k, v, go, lse, dots, table)
-
-
 mesh_ids = pl.DeviceIdType.MESH
 
 
@@ -553,31 +481,33 @@
 
 
 class Gather:
-    def __init__(self, blocks, s, z, send, recv, half):
+    def __init__(self, blocks, s, z, send, recv, half, base=0):
         self.at = blocks
         self.s = s
         self.z = z
         self.send = send
         self.recv = recv
         self.half = half
+        self.base = base
 
     def rows(self, part):
-        return pl.ds(part * self.half, self.half)
+        if part is None:
+            return pl.ds(self.base, 2 * self.half)
+        return pl.ds(self.base + part * self.half, self.half)
 
     def copy(self, index, span, part, target):
-        ref = self.at.at[span] if part is None else self.at.at[span, self.rows(part)]
+        ref = self.at.at[span, self.rows(part)]
         return remote(ref, ref, self.send.at[index], self.recv.at[index], (target, self.z))
 
     def begin(self):
         s, x, y, other = self.s, flip(self.s, 2), flip(self.s, 4), flip(self.s, 1)
-        self.copies = [
+        for one in (
             self.copy(0, s, 0, x),
             self.copy(1, s, 1, y),
             self.copy(2, s, 1, x),
             self.copy(3, s, 0, y),
             self.copy(6, s, None, other),
-        ]
-        for one in self.copies:
+        ):
             one.start()
 
     def arrive_first(self):
@@ -588,7 +518,6 @@
         self.copy(1, y, 1, y).wait_recv()
         two = self.copy(5, y, 1, x)
         two.start()
-        self.copies += [one, two]
 
     def arrive_neighbours(self):
         s, x, y, other = self.s, flip(self.s, 2), flip(self.s, 4), flip(self.s, 1)
@@ -598,7 +527,6 @@
         self.copy(3, y, 0, y).wait_recv()
         two = self.copy(8, y, None, other)
         two.start()
-        self.copies += [one, two]
 
     def arrive_diagonal(self):
         s, other = self.s, flip(self.s, 1)
@@ -607,7 +535,6 @@
         self.copy(5, diagonal, 1, other).wait_recv()
         one = self.copy(9, diagonal, None, other)
         one.start()
-        self.copies += [one]
 
     def arrive_core(self, index):
         s = self.s
@@ -617,8 +544,20 @@
         return span
 
     def end(self):
-        for one in self.copies:
-            one.wait_send()
+        s, x, y, other = self.s, flip(self.s, 2), flip(self.s, 4), flip(self.s, 1)
+        for index, span, part, target in (
+            (0, s, 0, x),
+            (1, s, 1, y),
+            (2, s, 1, x),
+            (3, s, 0, y),
+            (4, x, 0, y),
+            (5, y, 1, x),
+            (6, s, None, other),
+            (7, x, None, other),
+            (8, y, None, other),
+            (9, flip(x, 4), None, other),
+        ):
+            self.copy(index, span, part, target).wait_send()
 
 
 gather_sems = 10
@@ -756,12 +695,15 @@
 
 
 class Reduce:
-    def __init__(self, product, s, z, out, inn, send, recv):
-        self.product = product
+    def __init__(self, rows, multiply, width, s, z, out, inn, own, send, recv):
+        self.rows = rows
+        self.multiply = multiply
+        self.width = width
         self.s = s
         self.z = z
         self.out = out
         self.inn = inn
+        self.own = own
         self.send = send
         self.recv = recv
         chip = s // 2
@@ -776,44 +718,80 @@
             self.out.at[index], self.inn.at[index], self.send.at[index], self.recv.at[index], (target, self.z)
         )
 
-    def give(self, index, chip, half, extra=None):
-        value = self.product(chip, half)
-        if extra is not None:
-            self.copy(extra).wait_recv()
-            value = value + self.inn[extra].astype(jnp.float32)
-        self.out[index] = value.astype(jnp.bfloat16)
-        self.copy(index).start()
+    def give(self, first, second):
+        both = jnp.concatenate([self.rows(*first[1:3]), self.rows(*second[1:3])], axis=0)
+        for job in (first, second):
+            if job[3] is not None:
+                self.copy(job[3]).wait_recv()
+
+        def one(part, _):
+            wide = pl.ds(pl.multiple_of(part * 512, 512), 512)
+            value = self.multiply(both, wide)
+            for job, piece in ((first, value[:128]), (second, value[128:])):
+                if job[3] is not None:
+                    piece = piece + self.inn[job[3], :, wide].astype(jnp.float32)
+                self.out[job[0], :, wide] = piece.astype(jnp.bfloat16)
+            return 0
+
+        lax.fori_loop(0, self.width // 512, one, 0)
+        self.copy(first[0]).start()
+        self.copy(second[0]).start()
 
     def begin(self):
-        self.give(0, self.cd, 0)
-        self.give(1, self.cd, 1)
-        self.give(2, self.cx, 0)
-        self.give(3, self.cy, 1)
-
-    def middle(self):
-        self.give(4, self.cy, 0, 0)
-        self.give(5, self.cx, 1, 1)
-
-    def finish(self, half):
-        indices = (2, 4) if half == 0 else (3, 5)
-        total = self.product(self.chip, half)
-        for index in indices:
-            self.copy(index).wait_recv()
-            total = total + self.inn[index].astype(jnp.float32)
-        return total
+        self.give((0, self.cd, 0, None), (1, self.cd, 1, None))
+
+    def second(self):
+        self.give((2, self.cx, 0, None), (4, self.cy, 0, 0))
+
+    def third(self):
+        self.copy(2).wait_send()
+        self.copy(4).wait_send()
+        self.give((5, self.cx, 1, 1), (3, self.cy, 1, None))
+
+    def keep(self):
+        both = jnp.concatenate([self.rows(self.chip, 0), self.rows(self.chip, 1)], axis=0)
+
+        def one(part, _):
+            wide = pl.ds(pl.multiple_of(part * 512, 512), 512)
+            self.own[:, wide] = self.multiply(both, wide)
+            return 0
+
+        lax.fori_loop(0, self.width // 512, one, 0)
+
+    def finish(self, half, use):
+        first, second = (2, 4) if half == 0 else (3, 5)
+        self.copy(first).wait_recv()
+        self.copy(second).wait_recv()
+
+        def one(part, _):
+            at = pl.ds(pl.multiple_of(part * 32, 32), 32)
+            row = pl.multiple_of(part * 64 + half * 32, 32)
+            total = (
+                self.own[pl.ds(pl.multiple_of(half * 128 + part * 32, 32), 32), :]
+                + self.inn[first, at, :].astype(jnp.float32)
+                + self.inn[second, at, :].astype(jnp.float32)
+            )
+            use(row, total)
+            return 0
+
+        lax.fori_loop(0, 4, one, 0)
 
     def end(self):
-        for index in range(6):
+        for index in (0, 1, 3, 5):
             self.copy(index).wait_send()
+
+
+def some_rows(load, half):
+    return jnp.concatenate([load(64 * j + 32 * half) for j in range(4)], axis=0)
 
 
 def front_kernel(
     x_ref, w_qkv_ref, w_out_ref, b_qkv_ref, a_out_ref, a_in_ref, b_od_ref, table_ref, cot_ref, set_ref,
     x_own_ref, m_own_ref, residual_ref, o_eff_ref, b_sel_ref, a_sel_ref, lse_ref,
     u_out, q_out, k_out, v_out, low_out, table_out, mixed_out, w_cat_out, cots_ref,
-    u_ref, w_buf, w_cat, q_buf, k_buf, v_buf, low_buf, tables, mixed, o_all, o_big, sib, out_buf, in_buf,
+    u_ref, w_buf, w_cat, q_buf, k_buf, v_buf, low_buf, tables, mixed, o_all, o_big, sib, out_buf, in_buf, own_sum,
     b_small, a_small,
-    a2a_send, a2a_recv, tab_send, tab_recv, ag_send, ag_recv, w_send, w_recv, o_send, o_recv, cot_send, cot_recv,
+    a2a_send, a2a_recv, tab_send, tab_recv, ag_send, ag_recv, ag2_send, ag2_recv, w_send, w_recv, o_send, o_recv, cot_send, cot_recv,
     small_send, small_recv, sib_send, sib_recv, red_send, red_recv, local_sem, store_sem,
 ):
     f32 = jnp.float32
@@ -845,13 +823,32 @@
     table_gather = Gather(tables, s, z, tab_send, tab_recv, 128)
     table_gather.begin()
     x_own_ref[z] = x_ref[z]
+
+    def arrived(d):
+        j = zs[d]
+        remote(x_ref.at[j], x_own_ref.at[j], a2a_send.at[d], a2a_recv.at[d], (s, j)).wait_recv()
+
+    def normalize(j):
+        def one(part, _):
+            normed, _ = norm_rows(x_own_ref[j, pl.ds(pl.multiple_of(part * 32, 32), 32), :].astype(f32))
+            u_ref[s, pl.ds(pl.multiple_of(j * 64 + part * 32, 32), 32), :] = normed.astype(bf16)
+            return 0
+
+        lax.fori_loop(0, 2, one, 0)
+
+    near = Gather(u_ref, s, z, ag_send, ag_recv, 64, pl.multiple_of((z // 2) * 128, 128))
+    rest = Gather(u_ref, s, z, ag2_send, ag2_recv, 64, pl.multiple_of((1 - z // 2) * 128, 128))
+    arrived(0)
+    normalize(z)
+    normalize(zs[0])
+    near.begin()
     table_gather.arrive_first()
     table_gather.arrive_neighbours()
-    table_gather.arrive_diagonal()
     for one in owns:
         one.wait()
-    for d, j in enumerate(zs):
-        remote(x_ref.at[j], x_own_ref.at[j], a2a_send.at[d], a2a_recv.at[d], (s, j)).wait_recv()
+    near.arrive_first()
+    arrived(1)
+    arrived(2)
     line = Line(w_buf, core, s, z, w_send, w_recv)
     line.begin()
     smalls = []
@@ -860,19 +857,21 @@
         smalls.append(remote(a_small.at[z], a_small.at[z], small_send.at[3 + d], small_recv.at[3 + d], (s, j)))
     for one in smalls:
         one.start()
-    for part in range(4):
-        normed, _ = norm_rows(x_own_ref[part].astype(f32))
-        u_ref[s, pl.ds(part * 64, 64), :] = normed.astype(bf16)
-    gather = Gather(u_ref, s, z, ag_send, ag_recv, 128)
-    gather.begin()
-    gather.arrive_first()
+    normalize(zs[1])
+    normalize(zs[2])
+    rest.begin()
+    table_gather.arrive_diagonal()
+    near.arrive_neighbours()
+    near.arrive_diagonal()
+    rest.arrive_first()
     line.hop(1)
-    gather.arrive_neighbours()
+    rest.arrive_neighbours()
+    rest.arrive_diagonal()
+    for index in range(4):
+        near.arrive_core(index)
+        rest.arrive_core(index)
+        table_gather.arrive_core(index)
     line.hop(2)
-    gather.arrive_diagonal()
-    for index in range(4):
-        gather.arrive_core(index)
-        table_gather.arrive_core(index)
     stores = [pltpu.make_async_copy(u_ref, u_out, store_sem.at[0])]
     stores[0].start()
     mine = set_ref[z]
@@ -908,7 +907,6 @@
     o_line = Line(o_all, core, s, z, o_send, o_recv)
     o_line.begin()
     cot_line = Line(cots_ref, None, s, z, cot_send, cot_recv)
-    cot_line.begin()
     line.arrive_core()
     lax.fori_loop(0, 6, merge, 0)
     left = lax.broadcasted_iota(jnp.int32, (256, HDIM), 1) < HDIM // 2
@@ -929,11 +927,18 @@
                 out[rows, HDIM * head : HDIM * head + HDIM] = piece.astype(bf16)
         return 0
 
-    lax.fori_loop(0, 3, project, 0)
-    o_line.hop(1)
-    lax.fori_loop(3, 6, project, 0)
-    o_line.hop(2)
-    lax.fori_loop(6, 8, project, 0)
+    def project_all(t, _):
+        project(t, 0)
+        for step, at in ((1, 2), (2, 6)):
+
+            @pl.when(t == at)
+            def _():
+                o_line.hop(step)
+
+        return 0
+
+    lax.fori_loop(0, 8, project_all, 0)
+    cot_line.begin()
     stores += [
         pltpu.make_async_copy(source, target, store_sem.at[1 + i])
         for i, (source, target) in enumerate(
@@ -977,9 +982,16 @@
         lse_ref[head, i] = top * factor + jnp.log2(total)
         return 0
 
-    lax.fori_loop(0, 3, attend, 0)
-    o_line.hop(3)
-    lax.fori_loop(3, 8, attend, 0)
+    def attend_all(index, _):
+        attend(index, 0)
+
+        @pl.when(index == 3)
+        def _():
+            o_line.hop(3)
+
+        return 0
+
+    lax.fori_loop(0, 8, attend_all, 0)
 
     def span_rows(span, first, count):
         return pl.ds(pl.multiple_of(span * 256 + first, 128), count)
@@ -994,39 +1006,52 @@
     stores[-1].start()
     o_line.arrive_core()
     b_row = b_od_ref[mine, 0]
-    for j in range(4):
+
+    def merge_out(j, _):
         head = (2 * core + j) % 4
-        merged = adapt_scale * dot_tn(a_sel_ref[head], b_row)
         for side in range(2):
-            o_big[pl.ds(j * HDIM, HDIM), pl.ds(side * 1024, 1024)] = (
-                o_all[head, side].astype(f32) + merged[:, side * 1024 : side * 1024 + 1024]
+            wide = slice(side * 1024, side * 1024 + 1024)
+            merged = adapt_scale * dot_tn(a_sel_ref[head], b_row[:, wide])
+            o_big[pl.ds(pl.multiple_of(j * HDIM, HDIM), HDIM), wide] = (
+                o_all[head, side].astype(f32) + merged
             ).astype(bf16)
+        return 0
+
+    lax.fori_loop(0, 4, merge_out, 0)
     o_eff_ref[...] = o_big[0 : 2 * HDIM, :]
     for one in crosses:
         one.wait_recv()
 
-    def product(c, half):
-        both = jnp.concatenate(
-            [mixed[span_rows(2 * c + core, half * 128, 128), :], sib[c, pl.ds(half * 128, 128), :]], axis=1
-        )
-        return dot_nn(both, o_big[...])
-
-    reduce = Reduce(product, s, z, out_buf, in_buf, red_send, red_recv)
+    def rows_of(c, half):
+        def load(row):
+            at = pl.ds(pl.multiple_of((2 * c + core) * 256 + row, 32), 32)
+            return jnp.concatenate([mixed[at, :], sib[c, pl.ds(row, 32), :]], axis=1)
+
+        return some_rows(load, half)
+
+    reduce = Reduce(
+        rows_of, lambda rows, wide: dot_nn(rows, o_big[:, wide]), x_ref.shape[2], s, z,
+        out_buf, in_buf, own_sum, red_send, red_recv,
+    )
     reduce.begin()
+    reduce.keep()
     cot_line.hop(1)
-    lax.fori_loop(6, 8, merge, 0)
-    reduce.middle()
-    lax.fori_loop(8, 12, merge, 0)
+    reduce.second()
+    lax.fori_loop(6, 12, merge, 0)
     stores.append(pltpu.make_async_copy(w_cat, w_cat_out, store_sem.at[7]))
     stores[-1].start()
+    reduce.third()
+    def settle(row, total):
+        at = pl.ds(row, 32)
+        x = x_own_ref[row // 64, pl.ds(pl.multiple_of(row % 64, 32), 32), :].astype(f32)
+        residual = x + total
+        residual_ref[at, :] = residual
+        normed, _ = norm_rows(residual)
+        m_own_ref[at, :] = normed.astype(bf16)
+
+    reduce.finish(0, settle)
     cot_line.hop(2)
-    for half in range(2):
-        total = reduce.finish(half)
-        x = x_own_ref[2 * half : 2 * half + 2].reshape(128, -1).astype(f32)
-        residual = x + total
-        residual_ref[pl.ds(half * 128, 128), :] = residual
-        normed, _ = norm_rows(residual)
-        m_own_ref[pl.ds(half * 128, 128), :] = normed.astype(bf16)
+    reduce.finish(1, settle)
     cot_line.hop(3)
     for one in stores:
         one.wait()
@@ -1035,7 +1060,8 @@
     line.end()
     o_line.end()
     cot_line.end()
-    gather.end()
+    near.end()
+    rest.end()
     table_gather.end()
     reduce.end()
 
@@ -1086,12 +1112,13 @@
             vm((4, 256, 256), bf16),
             vm((6, 128, width), bf16),
             vm((6, 128, width), bf16),
+            vm((256, width), f32),
             vm((4, 4, 3, 16, HDIM), bf16),
             vm((4, 4, 16, HDIM), bf16),
         ]
         + [
             dma((count,))
-            for count in (3, 3, 10, 10, 10, 10, 13, 13, 13, 13, 13, 13, 6, 6, 4, 4, 6, 6, 5, 8)
+            for count in (3, 3, 10, 10, 10, 10, 10, 10, 13, 13, 13, 13, 13, 13, 6, 6, 4, 4, 6, 6, 5, 8)
         ],
         cost_estimate=spend(150),
         compiler_params=pltpu.CompilerParams(
@@ -1100,88 +1127,261 @@
     )(x, w_qkv, w_out, b_qkv, a_out, a_in, b_out_down, table, cotangent, set_index)
 
 
-def spread_kernel(
-    g_ref, o_eff_ref, mixed_ref, b_od_ref, down1_ref, down2_ref, set_ref,
-    g_out, gm_ref, dots_ref, rank_ref, got1_ref, got2_ref, g_buf, send, recv, local_sem, down_send, down_recv,
+def turn_back(gradient, packed):
+    left = lax.broadcasted_iota(jnp.int32, packed.shape, 1) < HDIM // 2
+    turned = pltpu.roll(packed, HDIM // 2, 1)
+    cos = jnp.where(left, packed, turned)
+    sin = jnp.where(left, turned, -packed)
+    return gradient * cos + pltpu.roll(gradient, HDIM // 2, 1) * sin
+
+
+def back_kernel(
+    g_ref, o_eff_ref, mixed_in, b_od_ref, q_in, k_in, v_in, lse_ref, table_in,
+    grad_b_ref, grad_ad_ref, grad_a_ref, grad_bd_ref, down1_ref, down2_ref, down3_ref, set_ref,
+    dq_ref, dk_ref, dv_ref, rank_ref, chunk_ref, pair_ref, g_out, got1_ref, got2_ref,
+    mixed_ref, q_ref, k_ref, v_ref, table_ref, down2_buf, got3_buf, pair_sum, g_buf, gm_buf, dots, dk_acc, dv_acc, chunk_src, chunk_sib, chunk_sum, chunk_in,
+    send, recv, down_send, down_recv, cs_send, cs_recv, cx_send, cx_recv, store_sem, load_sem,
 ):
+    f32 = jnp.float32
+    bf16 = jnp.bfloat16
     s, z = places()
-    meet(
-        [(None, (flip(s, 1), z)), (None, (flip(s, 2), z)), (None, (flip(s, 4), z))]
-        + [(None, (s, flip(z, 1))), (None, (s, flip(z, 2)))]
-    )
+    loads = [
+        pltpu.make_async_copy(source, target, load_sem.at[i])
+        for i, (source, target) in enumerate(
+            (
+                (mixed_in, mixed_ref),
+                (q_in, q_ref),
+                (k_in, k_ref),
+                (v_in, v_ref),
+                (table_in, table_ref),
+                (down2_ref, down2_buf),
+            )
+        )
+    ]
+    for one in loads:
+        one.start()
+    core = s % 2
+    chip = s // 2
+    other = flip(s, 1)
+    sx = flip(s, 2)
+    sy = flip(s, 4)
+    sd = flip(sx, 4)
+    meet([(None, (t, z)) for t in (other, sx, sy, sd)] + [(None, (s, flip(z, 1))), (None, (s, flip(z, 2)))])
+    g_buf[s] = g_ref[...]
+    gather = Gather(g_buf, s, z, send, recv, 128)
+    gather.begin()
     results = [
-        remote(down1_ref, got1_ref, down_send.at[0], down_recv.at[0], (s, flip(z, 1))),
-        remote(down2_ref, got2_ref, down_send.at[1], down_recv.at[1], (s, flip(z, 2))),
+        remote(down3_ref, got3_buf, down_send.at[0], down_recv.at[0], (s, flip(z, 1))),
+        remote(down1_ref, got1_ref, down_send.at[1], down_recv.at[1], (s, flip(z, 1))),
     ]
     for one in results:
         one.start()
-    g_buf[s] = g_ref[...]
-    gather = Gather(g_buf, s, z, send, recv, 128)
-    gather.begin()
+    onward = remote(pair_sum, got2_ref, down_send.at[2], down_recv.at[2], (s, flip(z, 2)))
+    member = set_ref[z]
+    tile = attn_tile
+    scale = 1.0 / math.sqrt(HDIM)
+    factor = log2e * scale
+    dk_acc[...] = jnp.zeros_like(dk_acc)
+    dv_acc[...] = jnp.zeros_like(dv_acc)
 
     def store(t):
-        return pltpu.make_async_copy(g_buf.at[t], g_out.at[t], local_sem.at[0])
-
-    def work(t):
-        g = g_buf[t]
-        store(t).start()
-        back = dot_nt(g, o_eff_ref[...]).astype(jnp.bfloat16)
-        gm_ref[t] = back
-        product = back.astype(jnp.float32) * mixed_ref[t].astype(jnp.float32)
+        return pltpu.make_async_copy(g_buf.at[t], g_out.at[t], store_sem.at[t])
+
+    def chip_rows(c):
+        here = pl.ds(pl.multiple_of(c * tile, tile), tile)
+
+        def head_rows(part, _):
+            t = 2 * c + part
+            store(t).start()
+            g = g_buf[t]
+            back = dot_nt(g, o_eff_ref[...]).astype(bf16)
+            gm_buf[pl.ds(pl.multiple_of(part * 256, 256), 256), :] = back
+            product = back.astype(f32) * mixed_ref[
+                pl.ds(pl.multiple_of(t * 256, 256), 256), :
+            ].astype(f32)
+            for head in range(2):
+                turned = jnp.transpose(product[:, HDIM * head : HDIM * head + HDIM])
+                dots[head, :, pl.ds(pl.multiple_of(part * 256, 256), 256)] = jnp.sum(turned, axis=0, keepdims=True)
+            rank_ref[t] = (adapt_scale * dot_nt(g, b_od_ref[member, 0])).astype(bf16)
+            return 0
+
+        lax.fori_loop(0, 2, head_rows, 0)
+
+        def one_head(head, _):
+            lanes = pl.ds(pl.multiple_of(head * HDIM, HDIM), HDIM)
+            q = q_ref[here, lanes]
+            go = gm_buf[:, lanes]
+            row_dots = dots[head]
+            lse = lse_ref[head, c]
+
+            def fold(j, dq, diagonal):
+                at = pl.ds(pl.multiple_of(j * tile, tile), tile)
+                k = k_ref[at, lanes]
+                scores = dot_nt(k, q)
+                weight = jnp.exp2(scores * factor - lse)
+                if diagonal:
+                    weight = jnp.where(causal(scores, 0, 0), weight, 0.0)
+                grad_weight = dot_nt(v_ref[at, lanes], go)
+                grad_scores = (weight * (grad_weight - row_dots)).astype(bf16)
+                dv_acc[at, lanes] += dot_nn(weight.astype(bf16), go)
+                dk_acc[at, lanes] += dot_nn(grad_scores, q)
+                return dq + dot_tn(grad_scores, k)
+
+            dq = lax.fori_loop(0, c, lambda j, total: fold(j, total, False), jnp.zeros((tile, HDIM), f32))
+            dq = fold(c, dq, True)
+            dq_ref[here, lanes] = turn_back(dq * scale, table_ref[here, :]).astype(bf16)
+            return 0
+
+        lax.fori_loop(0, 2, one_head, 0)
+
+    def fill(one, _):
+        whole = jnp.zeros((48, dk_acc.shape[0]), f32)
+        split = jnp.zeros((48, dk_acc.shape[0]), f32)
+        for seq in range(4):
+            used = (set_ref[seq] == one).astype(f32)
+            whole += used * jnp.concatenate([grad_a_ref[seq], grad_bd_ref[seq]], axis=0)
+            split += used * jnp.concatenate([grad_b_ref[seq, 0], grad_b_ref[seq, 1], grad_ad_ref[seq]], axis=0)
+        for part in range(2):
+            rows = slice(24 * part, 24 * part + 24)
+            chunk_src[2 * one + part] = jnp.concatenate([whole[rows], split[rows]], axis=0).astype(bf16)
+        return 0
+
+    lax.fori_loop(0, 4, fill, 0)
+    crosses = [
+        remote(chunk_src.at[2 * c + 1 - core], chunk_sib.at[c], cs_send.at[c], cs_recv.at[c], (other, z))
+        for c in range(4)
+    ]
+    for one in crosses:
+        one.start()
+    for one in loads:
+        one.wait()
+    around = [
+        remote(chunk_sum.at[t // 2], chunk_in.at[d], cx_send.at[d], cx_recv.at[d], (t, z))
+        for d, t in enumerate((sx, sy, sd))
+    ]
+
+    def total_chunks(c, _):
+        chunk_sum[c] = (chunk_src[2 * c + core].astype(f32) + chunk_sib[c].astype(f32)).astype(bf16)
+        return 0
+
+    def pair_rows(seq, _):
+        for first, target in ((0, pair_sum), (2, pair_ref)):
+            target[seq] = (
+                down2_buf[first + seq].astype(f32) + got3_buf[first + seq].astype(f32)
+            ).astype(bf16)
+        return 0
+
+    def visit(step, _):
+        @pl.when(step == 0)
+        def _():
+            gather.arrive_core(0)
+
+        @pl.when(step == 1)
+        def _():
+            gather.arrive_first()
+            for one in crosses:
+                one.wait_recv()
+            lax.fori_loop(0, 4, total_chunks, 0)
+            for one in around:
+                one.start()
+            gather.arrive_neighbours()
+            results[0].wait_recv()
+            lax.fori_loop(0, 2, pair_rows, 0)
+            onward.start()
+            gather.arrive_core(1)
+
+        @pl.when(step == 2)
+        def _():
+            gather.arrive_core(2)
+
+        @pl.when(step == 3)
+        def _():
+            gather.arrive_diagonal()
+            gather.arrive_core(3)
+
+        by_x = step % 2
+        by_y = step // 2
+        chip_rows(chip + by_x * (1 - 2 * (chip % 2)) + by_y * (2 - 4 * (chip // 2)))
+        return 0
+
+    lax.fori_loop(0, 4, visit, 0)
+
+    def last(j, _):
+        at = pl.ds(pl.multiple_of(j * tile, tile), tile)
         for head in range(2):
-            turned = jnp.transpose(product[:, HDIM * head : HDIM * head + HDIM])
-            dots_ref[head, t] = jnp.sum(turned, axis=0, keepdims=True)
-        rank_ref[t] = (adapt_scale * dot_nt(g, b_od_ref[set_ref[z], 0])).astype(jnp.bfloat16)
+            lanes = slice(HDIM * head, HDIM * head + HDIM)
+            dk_ref[at, lanes] = turn_back(dk_acc[at, lanes] * scale, table_ref[at, :]).astype(bf16)
+            dv_ref[at, lanes] = dv_acc[at, lanes].astype(bf16)
+        return 0
+
+    lax.fori_loop(0, 4, last, 0)
+    for one in around:
+        one.wait_recv()
+    chunk = chunk_sum[chip].astype(f32)
+    for d in range(3):
+        chunk += chunk_in[d].astype(f32)
+    chunk_ref[...] = chunk
+    for t in range(8):
         store(t).wait()
-
-    work(s)
-    gather.arrive_first()
-    work(gather.arrive_core(0))
-    gather.arrive_neighbours()
-    work(flip(s, 2))
-    work(flip(s, 4))
-    work(gather.arrive_core(1))
-    work(gather.arrive_core(2))
-    gather.arrive_diagonal()
-    work(flip(flip(s, 2), 4))
-    work(gather.arrive_core(3))
     gather.end()
-    for one in results:
-        one.wait()
-
-
-def spread_layer(g_own, o_eff, mixed, b_out_down, down1, down2, set_index):
+    results[1].wait_recv()
+    onward.wait()
+    for one in crosses + around + results:
+        one.wait_send()
+
+
+def back_layer(*operands):
     bf16 = jnp.bfloat16
+    f32 = jnp.float32
     vmem = pl.BlockSpec(memory_space=pltpu.VMEM)
     anywhere = pl.BlockSpec(memory_space=pl.ANY)
-    width = g_own.shape[1]
+    width = operands[0].shape[1]
     shape = jax.ShapeDtypeStruct
     dma = pltpu.SemaphoreType.DMA
+    vm = pltpu.VMEM
     return pl.pallas_call(
-        spread_kernel,
-        in_specs=[vmem] * 4 + [anywhere] * 2 + [pl.BlockSpec(memory_space=pltpu.SMEM)],
-        out_specs=[anywhere, vmem, vmem, vmem, anywhere, anywhere],
+        back_kernel,
+        in_specs=[vmem, vmem, anywhere, vmem, anywhere, anywhere, anywhere, vmem, anywhere]
+        + [vmem] * 4
+        + [anywhere] * 3
+        + [pl.BlockSpec(memory_space=pltpu.SMEM)],
+        out_specs=[vmem] * 6 + [anywhere] * 3,
         out_shape=[
+            shape((2048, 256), bf16),
+            shape((2048, 256), bf16),
+            shape((2048, 256), bf16),
+            shape((8, 256, 16), bf16),
+            shape((48, width), f32),
+            shape((2, 64, width), bf16),
             shape((8, 256, width), bf16),
-            shape((8, 256, 256), bf16),
-            shape((2, 8, 1, 256), jnp.float32),
-            shape((8, 256, 16), bf16),
-            shape(down1.shape, bf16),
-            shape(down2.shape, bf16),
+            shape((4, 64, width), bf16),
+            shape((2, 64, width), bf16),
         ],
         scratch_shapes=[
-            pltpu.VMEM((8, 256, width), bf16),
-            dma((gather_sems,)),
-            dma((gather_sems,)),
-            dma((1,)),
-            dma((2,)),
-            dma((2,)),
-        ],
-        cost_estimate=spend(40),
+            vm((2048, 256), bf16),
+            vm((2048, 256), bf16),
+            vm((2048, 256), bf16),
+            vm((2048, 256), bf16),
+            vm((2048, HDIM), f32),
+            vm((4, 64, width), bf16),
+            vm((4, 64, width), bf16),
+            vm((2, 64, width), bf16),
+            vm((8, 256, width), bf16),
+            vm((512, 256), bf16),
+            vm((2, 1, 512), f32),
+            vm((2048, 256), f32),
+            vm((2048, 256), f32),
+            vm((8, 48, width), bf16),
+            vm((4, 48, width), bf16),
+            vm((4, 48, width), bf16),
+            vm((3, 48, width), bf16),
+        ]
+        + [dma((count,)) for count in (gather_sems, gather_sems, 3, 3, 4, 4, 3, 3, 8, 6)],
+        cost_estimate=spend(60),
         compiler_params=pltpu.CompilerParams(
-            collective_id=3, has_side_effects=True, vmem_limit_bytes=48 << 20
+            collective_id=3, has_side_effects=True, vmem_limit_bytes=52 << 20
         ),
-    )(g_own, o_eff, mixed, b_out_down, down1, down2, set_index)
+    )(*operands)
 
 
 def mlp_line_kernel(
@@ -1205,17 +1405,16 @@
     ids = [z, pair, 2 - high, 3 - 3 * high]
     far = 3 - 3 * high
 
-    loads = []
+    def load_tile(h):
+        columns = pl.ds(h * tile if isinstance(h, int) else pl.multiple_of(h * tile, tile), tile)
+        return [
+            pltpu.make_async_copy(w_gu_ref.at[0, :, columns], wg.at[h], weight_sem.at[3 * h]),
+            pltpu.make_async_copy(w_gu_ref.at[1, :, columns], wu.at[h], weight_sem.at[3 * h + 1]),
+            pltpu.make_async_copy(w_d_ref.at[columns, :], wd.at[h], weight_sem.at[3 * h + 2]),
+        ]
+
     for h in range(tiles):
-        columns = pl.ds(h * tile, tile)
-        loads.append(
-            [
-                pltpu.make_async_copy(w_gu_ref.at[0, :, columns], wg.at[h], weight_sem.at[3 * h]),
-                pltpu.make_async_copy(w_gu_ref.at[1, :, columns], wu.at[h], weight_sem.at[3 * h + 1]),
-                pltpu.make_async_copy(w_d_ref.at[columns, :], wd.at[h], weight_sem.at[3 * h + 2]),
-            ]
-        )
-        for one in loads[-1]:
+        for one in load_tile(h):
             one.start()
 
     others = [z, pair, flip(z, 2), opposite]
@@ -1284,7 +1483,7 @@
                 down(t, z + t).wait_send()
 
     def piece(p):
-        return pl.ds(p * 64, 64)
+        return pl.ds(p * 64 if isinstance(p, int) else pl.multiple_of(p * 64, 64), 64)
 
     def copy1():
         return remote(slots.at[1], r1, send1.at[0], recv1.at[0], (s, pair))
@@ -1309,21 +1508,43 @@
     def in_maps(seq):
         return a_ref[set_ref[seq], 3:5].reshape(32, -1)
 
-    def compute(slot):
-        seq = ids[slot]
+    def sequence(slot):
+        return sum((slot == i).astype(jnp.int32) * one for i, one in enumerate(ids + [z]))
+
+    def add(slot, extra):
+        def one(p, _):
+            slots[slot, piece(p), :] = (
+                slots[slot, piece(p), :].astype(f32) + extra[piece(p), :].astype(f32)
+            ).astype(bf16)
+            return 0
+
+        lax.fori_loop(0, 4, one, 0)
+
+    begin()
+
+    def chunk(slot, _):
+        seq = sequence(slot)
         member = set_ref[seq]
-        rows = m_buf[seq]
         for one in load_cot(seq):
             one.wait()
-        ranks[:, 0:32] = adapt_scale * dot_nt(rows, in_maps(seq))
-        cot = cot_buf[...].reshape(256, -1)
-        ranks[:, 32:48] = adapt_scale * dot_nt(cot, bd_ref[member, 1])
+        ranks[:, 0:32] = adapt_scale * dot_nt(m_buf[seq], in_maps(seq))
+        ranks[:, 32:48] = adapt_scale * dot_nt(cot_buf[...].reshape(256, -1), bd_ref[member, 1])
         ranks[:, 48:96] = jnp.zeros((256, 48), f32)
         back_acc[...] = jnp.zeros_like(back_acc)
         down_acc[...] = jnp.zeros_like(down_acc)
 
         def step(h, _):
             columns = pl.ds(pl.multiple_of(h * tile, tile), tile)
+
+            @pl.when(slot == 0)
+            def _():
+                for one in load_tile(h):
+                    one.wait()
+
+            @pl.when((slot == 3) & (h == 1) & middle)
+            def _():
+                copy1().start()
+
             low = ranks[...].astype(bf16)
             low_gate = low[:, 0:16]
             low_up = low[:, 16:32]
@@ -1352,77 +1573,54 @@
             grad_ad_ref[seq, :, columns] = dot_tn(low_cot, act)
             return 0
 
-        if slot == 0:
-            for h in range(tiles):
-                for one in loads[h]:
-                    one.wait()
         lax.fori_loop(0, tiles, step, 0)
+        for t in (1, 2, 3):
+
+            @pl.when(slot == t - 1)
+            def _():
+                hop(t)
+
         back_rank = (adapt_scale * ranks[:, 64:96]).astype(bf16)
         slots[slot] = (back_acc[...] + dot_nn(back_rank, in_maps(seq))).astype(bf16)
 
-    def rest(slot):
-        seq = ids[slot]
-        back_rank = (adapt_scale * ranks[:, 64:96]).astype(bf16)
+        @pl.when((slot == 1) & at_end)
+        def _():
+            copy1().start()
+
+        @pl.when((slot == 2) & at_end)
+        def _():
+            copy3().start()
+
+        @pl.when((slot == 3) & at_end)
+        def _():
+            copy5(0).start()
+            copy5(1).start()
+
+        @pl.when((slot == 3) & middle)
+        def _():
+            copy3().wait_recv()
+            add(2, r3)
+            copy2().start()
+
         low_down = (adapt_scale * ranks[:, 48:64]).astype(bf16)
         grad_a_ref[seq] = dot_tn(back_rank, m_buf[seq])
         grad_bd_ref[seq] = dot_tn(low_down, cot_buf[...].reshape(256, -1))
-        if slot > 0:
-            for one in stage_copies(ids[slot - 1]):
+
+        @pl.when(slot > 0)
+        def _():
+            for one in stage_copies(seq):
                 one.wait()
-        value = down_acc[...] + dot_nn(low_down, bd_ref[set_ref[seq], 1])
-        if slot == 0:
-            value = value + residual_ref[...]
+
+        own = (slot == 0).astype(f32)
+        value = down_acc[...] + dot_nn(low_down, bd_ref[member, 1]) + own * residual_ref[...]
         stage[...] = value.astype(bf16).reshape(4, 64, -1)
         for one in stage_copies(seq):
             one.start()
-        following = ids[slot + 1] if slot < 3 else z
-        for one in load_cot(following):
+        for one in load_cot(sequence(slot + 1)):
             one.start()
-
-    def add(slot, p, extra):
-        slots[slot, piece(p), :] = (
-            slots[slot, piece(p), :].astype(f32) + extra[piece(p), :].astype(f32)
-        ).astype(bf16)
-
-    begin()
-    compute(0)
-    rest(0)
-    hop(1)
-    compute(1)
-
-    @pl.when(at_end)
-    def _():
-        copy1().start()
-
-    rest(1)
-    hop(2)
-    compute(2)
-
-    @pl.when(at_end)
-    def _():
-        copy3().start()
-
-    @pl.when(middle)
-    def _():
-        copy1().start()
-
-    rest(2)
-    hop(3)
-    compute(3)
-
-    @pl.when(at_end)
-    def _():
-        copy5(0).start()
-        copy5(1).start()
-
-    @pl.when(middle)
-    def _():
-        copy3().wait_recv()
-        for p in range(4):
-            add(2, p, r3)
-        copy2().start()
-
-    rest(3)
+        return 0
+
+    lax.fori_loop(0, 4, chunk, 0)
 
     @pl.when(at_end)
     def _():
@@ -1432,36 +1630,50 @@
 
     @pl.when(middle)
     def _():
-        for p in range(4):
+        def one(p, _):
             copy5(p).wait_recv()
-            add(3, p, r5)
+            slots[3, piece(p), :] = (
+                slots[3, piece(p), :].astype(f32) + r5[piece(p), :].astype(f32)
+            ).astype(bf16)
             copy4(p).start()
+            return 0
+
+        lax.fori_loop(0, 4, one, 0)
 
     copy1().wait_recv()
-    for p in range(4):
-        add(0, p, r1)
+    add(0, r1)
 
     @pl.when(middle)
     def _():
         copy2().wait_recv()
-        for p in range(4):
-            add(0, p, r2)
+        add(0, r2)
 
     for one in load_cot(z):
         one.wait()
-    for p in range(4):
-
+
+    def settle(p, _):
         @pl.when(at_end)
         def _():
             copy4(p).wait_recv()
-            add(0, p, r4)
-
-        grad = slots[0, piece(p), :].astype(f32)
-        normed, inverse = norm_rows(residual_ref[piece(p), :])
-        value = cot_buf[p].astype(f32) + norm_back(grad, normed, inverse)
-        grad_res_ref[piece(p), :] = value
-        g_ref[piece(p), :] = value.astype(bf16)
-    for one in stage_copies(ids[3]):
+            slots[0, piece(p), :] = (
+                slots[0, piece(p), :].astype(f32) + r4[piece(p), :].astype(f32)
+            ).astype(bf16)
+
+        def rows32(half, _):
+            at = pl.ds(pl.multiple_of(p * 64 + half * 32, 32), 32)
+            grad = slots[0, at, :].astype(f32)
+            normed, inverse = norm_rows(residual_ref[at, :])
+            cot = cot_buf[p, pl.ds(pl.multiple_of(half * 32, 32), 32), :].astype(f32)
+            value = cot + norm_back(grad, normed, inverse)
+            grad_res_ref[at, :] = value
+            g_ref[at, :] = value.astype(bf16)
+            return 0
+
+        lax.fori_loop(0, 2, rows32, 0)
+        return 0
+
+    lax.fori_loop(0, 4, settle, 0)
+    for one in stage_copies(z):
         one.wait()
     hop_end()
     copy1().wait_send()
@@ -1538,18 +1750,35 @@
 
 
 def finish_kernel(
-    dq_ref, dk_ref, dv_ref, w_ref, x_own_ref, residual_ref, u_ref, g_ref, low_ref, rank_ref, mixed_ref,
-    b_sel_ref, a_sel_ref, grad_b_ref, grad_ad_ref, grad_a_ref, grad_bd_ref, down0_ref, got1_ref, got2_ref, down3_ref,
+    dq_ref, dk_ref, dv_ref, w_in, x_own_ref, residual_in, u_ref, g_ref, low_ref, rank_ref, mixed_in,
+    b_sel_ref, a_sel_ref, chunk_ref, down0_in, got1_in, got2_in, pair_ref,
     set_ref,
-    result_ref, grad_ref, pool_ref, heads_ref, got3_ref,
-    own_ref, sib_q, sib_k, sib_v, out_buf, in_buf, u_buf, g_buf, a_acc, b_acc, chunk_src, chunk_sib, chunk_sum,
-    chunk_in, z_src, z_in, head_src, head_in,
+    result_ref, grad_ref, sets_ref, pool_ref, heads_ref, got3_ref,
+    w_ref, residual_ref, mixed_ref, down0_ref, got1_ref, got2_ref,
+    own_ref, sib_q, sib_k, sib_v, out_buf, in_buf, own_sum, u_buf, g_buf, a_acc, b_acc, chunk_src, chunk_sib, chunk_sum,
+    chunk_in, z_src, z_in, sets_src, sets_in, head_src, head_in,
     a2a_send, a2a_recv, sib_send, sib_recv, send, recv, load_sem, cs_send, cs_recv, cx_send, cx_recv,
     cz_send, cz_recv, cg_send, cg_recv, hz_send, hz_recv, hg_send, hg_recv, down_send, down_recv,
+    sz_send, sz_recv, sg_send, sg_recv, late_sem,
 ):
     f32 = jnp.float32
     bf16 = jnp.bfloat16
     s, z = places()
+    loads = [
+        pltpu.make_async_copy(source, target, late_sem.at[i])
+        for i, (source, target) in enumerate(
+            (
+                (w_in, w_ref),
+                (mixed_in, mixed_ref),
+                (residual_in, residual_ref),
+                (down0_in, down0_ref),
+                (got1_in, got1_ref),
+                (got2_in, got2_ref),
+            )
+        )
+    ]
+    for one in loads[:2]:
+        one.start()
     core = s % 2
     chip = s // 2
     other = flip(s, 1)
@@ -1558,8 +1787,12 @@
     sd = flip(sx, 4)
     zs = [flip(z, 1), flip(z, 2), 3 - z]
     meet([(None, (t, z)) for t in (other, sx, sy, sd)] + [(None, (s, j)) for j in zs])
-    last_down = remote(down3_ref, got3_ref, down_send.at[0], down_recv.at[0], (s, 3 - z))
+    last_down = remote(pair_ref, got3_ref, down_send.at[0], down_recv.at[0], (s, flip(z, 2)))
     last_down.start()
+    sets_src[...] = chunk_ref[0:32].astype(bf16)
+    sets_along = [remote(sets_src, sets_in.at[d], sz_send.at[d], sz_recv.at[d], (s, j)) for d, j in enumerate(zs)]
+    for one in sets_along:
+        one.start()
     mine = (dq_ref, dk_ref, dv_ref)
     theirs = (sib_q, sib_k, sib_v)
     swaps = [
@@ -1583,15 +1816,25 @@
     for one in swaps:
         one.wait_recv()
 
-    def product(c, half):
-        rows = pl.ds(half * 128, 128)
-        both = jnp.concatenate(
-            [ref[2 * c + core, rows, :] for ref in mine] + [ref[c, rows, :] for ref in theirs], axis=1
-        )
-        return dot_nt(both, w_ref[...])
-
-    reduce = Reduce(product, s, z, out_buf, in_buf, send, recv)
+    def rows_of(c, half):
+        def load(row):
+            at = pl.ds(row, 32)
+            return jnp.concatenate(
+                [ref[2 * c + core, at, :] for ref in mine] + [ref[c, at, :] for ref in theirs], axis=1
+            )
+
+        return some_rows(load, half)
+
+    reduce = Reduce(
+        rows_of, lambda rows, wide: dot_nt(rows, w_ref[wide, :]), x_own_ref.shape[2], s, z,
+        out_buf, in_buf, own_sum, send, recv,
+    )
+    loads[0].wait()
     reduce.begin()
+    for one in loads[2:]:
+        one.start()
+    reduce.keep()
+    loads[1].wait()
 
     b_two = [
         jnp.concatenate(
@@ -1601,29 +1844,43 @@
     ]
     a_two = jnp.concatenate([a_sel_ref[2 * core], a_sel_ref[2 * core + 1]], axis=1)
 
-    def adapt(t, first):
+    a_acc[...] = jnp.zeros_like(a_acc)
+    b_acc[...] = jnp.zeros_like(b_acc)
+
+    def adapt(t, _):
         for one in load(t):
             one.wait()
-        if t < 7:
+
+        @pl.when(t < 7)
+        def _():
             for one in load(t + 1):
                 one.start()
+
         back = jnp.concatenate([dot_nt(mine[p][t], b_two[p]) for p in range(3)], axis=1)
         back = (adapt_scale * back).astype(bf16)
-        a_part = dot_tn(back, u_buf[t % 2])
         lows = (adapt_scale * dot_nt(mixed_ref[t], a_two)).astype(bf16)
-        b_part = dot_tn(lows, g_buf[t % 2])
-        if first:
-            a_acc[...] = a_part
-            b_acc[...] = b_part
-        else:
-            a_acc[...] += a_part
-            b_acc[...] += b_part
-
-    for t in range(3):
-        adapt(t, t == 0)
-    reduce.middle()
-    for t in range(3, 8):
-        adapt(t, False)
+        u = u_buf.at[t % 2]
+        g = g_buf.at[t % 2]
+
+        def one(part, _):
+            wide = pl.ds(pl.multiple_of(part * 512, 512), 512)
+            a_acc[:, wide] += dot_tn(back, u[:, wide])
+            b_acc[:, wide] += dot_tn(lows, g[:, wide])
+            return 0
+
+        lax.fori_loop(0, 4, one, 0)
+
+        @pl.when(t == 2)
+        def _():
+            reduce.second()
+
+        @pl.when(t == 6)
+        def _():
+            reduce.third()
+
+        return 0
+
+    lax.fori_loop(0, 8, adapt, 0)
     per_head = [
         dot_tn(low_ref[...].reshape(2048, 48)[:, 16 * p : 16 * p + 16], mine[p][...].reshape(2048, 256))
         for p in range(3)
@@ -1647,25 +1904,9 @@
         def _():
             head_in[z] = head_src[head]
 
-    for member in range(4):
-        whole = jnp.zeros((48, a_acc.shape[1]), f32)
-        split = jnp.zeros((48, a_acc.shape[1]), f32)
-        for seq in range(4):
-            used = (set_ref[seq] == member).astype(f32)
-            whole += used * jnp.concatenate([grad_a_ref[seq], grad_bd_ref[seq]], axis=0)
-            split += used * jnp.concatenate([grad_b_ref[seq, 0], grad_b_ref[seq, 1], grad_ad_ref[seq]], axis=0)
-        for part in range(2):
-            i = 2 * member + part
-            sequence = a_acc[8 * i : 8 * i + 8] if i < 6 else b_acc[8 * i - 48 : 8 * i - 40]
-            chunk_src[i] = jnp.concatenate(
-                [
-                    whole[24 * part : 24 * part + 24],
-                    sequence,
-                    split[24 * part : 24 * part + 24],
-                    jnp.zeros((8, a_acc.shape[1]), f32),
-                ],
-                axis=0,
-            ).astype(bf16)
+    for i in range(8):
+        sequence = a_acc[8 * i : 8 * i + 8] if i < 6 else b_acc[8 * i - 48 : 8 * i - 40]
+        chunk_src[i] = jnp.concatenate([sequence, jnp.zeros((8, a_acc.shape[1]), f32)], axis=0).astype(bf16)
     crosses = [
         remote(chunk_src.at[2 * c + 1 - core], chunk_sib.at[c], cs_send.at[c], cs_recv.at[c], (other, z))
         for c in range(4)
@@ -1683,37 +1924,66 @@
     for one in around:
         one.start()
 
+    for one in sets_along:
+        one.wait_recv()
+    whole = chunk_ref[0:24]
+    for d in range(3):
+        whole += sets_in[d, 0:24].astype(f32)
+    sets_ref[s] = jnp.concatenate([whole, chunk_ref[24:48]], axis=0).astype(bf16)
+
+    for one in loads[2:]:
+        one.wait()
+    def settle(row, total):
+        at = pl.ds(row, 32)
+        inside = pl.ds(pl.multiple_of(row % 64, 32), 32)
+        normed, inverse = norm_rows(x_own_ref[row // 64, inside, :].astype(f32))
+        value = residual_ref[at, :] + norm_back(total, normed, inverse)
+        own_ref[row // 64, inside, :] = value.astype(bf16)
+
+    def back(d, half):
+        rows = pl.ds(32 * half, 32)
+        return remote(
+            own_ref.at[zs[d], rows], grad_ref.at[z, rows], a2a_send.at[2 * d + half], a2a_recv.at[2 * d + half],
+            (s, zs[d]),
+        )
+
+    backs = []
     for half in range(2):
-        total = reduce.finish(half)
-        x = x_own_ref[2 * half : 2 * half + 2].reshape(128, -1).astype(f32)
-        normed, inverse = norm_rows(x)
-        value = residual_ref[pl.ds(half * 128, 128), :] + norm_back(total, normed, inverse)
-        own_ref[2 * half : 2 * half + 2] = value.astype(bf16).reshape(2, 64, -1)
-    backs = [
-        remote(own_ref.at[j], grad_ref.at[z], a2a_send.at[d], a2a_recv.at[d], (s, j)) for d, j in enumerate(zs)
-    ]
-    for one in backs:
+        reduce.finish(half, settle)
+        for d in range(3):
+            backs.append(back(d, half))
+            backs[-1].start()
+        if half == 0:
+            for one in around:
+                one.wait_recv()
+            chunk = chunk_sum[chip].astype(f32)
+            for d in range(3):
+                chunk += chunk_in[d].astype(f32)
+            z_src[...] = chunk.astype(bf16)
+            along = [remote(z_src, z_in.at[d], cz_send.at[d], cz_recv.at[d], (s, j)) for d, j in enumerate(zs)]
+            for one in along:
+                one.start()
+    grad_ref[z] = own_ref[z]
+
+    def sets_copy(t, index, target):
+        return remote(sets_ref.at[t], sets_ref.at[t], sg_send.at[index], sg_recv.at[index], (target, z))
+
+    sets_gives = [sets_copy(s, index, target) for index, target in enumerate((sx, sy, sd, other))]
+    for one in sets_gives:
         one.start()
-    grad_ref[z] = own_ref[z]
 
     last_down.wait_recv()
-    for part in range(4):
-        result_ref[part] = (
-            down0_ref[part].astype(f32)
-            + got1_ref[part].astype(f32)
-            + got2_ref[part].astype(f32)
-            + got3_ref[part].astype(f32)
-        ).astype(bf16)
-    for one in around:
-        one.wait_recv()
-    chunk = chunk_sum[chip].astype(f32)
-    for d in range(3):
-        chunk += chunk_in[d].astype(f32)
-    z_src[...] = chunk[0:32].astype(bf16)
-    along = [remote(z_src, z_in.at[d], cz_send.at[d], cz_recv.at[d], (s, j)) for d, j in enumerate(zs)]
-    for one in along:
-        one.start()
-
+
+    def result_rows(part, _):
+        for first, other_pair in ((0, got2_ref), (2, got3_ref)):
+            result_ref[first + part] = (
+                down0_ref[first + part].astype(f32)
+                + got1_ref[first + part].astype(f32)
+                + other_pair[part].astype(f32)
+            ).astype(bf16)
+        return 0
+
+    lax.fori_loop(0, 2, result_rows, 0)
     def head_spread(target, index):
         return remote(heads_ref.at[chip], heads_ref.at[chip], hg_send.at[index], hg_recv.at[index], (target, z))
 
@@ -1739,15 +2009,12 @@
 
     for one in along:
         one.wait_recv()
-    whole = chunk[0:24]
     places_z = [z] + zs
-    parts = [chunk[24:32]] + [z_in[d, 24:32].astype(f32) for d in range(3)]
-    for d in range(3):
-        whole += z_in[d, 0:24].astype(f32)
+    parts = [chunk[0:8]] + [z_in[d, 0:8].astype(f32) for d in range(3)]
     by_member = [
         sum((set_ref[places_z[d]] == member).astype(f32) * parts[d] for d in range(4)) for member in range(4)
     ]
-    pool_ref[s] = jnp.concatenate([whole] + by_member + [chunk[32:56]], axis=0).astype(bf16)
+    pool_ref[s] = jnp.concatenate(by_member, axis=0).astype(bf16)
 
     def pool_copy(t, index, target):
         return remote(pool_ref.at[t], pool_ref.at[t], cg_send.at[index], cg_recv.at[index], (target, z))
@@ -1762,12 +2029,14 @@
             head_pass(t, index).wait_recv()
             head_pass(t, 4 + index).start()
 
-    for index, t in enumerate((sx, sy, sd)):
-        pool_copy(t, index, other).wait_recv()
-        pool_copy(t, 4 + index, other).start()
-    pool_copy(other, 3, other).wait_recv()
-    for index, t in enumerate((sx, sy, sd)):
-        pool_copy(flip(t, 1), 4 + index, other).wait_recv()
+    for copy in (sets_copy, pool_copy):
+        for index, t in enumerate((sx, sy, sd)):
+            copy(t, index, other).wait_recv()
+            copy(t, 4 + index, other).start()
+    for copy in (sets_copy, pool_copy):
+        copy(other, 3, other).wait_recv()
+        for index, t in enumerate((sx, sy, sd)):
+            copy(flip(t, 1), 4 + index, other).wait_recv()
 
     @pl.when(z // 2 != core)
     def _():
@@ -1776,11 +2045,17 @@
             head_pass(t, 4 + index).wait_recv()
 
     for d, j in enumerate(zs):
-        remote(own_ref.at[j], grad_ref.at[j], a2a_send.at[d], a2a_recv.at[d], (s, j)).wait_recv()
-    for one in swaps + crosses + around + backs + along + gives + [last_down]:
+        for half in range(2):
+            rows = pl.ds(32 * half, 32)
+            index = 2 * d + half
+            remote(
+                own_ref.at[j, rows], grad_ref.at[j, rows], a2a_send.at[index], a2a_recv.at[index], (s, j)
+            ).wait_recv()
+    for one in swaps + crosses + around + backs + along + gives + sets_along + sets_gives + [last_down]:
         one.wait_send()
     for index, t in enumerate((sx, sy, sd)):
         pool_copy(t, 4 + index, other).wait_send()
+        sets_copy(t, 4 + index, other).wait_send()
     reduce.end()
     for head in range(2):
 
@@ -1807,30 +2082,44 @@
     shape = jax.ShapeDtypeStruct
     return pl.pallas_call(
         finish_kernel,
-        in_specs=[vmem] * 6 + [anywhere] * 2 + [vmem] * 13 + [pl.BlockSpec(memory_space=pltpu.SMEM)],
-        out_specs=[vmem] * 5,
+        in_specs=[vmem] * 3
+        + [anywhere, vmem, anywhere, anywhere, anywhere, vmem, vmem, anywhere]
+        + [vmem] * 3
+        + [anywhere] * 3
+        + [vmem, pl.BlockSpec(memory_space=pltpu.SMEM)],
+        out_specs=[vmem] * 6,
         out_shape=[
             shape((4, 64, width), bf16),
             shape((4, 64, width), bf16),
-            shape((8, 80, width), bf16),
+            shape((8, 48, width), bf16),
+            shape((8, 32, width), bf16),
             shape((4, 256, HDIM), bf16),
-            shape((4, 64, width), bf16),
+            shape((2, 64, width), bf16),
         ],
         scratch_shapes=[
+            vm((width, 1536), bf16),
+            vm((256, width), f32),
+            vm((8, 256, 256), bf16),
+            vm((4, 64, width), bf16),
+            vm((4, 64, width), bf16),
+            vm((2, 64, width), bf16),
             vm((4, 64, width), bf16),
             vm((4, 256, 256), bf16),
             vm((4, 256, 256), bf16),
             vm((4, 256, 256), bf16),
             vm((6, 128, width), bf16),
             vm((6, 128, width), bf16),
+            vm((256, width), f32),
             vm((2, 256, width), bf16),
             vm((2, 256, width), bf16),
             vm((48, width), f32),
             vm((16, width), f32),
-            vm((8, 64, width), bf16),
-            vm((4, 64, width), bf16),
-            vm((4, 64, width), bf16),
-            vm((3, 64, width), bf16),
+            vm((8, 16, width), bf16),
+            vm((4, 16, width), bf16),
+            vm((4, 16, width), bf16),
+            vm((3, 16, width), bf16),
+            vm((16, width), bf16),
+            vm((3, 16, width), bf16),
             vm((32, width), bf16),
             vm((3, 32, width), bf16),
             vm((2, 64, HDIM), bf16),
@@ -1838,7 +2127,7 @@
         ]
         + [
             dma((count,))
-            for count in (3, 3, 12, 12, 6, 6, 4, 4, 4, 3, 3, 3, 3, 7, 7, 2, 4, 7, 7, 1, 1)
+            for count in (6, 6, 12, 12, 6, 6, 4, 4, 4, 3, 3, 3, 3, 7, 7, 2, 4, 7, 7, 1, 1, 3, 3, 7, 7, 6)
         ],
         cost_estimate=spend(80),
         compiler_params=pltpu.CompilerParams(
@@ -1884,21 +2173,19 @@
     ) = mlp_line(
         m_own, residual, cots, w_gate_up, w_down, a_in, b_gate_up, a_down, b_out_down, set_index
     )
-    g, grad_mixed, dots, out_rank, got1, got2 = spread_layer(
-        g_own, o_eff, spans(mixed), b_out_down, down1, down2, set_index
-    )
-    dq, dk, dv = attend_back(
-        q, k, v, grad_mixed.reshape(length, -1), lse.reshape(2, 1, length), dots.reshape(2, 1, length),
-        tables.reshape(length, HDIM),
-    )
-    result, grad_in, pool, heads, _ = finish_layer(
+    dq, dk, dv, out_rank, chunk, pair, g, got1, got2 = back_layer(
+        g_own, o_eff, mixed, b_out_down, q, k, v, lse, tables.reshape(length, HDIM),
+        grad_b_mlp, grad_ad, grad_a_mlp, grad_bd, down1, down2, down3, set_index,
+    )
+    result, grad_in, pooled, pool, heads, _ = finish_layer(
         spans(dq), spans(dk), spans(dv), w_cat, x_own, grad_residual, u, g, low, out_rank, spans(mixed),
-        b_sel, a_sel, grad_b_mlp, grad_ad, grad_a_mlp, grad_bd, down0, got1, got2, down3, set_index,
-    )
-    pool = pool.astype(f32)
-    whole = pool[:, 0:24].reshape(sets, 48, width)
-    sequence = jnp.transpose(pool[:, 24:56].reshape(8, sets, 8, width), (1, 0, 2, 3)).reshape(sets, 64, width)
-    split = pool[:, 56:80].reshape(sets, 48, width)
+        b_sel, a_sel, chunk, down0, got1, got2, pair, set_index,
+    )
+    pooled = pooled.astype(f32)
+    whole = pooled[:, 0:24].reshape(sets, 48, width)
+    split = pooled[:, 24:48].reshape(sets, 48, width)
+    pool = pool.astype(f32).reshape(8, sets, 8, width)
+    sequence = jnp.transpose(pool, (1, 0, 2, 3)).reshape(sets, 64, width)
     heads = heads.astype(f32).reshape(4, sets, 64, HDIM)
     heads = jnp.transpose(heads, (1, 2, 0, 3)).reshape(sets, 4, rank, 4 * HDIM)
     return (

time: 551 us -> 500 us (0.907); the launches traced: 541 us -> 497 us
  Pallas kernels: 520 us -> 477 us
    pallas_call x3 -> x2, Pallas kernels: 192 us -> 153 us  [the longest x1 82.5 us: finish_layer(): pl.pallas_call(finish_kernel, in_specs=[vmem] * 3 + [anywhere, vmem, anyw...]
where the time goes in v4:
time: 500 us; the launch traced here: 497 us
  Pallas kernels  477 us (95%)
  local copies, waits for them, and re-layouts  13.7 us (3%)
    pallas_call x1, Pallas kernels, front_layer(): pl.pallas_call(front_kernel, in_specs=[vmem] + [anywhere] * 4 + [vmem] *...  184 us
    pallas_call x1, Pallas kernels, mlp_line(): pl.pallas_call(mlp_line_kernel, in_specs=[vmem, vmem] + [anywhere] * 3 +...  140 us
    pallas_call x1, Pallas kernels, finish_layer(): pl.pallas_call(finish_kernel, in_specs=[vmem] * 3 + [anywhere, vmem, anyw...  82.5 us
    pallas_call x1, Pallas kernels, back_layer(): pl.pallas_call(back_kernel, in_specs=[vmem, vmem, anywhere, vmem, anywher...  70.6 us

profile of v4, /device:TPU:13, one launch (start us, length us, event | category | flops | bytes accessed | tf_op | source)
XLA Modules:
  0.0 496.6 jit_solution(13147449239137633816)
XLA Ops:
  0.6 0.7 dynamic-slice_convert_fusion
  1.3 0.5 multiply_cosine_fusion
  1.9 0.8 pad_maximum_fusion.2.table_ref
  2.6 184.2 %shard_map.197 = (bf16[4,64,2048]{2,1,0:T(8,128)(2,1)}, bf16[256,2048]{1,0:T(8,128)(2,1)}, f32[256,2048]{1,0:T(8,128)}, bf16[256,2048]{1,0:T(8,128)(2,1)}, bf16[...) custom-call(bf16[4,64,2048]{2,1,0:T(8,128)(2,1)} %x_ref.1, ...), custom_call_target="tpu_custom_call" | custom-call | flops 149999992832 | bytes 1000000 | tf_op jit(solution)/shard_map/pallas_call | solution.py:1078
  186.9 0.0 copy-start
  186.9 0.0 copy-start.5
  186.9 139.7 %shard_map.198 = (bf16[256,2048]{1,0:T(8,128)(2,1)}, f32[256,2048]{1,0:T(8,128)}, bf16[4,64,2048]{2,1,0:T(8,128)(2,1)}, bf16[4,64,2048]{2,1,0:T(8,128)(2,1)}, bf...) custom-call(bf16[256,2048]{1,0:T(8,128)(2,1)} %get-tuple-element.48., ...), custom_call_target="tpu_custom_call" | custom-call | flops 109999996928 | bytes 1000000 | tf_op jit(solution)/shard_map/pallas_call | solution.py:1706
  326.6 0.0 copy-done
  326.6 0.0 copy-done.5
  326.6 70.6 %shard_map.199 = (bf16[2048,256]{1,0:T(8,128)(2,1)}, bf16[2048,256]{1,0:T(8,128)(2,1)}, bf16[2048,256]{1,0:T(8,128)(2,1)}, bf16[8,256,16]{2,1,0:T(8,128)(2,1)S(1...) custom-call(bf16[256,2048]{1,0:T(8,128)(2,1)} %get-tuple-element.51., ...), custom_call_target="tpu_custom_call" | custom-call | flops 60000002048 | bytes 1000000 | tf_op jit(solution)/shard_map/pallas_call | solution.py:1342
  397.3 0.0 copy-start.1
  397.3 0.8 copy-done.1
  398.1 0.0 copy-start.2
  398.1 0.8 copy-done.2
  398.9 0.0 copy-start.3
  398.9 0.8 copy-done.3
  399.7 0.0 copy-start.4
  399.7 0.7 copy-done.4
  400.4 82.5 %shard_map.200 = (bf16[4,64,2048]{2,1,0:T(8,128)(2,1)}, bf16[4,64,2048]{2,1,0:T(8,128)(2,1)}, bf16[8,48,2048]{2,1,0:T(8,128)(2,1)}, bf16[8,32,2048]{2,1,0:T(8,12...) custom-call(bf16[8,256,256]{2,1,0:T(8,128)(2,1)} %bitcast.41, bf16[8,256,256]{2,1,0:T(8,128)(2,1)} %bitcast.42, ...), custom_call_target="tpu_custom_call" | custom-call | flops 80000000000 | bytes 1000000 | tf_op jit(solution)/shard_map/pallas_call | solution.py:2083
  482.9 0.0 copy-start.8
  483.0 1.2 copy.28
  484.2 0.2 reshape.92
  484.4 0.7 slice_bitcast_fusion.2
  485.1 0.8 slice.43
  485.9 0.0 copy-done.8
  485.9 0.2 copy_bitcast_fusion
  486.1 0.0 copy-start.6
  486.1 0.0 copy-start.7
  486.1 2.2 copy-done.7
  488.3 0.2 fusion
  488.5 0.0 copy-done.6
  488.5 0.1 slice_bitcast_fusion
  488.6 0.0 slice-start
  488.6 0.1 slice.42
  488.7 1.3 slice-done
  490.0 1.7 pad_maximum_fusion
  491.7 1.0 pad_maximum_fusion.1
  492.7 0.0 copy-start.10
  492.7 0.8 slice.47
  493.6 0.0 copy-start.9
  493.6 1.0 slice.45
  494.6 0.0 copy-done.10
  494.6 1.0 copy.31
  495.6 0.0 copy-done.9
  495.6 1.0 copy.32
  (1 shorter events, 0.0 us)
Async XLA Ops:
  186.9 139.7 %copy-start = (s32[4]{0:T(128)S(1)}, s32[4]{0:T(128)}, u32[]{:S(2)}) copy-start(s32[4]{0:T(128)} %set_ref.7) | copy-start | bytes 52
  186.9 139.7 %copy-start.5 = (f32[2,4,1,512]{3,2,1,0:T(1,128)S(1)}, f32[2,4,1,512]{3,2,1,0:T(1,128)}, u32[]{:S(2)}) copy-start(f32[2,4,1,512]{3,2,1,0:T(1,128)} %get-tuple-element.57.lse_ref) | copy-start | bytes 49156
  397.3 0.8 copy-start.1
  398.1 0.8 copy-start.2
  398.9 0.8 copy-start.3
  399.7 0.7 copy-start.4
  482.9 2.9 copy-start.8
  486.1 2.4 copy-start.6
  486.1 2.2 copy-start.7
  488.6 1.4 slice-start
  492.7 1.9 copy-start.10
  493.6 2.0 copy-start.9

commit v5 on v4

--- a/solution.py
+++ b/solution.py
@@ -608,6 +608,20 @@
     def hop(self, t):
         z = self.z
 
+        def from_above(side):
+            @pl.when((z + t <= 3) & side)
+            def _():
+                self.down(t - 1, z + t).wait_recv()
+                if self.core is not None:
+                    self.across(3 + t, z + t).start()
+                if t < 3:
+
+                    @pl.when(z > 0)
+                    def _():
+                        self.down(t, z + t).start()
+
+        from_above(z < 2)
+
         @pl.when(z >= t)
         def _():
             self.up(t - 1, z - t).wait_recv()
@@ -619,16 +633,7 @@
                 def _():
                     self.up(t, z - t).start()
 
-        @pl.when(z + t <= 3)
-        def _():
-            self.down(t - 1, z + t).wait_recv()
-            if self.core is not None:
-                self.across(3 + t, z + t).start()
-            if t < 3:
-
-                @pl.when(z > 0)
-                def _():
-                    self.down(t, z + t).start()
+        from_above(z >= 2)
 
     def arrive_core(self):
         z = self.z
@@ -801,6 +806,7 @@
     chip = s // 2
     other = flip(s, 1)
     zs = [flip(z, 1), flip(z, 2), 3 - z]
+    middle = z * (3 - z) == 2
     columns = pl.ds(pl.multiple_of(chip * HDIM, HDIM), HDIM)
     half_rows = pl.ds(pl.multiple_of(core * 1024, 1024), 1024)
     owns = [
@@ -820,6 +826,10 @@
     ]
     for one in swaps:
         one.start()
+    for one in owns:
+        one.wait()
+    line = Line(w_buf, core, s, z, w_send, w_recv)
+    line.begin()
     table_gather = Gather(tables, s, z, tab_send, tab_recv, 128)
     table_gather.begin()
     x_own_ref[z] = x_ref[z]
@@ -844,13 +854,9 @@
     near.begin()
     table_gather.arrive_first()
     table_gather.arrive_neighbours()
-    for one in owns:
-        one.wait()
     near.arrive_first()
     arrived(1)
     arrived(2)
-    line = Line(w_buf, core, s, z, w_send, w_recv)
-    line.begin()
     smalls = []
     for d, j in enumerate(zs):
         smalls.append(remote(b_small.at[z], b_small.at[z], small_send.at[d], small_recv.at[d], (s, j)))
@@ -863,8 +869,8 @@
     table_gather.arrive_diagonal()
     near.arrive_neighbours()
     near.arrive_diagonal()
+    line.hop(1)
     rest.arrive_first()
-    line.hop(1)
     rest.arrive_neighbours()
     rest.arrive_diagonal()
     for index in range(4):
@@ -937,8 +943,8 @@
 
         return 0
 
+    cot_line.begin()
     lax.fori_loop(0, 8, project_all, 0)
-    cot_line.begin()
     stores += [
         pltpu.make_async_copy(source, target, store_sem.at[1 + i])
         for i, (source, target) in enumerate(
@@ -989,6 +995,10 @@
         def _():
             o_line.hop(3)
 
+        @pl.when((index == 5) & middle)
+        def _():
+            cot_line.hop(1)
+
         return 0
 
     lax.fori_loop(0, 8, attend_all, 0)
@@ -1035,8 +1045,12 @@
     )
     reduce.begin()
     reduce.keep()
-    cot_line.hop(1)
     reduce.second()
+
+    @pl.when(middle)
+    def _():
+        cot_line.hop(2)
+
     lax.fori_loop(6, 12, merge, 0)
     stores.append(pltpu.make_async_copy(w_cat, w_cat_out, store_sem.at[7]))
     stores[-1].start()
@@ -1050,9 +1064,12 @@
         m_own_ref[at, :] = normed.astype(bf16)
 
     reduce.finish(0, settle)
-    cot_line.hop(2)
     reduce.finish(1, settle)
-    cot_line.hop(3)
+    @pl.when(z * (3 - z) == 0)
+    def _():
+        for t in (1, 2, 3):
+            cot_line.hop(t)
+
     for one in stores:
         one.wait()
     for one in swaps + smalls + crosses:
@@ -1136,10 +1153,10 @@
 
 
 def back_kernel(
-    g_ref, o_eff_ref, mixed_in, b_od_ref, q_in, k_in, v_in, lse_ref, table_in,
-    grad_b_ref, grad_ad_ref, grad_a_ref, grad_bd_ref, down1_ref, down2_ref, down3_ref, set_ref,
-    dq_ref, dk_ref, dv_ref, rank_ref, chunk_ref, pair_ref, g_out, got1_ref, got2_ref,
-    mixed_ref, q_ref, k_ref, v_ref, table_ref, down2_buf, got3_buf, pair_sum, g_buf, gm_buf, dots, dk_acc, dv_acc, chunk_src, chunk_sib, chunk_sum, chunk_in,
+    g_ref, o_eff_in, mixed_in, b_od_ref, q_in, k_in, v_in, lse_ref, table_in,
+    grad_b_in, grad_ad_in, grad_a_in, grad_bd_in, down2_ref, down3_ref, set_ref,
+    dq_ref, dk_ref, dv_ref, rank_ref, chunk_ref, pair_ref, g_out, got2_ref,
+    grad_b_ref, grad_ad_ref, grad_a_ref, grad_bd_ref, o_eff_ref, mixed_ref, q_ref, k_ref, v_ref, table_ref, down2_buf, got3_buf, pair_sum, g_buf, gm_buf, dots, dk_acc, dv_acc, chunk_src, chunk_sib, chunk_sum, chunk_in,
     send, recv, down_send, down_recv, cs_send, cs_recv, cx_send, cx_recv, store_sem, load_sem,
 ):
     f32 = jnp.float32
@@ -1149,6 +1166,11 @@
         pltpu.make_async_copy(source, target, load_sem.at[i])
         for i, (source, target) in enumerate(
             (
+                (grad_b_in, grad_b_ref),
+                (grad_ad_in, grad_ad_ref),
+                (grad_a_in, grad_a_ref),
+                (grad_bd_in, grad_bd_ref),
+                (o_eff_in, o_eff_ref),
                 (mixed_in, mixed_ref),
                 (q_in, q_ref),
                 (k_in, k_ref),
@@ -1170,13 +1192,9 @@
     g_buf[s] = g_ref[...]
     gather = Gather(g_buf, s, z, send, recv, 128)
     gather.begin()
-    results = [
-        remote(down3_ref, got3_buf, down_send.at[0], down_recv.at[0], (s, flip(z, 1))),
-        remote(down1_ref, got1_ref, down_send.at[1], down_recv.at[1], (s, flip(z, 1))),
-    ]
-    for one in results:
-        one.start()
-    onward = remote(pair_sum, got2_ref, down_send.at[2], down_recv.at[2], (s, flip(z, 2)))
+    across = remote(down3_ref, got3_buf, down_send.at[0], down_recv.at[0], (s, flip(z, 1)))
+    across.start()
+    onward = remote(pair_sum, got2_ref, down_send.at[1], down_recv.at[1], (s, flip(z, 2)))
     member = set_ref[z]
     tile = attn_tile
     scale = 1.0 / math.sqrt(HDIM)
@@ -1246,6 +1264,8 @@
             chunk_src[2 * one + part] = jnp.concatenate([whole[rows], split[rows]], axis=0).astype(bf16)
         return 0
 
+    for one in loads[:4]:
+        one.wait()
     lax.fori_loop(0, 4, fill, 0)
     crosses = [
         remote(chunk_src.at[2 * c + 1 - core], chunk_sib.at[c], cs_send.at[c], cs_recv.at[c], (other, z))
@@ -1253,7 +1273,7 @@
     ]
     for one in crosses:
         one.start()
-    for one in loads:
+    for one in loads[4:]:
         one.wait()
     around = [
         remote(chunk_sum.at[t // 2], chunk_in.at[d], cx_send.at[d], cx_recv.at[d], (t, z))
@@ -1285,7 +1305,7 @@
             for one in around:
                 one.start()
             gather.arrive_neighbours()
-            results[0].wait_recv()
+            across.wait_recv()
             lax.fori_loop(0, 2, pair_rows, 0)
             onward.start()
             gather.arrive_core(1)
@@ -1324,9 +1344,8 @@
     for t in range(8):
         store(t).wait()
     gather.end()
-    results[1].wait_recv()
     onward.wait()
-    for one in crosses + around + results:
+    for one in crosses + around + [across]:
         one.wait_send()
 
 
@@ -1341,11 +1360,10 @@
     vm = pltpu.VMEM
     return pl.pallas_call(
         back_kernel,
-        in_specs=[vmem, vmem, anywhere, vmem, anywhere, anywhere, anywhere, vmem, anywhere]
-        + [vmem] * 4
-        + [anywhere] * 3
+        in_specs=[vmem, anywhere, anywhere, vmem, anywhere, anywhere, anywhere, vmem, anywhere]
+        + [anywhere] * 6
         + [pl.BlockSpec(memory_space=pltpu.SMEM)],
-        out_specs=[vmem] * 6 + [anywhere] * 3,
+        out_specs=[vmem] * 6 + [anywhere] * 2,
         out_shape=[
             shape((2048, 256), bf16),
             shape((2048, 256), bf16),
@@ -1354,10 +1372,11 @@
             shape((48, width), f32),
             shape((2, 64, width), bf16),
             shape((8, 256, width), bf16),
-            shape((4, 64, width), bf16),
             shape((2, 64, width), bf16),
         ],
-        scratch_shapes=[
+        scratch_shapes=[vm(operands[i].shape, f32) for i in (9, 10, 11, 12)]
+        + [
+            vm((256, width), bf16),
             vm((2048, 256), bf16),
             vm((2048, 256), bf16),
             vm((2048, 256), bf16),
@@ -1376,22 +1395,36 @@
             vm((4, 48, width), bf16),
             vm((3, 48, width), bf16),
         ]
-        + [dma((count,)) for count in (gather_sems, gather_sems, 3, 3, 4, 4, 3, 3, 8, 6)],
+        + [dma((count,)) for count in (gather_sems, gather_sems, 2, 2, 4, 4, 3, 3, 8, 11)],
         cost_estimate=spend(60),
         compiler_params=pltpu.CompilerParams(
-            collective_id=3, has_side_effects=True, vmem_limit_bytes=52 << 20
+            collective_id=3, has_side_effects=True, vmem_limit_bytes=60 << 20
         ),
     )(*operands)
 
 
 def mlp_line_kernel(
-    m_ref, residual_ref, cots_ref, w_gu_ref, w_d_ref, a_ref, b_ref, ad_ref, bd_ref, set_ref,
+    m_ref, residual_in, cots_ref, w_gu_ref, w_d_ref, a_in, b_in, ad_in, bd_in, set_ref,
     g_ref, grad_res_ref, down0_ref, down1_ref, down2_ref, down3_ref, grad_b_ref, grad_ad_ref, grad_a_ref, grad_bd_ref,
-    m_buf, wg, wu, wd, cot_buf, back_acc, down_acc, ranks, slots, r1, r2, r3, r4, r5, stage,
+    residual_ref, a_ref, b_ref, ad_ref, bd_ref, m_buf, wg, wu, wd, acts, grad_gates, grad_ups, cot_buf, back_acc, ranks, slots, r1, r2, r3, r5, stage,
     up_send, up_recv, dn_send, dn_recv, send1, recv1, send4, recv4, send5, recv5, send23, recv23,
-    weight_sem, cot_sem, stage_sem,
+    weight_sem, cot_sem, stage_sem, late_sem,
 ):
     s, z = places()
+    late = [
+        pltpu.make_async_copy(source, target, late_sem.at[i])
+        for i, (source, target) in enumerate(
+            (
+                (a_in, a_ref),
+                (b_in, b_ref),
+                (ad_in, ad_ref),
+                (bd_in, bd_ref),
+                (residual_in, residual_ref),
+            )
+        )
+    ]
+    for one in late:
+        one.start()
     tiles = wg.shape[0]
     tile = wg.shape[2]
     f32 = jnp.float32
@@ -1445,6 +1478,18 @@
             down(0, z).start()
 
     def hop(t):
+        def from_above(side):
+            @pl.when((z + t <= 3) & side)
+            def _():
+                down(t - 1, z + t).wait_recv()
+                if t < 3:
+
+                    @pl.when(z > 0)
+                    def _():
+                        down(t, z + t).start()
+
+        from_above(z < 2)
+
         @pl.when(z >= t)
         def _():
             up(t - 1, z - t).wait_recv()
@@ -1454,14 +1499,7 @@
                 def _():
                     up(t, z - t).start()
 
-        @pl.when(z + t <= 3)
-        def _():
-            down(t - 1, z + t).wait_recv()
-            if t < 3:
-
-                @pl.when(z > 0)
-                def _():
-                    down(t, z + t).start()
+        from_above(z >= 2)
 
     def hop_end():
         @pl.when(z < 3)
@@ -1495,7 +1533,7 @@
         return remote(slots.at[2], r3, send23.at[1], recv23.at[1], (s, inner))
 
     def copy4(p):
-        return remote(slots.at[3, piece(p)], r4.at[piece(p)], send4.at[p], recv4.at[p], (s, far))
+        return remote(slots.at[3, piece(p)], r3.at[piece(p)], send4.at[p], recv4.at[p], (s, far))
 
     def copy5(p):
         return remote(slots.at[3, piece(p)], r5.at[piece(p)], send5.at[p], recv5.at[p], (s, inner))
@@ -1521,6 +1559,8 @@
         lax.fori_loop(0, 4, one, 0)
 
     begin()
+    for one in late:
+        one.wait()
 
     def chunk(slot, _):
         seq = sequence(slot)
@@ -1531,7 +1571,6 @@
         ranks[:, 32:48] = adapt_scale * dot_nt(cot_buf[...].reshape(256, -1), bd_ref[member, 1])
         ranks[:, 48:96] = jnp.zeros((256, 48), f32)
         back_acc[...] = jnp.zeros_like(back_acc)
-        down_acc[...] = jnp.zeros_like(down_acc)
 
         def step(h, _):
             columns = pl.ds(pl.multiple_of(h * tile, tile), tile)
@@ -1561,22 +1600,33 @@
             act = (gate * sig * up_value).astype(bf16)
             grad_up = (grad_act * gate * sig).astype(bf16)
             grad_gate = (grad_act * up_value * sig * (1.0 + gate * (1.0 - sig))).astype(bf16)
+            acts[h] = act
+            grad_gates[h] = grad_gate
+            grad_ups[h] = grad_up
             for part in range(4):
                 wide = pl.ds(part * 512, 512)
                 back_acc[:, wide] += dot_nt(grad_gate, wg[h, wide, :]) + dot_nt(grad_up, wu[h, wide, :])
-                down_acc[:, wide] += dot_nn(act, wd[h, :, wide])
-            ranks[:, 48:64] += dot_nt(act, ad)
             ranks[:, 64:80] += dot_nt(grad_gate, bg)
             ranks[:, 80:96] += dot_nt(grad_up, bu)
-            grad_b_ref[seq, 0, :, columns] = dot_tn(low_gate, grad_gate)
-            grad_b_ref[seq, 1, :, columns] = dot_tn(low_up, grad_up)
-            grad_ad_ref[seq, :, columns] = dot_tn(low_cot, act)
             return 0
 
+        def later(h, _):
+            columns = pl.ds(pl.multiple_of(h * tile, tile), tile)
+            low = ranks[:, 0:48].astype(bf16)
+            act = acts[h]
+            for part in range(4):
+                wide = pl.ds(part * 512, 512)
+                back_acc[:, wide] += dot_nn(act, wd[h, :, wide])
+            ranks[:, 48:64] += dot_nt(act, ad_ref[member, :, columns])
+            grad_b_ref[seq, 0, :, columns] = dot_tn(low[:, 0:16], grad_gates[h])
+            grad_b_ref[seq, 1, :, columns] = dot_tn(low[:, 16:32], grad_ups[h])
+            grad_ad_ref[seq, :, columns] = dot_tn(low[:, 32:48], act)
+            return 0
+
         lax.fori_loop(0, tiles, step, 0)
-        for t in (1, 2, 3):
-
-            @pl.when(slot == t - 1)
+        for t in (1, 2):
+
+            @pl.when((slot == t - 1) & middle)
             def _():
                 hop(t)
 
@@ -1602,6 +1652,8 @@
             add(2, r3)
             copy2().start()
 
+        back_acc[...] = jnp.zeros_like(back_acc)
+        lax.fori_loop(0, tiles, later, 0)
         low_down = (adapt_scale * ranks[:, 48:64]).astype(bf16)
         grad_a_ref[seq] = dot_tn(back_rank, m_buf[seq])
         grad_bd_ref[seq] = dot_tn(low_down, cot_buf[...].reshape(256, -1))
@@ -1612,12 +1664,18 @@
                 one.wait()
 
         own = (slot == 0).astype(f32)
-        value = down_acc[...] + dot_nn(low_down, bd_ref[member, 1]) + own * residual_ref[...]
+        value = back_acc[...] + dot_nn(low_down, bd_ref[member, 1]) + own * residual_ref[...]
         stage[...] = value.astype(bf16).reshape(4, 64, -1)
         for one in stage_copies(seq):
             one.start()
         for one in load_cot(sequence(slot + 1)):
             one.start()
+        for t in (1, 2, 3):
+
+            @pl.when((slot == t - 1) & at_end)
+            def _():
+                hop(t)
+
         return 0
 
     lax.fori_loop(0, 4, chunk, 0)
@@ -1656,7 +1714,7 @@
         def _():
             copy4(p).wait_recv()
             slots[0, piece(p), :] = (
-                slots[0, piece(p), :].astype(f32) + r4[piece(p), :].astype(f32)
+                slots[0, piece(p), :].astype(f32) + r3[piece(p), :].astype(f32)
             ).astype(bf16)
 
         def rows32(half, _):
@@ -1705,9 +1763,8 @@
     vm = pltpu.VMEM
     return pl.pallas_call(
         mlp_line_kernel,
-        in_specs=[vmem, vmem]
-        + [anywhere] * 3
-        + [vmem] * 4
+        in_specs=[vmem]
+        + [anywhere] * 8
         + [pl.BlockSpec(memory_space=pltpu.SMEM)],
         out_specs=[vmem, vmem] + [anywhere] * 4 + [vmem, vmem, vmem, vmem],
         out_shape=[
@@ -1722,16 +1779,22 @@
             shape((4, 16, width), f32),
         ],
         scratch_shapes=[
+            vm((256, width), f32),
+            vm(a_in.shape, bf16),
+            vm(b_gate_up.shape, bf16),
+            vm(a_down.shape, bf16),
+            vm(b_out_down.shape, bf16),
             vm((4, 256, width), bf16),
             vm((tiles, width, tile), bf16),
             vm((tiles, width, tile), bf16),
             vm((tiles, tile, width), bf16),
+            vm((tiles, 256, tile), bf16),
+            vm((tiles, 256, tile), bf16),
+            vm((tiles, 256, tile), bf16),
             vm((4, 64, width), bf16),
-            vm((256, width), f32),
             vm((256, width), f32),
             vm((256, 96), f32),
             vm((4, 256, width), bf16),
-            vm((256, width), bf16),
             vm((256, width), bf16),
             vm((256, width), bf16),
             vm((256, width), bf16),
@@ -1741,7 +1804,7 @@
         + [dma((3,))] * 4
         + [dma((4,))] * 6
         + [dma((2,))] * 2
-        + [dma((3 * tiles,)), dma((4,)), dma((4,))],
+        + [dma((3 * tiles,)), dma((4,)), dma((4,)), dma((5,))],
         cost_estimate=spend(110),
         compiler_params=pltpu.CompilerParams(
             collective_id=5, has_side_effects=True, vmem_limit_bytes=60 << 20
@@ -1750,11 +1813,12 @@
 
 
 def finish_kernel(
-    dq_ref, dk_ref, dv_ref, w_in, x_own_ref, residual_in, u_ref, g_ref, low_ref, rank_ref, mixed_in,
-    b_sel_ref, a_sel_ref, chunk_ref, down0_in, got1_in, got2_in, pair_ref,
+    dq_in, dk_in, dv_in, w_in, x_own_in, residual_in, u_ref, g_ref, low_in, rank_ref, mixed_in,
+    b_sel_ref, a_sel_ref, chunk_ref, down0_in, down1_ref, got2_ref, pair_ref,
     set_ref,
-    result_ref, grad_ref, sets_ref, pool_ref, heads_ref, got3_ref,
-    w_ref, residual_ref, mixed_ref, down0_ref, got1_ref, got2_ref,
+    result_ref, grad_ref, whole_ref, split_ref, sequence_ref, heads_ref, got3_ref,
+    sets_ref, pool_ref, dq_ref, dk_ref, dv_ref, x_own_ref, low_ref,
+    w_ref, residual_ref, mixed_ref, down0_ref, got1_ref,
     own_ref, sib_q, sib_k, sib_v, out_buf, in_buf, own_sum, u_buf, g_buf, a_acc, b_acc, chunk_src, chunk_sib, chunk_sum,
     chunk_in, z_src, z_in, sets_src, sets_in, head_src, head_in,
     a2a_send, a2a_recv, sib_send, sib_recv, send, recv, load_sem, cs_send, cs_recv, cx_send, cx_recv,
@@ -1768,16 +1832,19 @@
         pltpu.make_async_copy(source, target, late_sem.at[i])
         for i, (source, target) in enumerate(
             (
+                (dq_in, dq_ref),
+                (dk_in, dk_ref),
+                (dv_in, dv_ref),
                 (w_in, w_ref),
                 (mixed_in, mixed_ref),
+                (low_in, low_ref),
+                (x_own_in, x_own_ref),
                 (residual_in, residual_ref),
                 (down0_in, down0_ref),
-                (got1_in, got1_ref),
-                (got2_in, got2_ref),
             )
         )
     ]
-    for one in loads[:2]:
+    for one in loads[:5]:
         one.start()
     core = s % 2
     chip = s // 2
@@ -1789,15 +1856,18 @@
     meet([(None, (t, z)) for t in (other, sx, sy, sd)] + [(None, (s, j)) for j in zs])
     last_down = remote(pair_ref, got3_ref, down_send.at[0], down_recv.at[0], (s, flip(z, 2)))
     last_down.start()
+    pair_down = remote(down1_ref, got1_ref, down_send.at[1], down_recv.at[1], (s, zs[0]))
+    pair_down.start()
     sets_src[...] = chunk_ref[0:32].astype(bf16)
     sets_along = [remote(sets_src, sets_in.at[d], sz_send.at[d], sz_recv.at[d], (s, j)) for d, j in enumerate(zs)]
     for one in sets_along:
         one.start()
     mine = (dq_ref, dk_ref, dv_ref)
+    sources = (dq_in, dk_in, dv_in)
     theirs = (sib_q, sib_k, sib_v)
     swaps = [
         remote(
-            mine[p].at[2 * c + 1 - core], theirs[p].at[c], sib_send.at[4 * p + c], sib_recv.at[4 * p + c], (other, z)
+            sources[p].at[2 * c + 1 - core], theirs[p].at[c], sib_send.at[4 * p + c], sib_recv.at[4 * p + c], (other, z)
         )
         for c in range(4)
         for p in range(3)
@@ -1829,12 +1899,13 @@
         rows_of, lambda rows, wide: dot_nt(rows, w_ref[wide, :]), x_own_ref.shape[2], s, z,
         out_buf, in_buf, own_sum, send, recv,
     )
-    loads[0].wait()
+    for one in loads[:4]:
+        one.wait()
     reduce.begin()
-    for one in loads[2:]:
+    for one in loads[5:]:
         one.start()
     reduce.keep()
-    loads[1].wait()
+    loads[4].wait()
 
     b_two = [
         jnp.concatenate(
@@ -1881,6 +1952,8 @@
         return 0
 
     lax.fori_loop(0, 8, adapt, 0)
+    for one in loads[5:]:
+        one.wait()
     per_head = [
         dot_tn(low_ref[...].reshape(2048, 48)[:, 16 * p : 16 * p + 16], mine[p][...].reshape(2048, 256))
         for p in range(3)
@@ -1931,8 +2004,6 @@
         whole += sets_in[d, 0:24].astype(f32)
     sets_ref[s] = jnp.concatenate([whole, chunk_ref[24:48]], axis=0).astype(bf16)
 
-    for one in loads[2:]:
-        one.wait()
     def settle(row, total):
         at = pl.ds(row, 32)
         inside = pl.ds(pl.multiple_of(row % 64, 32), 32)
@@ -1973,6 +2044,7 @@
         one.start()
 
     last_down.wait_recv()
+    pair_down.wait_recv()
 
     def result_rows(part, _):
         for first, other_pair in ((0, got2_ref), (2, got3_ref)):
@@ -2038,6 +2110,17 @@
         for index, t in enumerate((sx, sy, sd)):
             copy(flip(t, 1), 4 + index, other).wait_recv()
 
+    def widen(t, _):
+        rows = sets_ref[t].astype(f32)
+        whole_ref[t] = rows[0:24]
+        split_ref[t] = rows[24:48]
+        rows = pool_ref[t].astype(f32)
+        for member in range(4):
+            sequence_ref[member, pl.ds(pl.multiple_of(8 * t, 8), 8), :] = rows[8 * member : 8 * member + 8]
+        return 0
+
+    lax.fori_loop(0, 8, widen, 0)
+
     @pl.when(z // 2 != core)
     def _():
         head_spread(other, 3).wait_recv()
@@ -2051,7 +2134,7 @@
             remote(
                 own_ref.at[j, rows], grad_ref.at[j, rows], a2a_send.at[index], a2a_recv.at[index], (s, j)
             ).wait_recv()
-    for one in swaps + crosses + around + backs + along + gives + sets_along + sets_gives + [last_down]:
+    for one in swaps + crosses + around + backs + along + gives + sets_along + sets_gives + [last_down, pair_down]:
         one.wait_send()
     for index, t in enumerate((sx, sy, sd)):
         pool_copy(t, 4 + index, other).wait_send()
@@ -2082,27 +2165,35 @@
     shape = jax.ShapeDtypeStruct
     return pl.pallas_call(
         finish_kernel,
-        in_specs=[vmem] * 3
-        + [anywhere, vmem, anywhere, anywhere, anywhere, vmem, vmem, anywhere]
+        in_specs=[anywhere] * 9
+        + [vmem, anywhere]
         + [vmem] * 3
-        + [anywhere] * 3
-        + [vmem, pl.BlockSpec(memory_space=pltpu.SMEM)],
-        out_specs=[vmem] * 6,
+        + [anywhere] * 2
+        + [vmem] * 2
+        + [pl.BlockSpec(memory_space=pltpu.SMEM)],
+        out_specs=[vmem] * 7,
         out_shape=[
             shape((4, 64, width), bf16),
             shape((4, 64, width), bf16),
-            shape((8, 48, width), bf16),
-            shape((8, 32, width), bf16),
+            shape((8, 24, width), f32),
+            shape((8, 24, width), f32),
+            shape((4, 64, width), f32),
             shape((4, 256, HDIM), bf16),
             shape((2, 64, width), bf16),
         ],
         scratch_shapes=[
+            vm((8, 48, width), bf16),
+            vm((8, 32, width), bf16),
+            vm((8, 256, 256), bf16),
+            vm((8, 256, 256), bf16),
+            vm((8, 256, 256), bf16),
+            vm((4, 64, width), bf16),
+            vm((8, 256, 48), bf16),
             vm((width, 1536), bf16),
             vm((256, width), f32),
             vm((8, 256, 256), bf16),
             vm((4, 64, width), bf16),
             vm((4, 64, width), bf16),
-            vm((2, 64, width), bf16),
             vm((4, 64, width), bf16),
             vm((4, 256, 256), bf16),
             vm((4, 256, 256), bf16),
@@ -2127,11 +2218,11 @@
         ]
         + [
             dma((count,))
-            for count in (6, 6, 12, 12, 6, 6, 4, 4, 4, 3, 3, 3, 3, 7, 7, 2, 4, 7, 7, 1, 1, 3, 3, 7, 7, 6)
+            for count in (6, 6, 12, 12, 6, 6, 4, 4, 4, 3, 3, 3, 3, 7, 7, 2, 4, 7, 7, 2, 2, 3, 3, 7, 7, 9)
         ],
         cost_estimate=spend(80),
         compiler_params=pltpu.CompilerParams(
-            collective_id=4, has_side_effects=True, vmem_limit_bytes=58 << 20
+            collective_id=4, has_side_effects=True, vmem_limit_bytes=60 << 20
         ),
     )(*operands)
 
@@ -2173,19 +2264,16 @@
     ) = mlp_line(
         m_own, residual, cots, w_gate_up, w_down, a_in, b_gate_up, a_down, b_out_down, set_index
     )
-    dq, dk, dv, out_rank, chunk, pair, g, got1, got2 = back_layer(
+    dq, dk, dv, out_rank, chunk, pair, g, got2 = back_layer(
         g_own, o_eff, mixed, b_out_down, q, k, v, lse, tables.reshape(length, HDIM),
-        grad_b_mlp, grad_ad, grad_a_mlp, grad_bd, down1, down2, down3, set_index,
-    )
-    result, grad_in, pooled, pool, heads, _ = finish_layer(
+        grad_b_mlp, grad_ad, grad_a_mlp, grad_bd, down2, down3, set_index,
+    )
+    result, grad_in, whole, split, sequence, heads, _ = finish_layer(
         spans(dq), spans(dk), spans(dv), w_cat, x_own, grad_residual, u, g, low, out_rank, spans(mixed),
-        b_sel, a_sel, chunk, down0, got1, got2, pair, set_index,
-    )
-    pooled = pooled.astype(f32)
-    whole = pooled[:, 0:24].reshape(sets, 48, width)
-    split = pooled[:, 24:48].reshape(sets, 48, width)
-    pool = pool.astype(f32).reshape(8, sets, 8, width)
-    sequence = jnp.transpose(pool, (1, 0, 2, 3)).reshape(sets, 64, width)
+        b_sel, a_sel, chunk, down0, down1, got2, pair, set_index,
+    )
+    whole = whole.reshape(sets, 48, width)
+    split = split.reshape(sets, 48, width)
     heads = heads.astype(f32).reshape(4, sets, 64, HDIM)
     heads = jnp.transpose(heads, (1, 2, 0, 3)).reshape(sets, 4, rank, 4 * HDIM)
     return (

time: 500 us -> 492 us (0.984)
  local copies, waits for them, and re-layouts: 13.7 us -> 8.46 us
where the time goes in v5:
time: 492 us
  Pallas kernels  479 us (97%)
  local copies, waits for them, and re-layouts  8.46 us (2%)
    pallas_call x1, Pallas kernels, front_layer(): pl.pallas_call(front_kernel, in_specs=[vmem] + [anywhere] * 4 + [vmem] *...  182 us
    pallas_call x1, Pallas kernels, mlp_line(): pl.pallas_call(mlp_line_kernel, in_specs=[vmem] + [anywhere] * 8 + [pl.Bl...  149 us
    pallas_call x1, Pallas kernels, finish_layer(): pl.pallas_call(finish_kernel, in_specs=[anywhere] * 9 + [vmem, anywhere]...  87.8 us
    pallas_call x1, Pallas kernels, back_layer(): pl.pallas_call(back_kernel, in_specs=[vmem, anywhere, anywhere, vmem, any...  60 us

profile of v5, /device:TPU:13, one launch (start us, length us, event | category | flops | bytes accessed | tf_op | source)
XLA Modules:
  0.0 491.6 jit_solution(15998906531658933006)
XLA Ops:
  0.6 0.7 dynamic-slice_convert_fusion
  1.3 0.5 multiply_cosine_fusion
  1.9 0.8 pad_maximum_fusion.2.table_ref
  2.6 182.3 %shard_map.197 = (bf16[4,64,2048]{2,1,0:T(8,128)(2,1)}, bf16[256,2048]{1,0:T(8,128)(2,1)}, f32[256,2048]{1,0:T(8,128)}, bf16[256,2048]{1,0:T(8,128)(2,1)}, bf16[...) custom-call(bf16[4,64,2048]{2,1,0:T(8,128)(2,1)} %x_ref.1, ...), custom_call_target="tpu_custom_call" | custom-call | flops 149999992832 | bytes 1000000 | tf_op jit(solution)/shard_map/pallas_call | solution.py:1095
  184.9 148.6 %shard_map.198 = (bf16[256,2048]{1,0:T(8,128)(2,1)}, f32[256,2048]{1,0:T(8,128)}, bf16[4,64,2048]{2,1,0:T(8,128)(2,1)}, bf16[4,64,2048]{2,1,0:T(8,128)(2,1)}, bf...) custom-call(bf16[256,2048]{1,0:T(8,128)(2,1)} %get-tuple-element.48., ...), custom_call_target="tpu_custom_call" | custom-call | flops 109999996928 | bytes 1000000 | tf_op jit(solution)/shard_map/pallas_call | solution.py:1764
  333.5 60.0 %shard_map.199 = (bf16[2048,256]{1,0:T(8,128)(2,1)}, bf16[2048,256]{1,0:T(8,128)(2,1)}, bf16[2048,256]{1,0:T(8,128)(2,1)}, bf16[8,256,16]{2,1,0:T(8,128)(2,1)}, ...) custom-call(bf16[256,2048]{1,0:T(8,128)(2,1)} %get-tuple-element.51., ...), custom_call_target="tpu_custom_call" | custom-call | flops 60000002048 | bytes 1000000 | tf_op jit(solution)/shard_map/pallas_call | solution.py:1361
  393.5 87.8 %shard_map.200 = (bf16[4,64,2048]{2,1,0:T(8,128)(2,1)}, bf16[4,64,2048]{2,1,0:T(8,128)(2,1)}, f32[8,24,2048]{2,1,0:T(8,128)}, f32[8,24,2048]{2,1,0:T(8,128)}, f3...) custom-call(bf16[8,256,256]{2,1,0:T(8,128)(2,1)} %bitcast.31, ...), custom_call_target="tpu_custom_call" | custom-call | flops 80000000000 | bytes 1000000 | tf_op jit(solution)/shard_map/pallas_call | solution.py:2166
  481.3 0.0 copy-start.1
  481.3 1.3 copy.27
  482.6 0.2 reshape.77
  482.8 0.0 copy-start.2
  482.8 0.7 slice_bitcast_fusion.2
  483.5 0.8 slice.33
  484.3 0.0 copy-done.1
  484.3 0.0 copy-start
  484.3 0.8 slice.36
  485.1 1.0 slice.34
  486.1 0.0 copy-done.2
  486.1 0.1 slice.32
  486.2 0.0 copy-done
  486.2 0.1 slice_bitcast_fusion
  486.3 0.1 slice.24
  486.4 1.7 pad_maximum_fusion
  488.1 0.0 copy-start.4
  488.1 0.1 pad_maximum_fusion.1
  488.2 0.0 copy-start.3
  488.2 1.1 copy.25
  489.3 0.4 copy-done.4
  489.6 1.0 copy.30
  490.6 0.0 copy-done.3
  490.6 1.0 copy.31
  (1 shorter events, 0.0 us)
Async XLA Ops:
  481.3 3.0 copy-start.1
  482.8 3.3 copy-start.2
  484.3 2.0 copy-start
  488.1 1.5 copy-start.4
  488.2 2.4 copy-start.3

commit v6 on v5

--- a/solution.py
+++ b/solution.py
@@ -872,12 +872,12 @@
     line.hop(1)
     rest.arrive_first()
     rest.arrive_neighbours()
+    line.hop(2)
     rest.arrive_diagonal()
     for index in range(4):
         near.arrive_core(index)
         rest.arrive_core(index)
         table_gather.arrive_core(index)
-    line.hop(2)
     stores = [pltpu.make_async_copy(u_ref, u_out, store_sem.at[0])]
     stores[0].start()
     mine = set_ref[z]
@@ -943,8 +943,8 @@
 
         return 0
 
+    lax.fori_loop(0, 8, project_all, 0)
     cot_line.begin()
-    lax.fori_loop(0, 8, project_all, 0)
     stores += [
         pltpu.make_async_copy(source, target, store_sem.at[1 + i])
         for i, (source, target) in enumerate(
@@ -995,10 +995,6 @@
         def _():
             o_line.hop(3)
 
-        @pl.when((index == 5) & middle)
-        def _():
-            cot_line.hop(1)
-
         return 0
 
     lax.fori_loop(0, 8, attend_all, 0)
@@ -1045,12 +1041,12 @@
     )
     reduce.begin()
     reduce.keep()
-    reduce.second()
 
     @pl.when(middle)
     def _():
-        cot_line.hop(2)
-
+        cot_line.hop(1)
+
+    reduce.second()
     lax.fori_loop(6, 12, merge, 0)
     stores.append(pltpu.make_async_copy(w_cat, w_cat_out, store_sem.at[7]))
     stores[-1].start()
@@ -1064,6 +1060,11 @@
         m_own_ref[at, :] = normed.astype(bf16)
 
     reduce.finish(0, settle)
+
+    @pl.when(middle)
+    def _():
+        cot_line.hop(2)
+
     reduce.finish(1, settle)
     @pl.when(z * (3 - z) == 0)
     def _():

time: 492 us -> 486 us (0.988)
  Pallas kernels: 479 us -> 472 us
    pallas_call x1, Pallas kernels: 149 us -> 140 us  [mlp_line(): pl.pallas_call(mlp_line_kernel, in_specs=[vmem] + [anywhere] * 8 + [pl.Bl...]
where the time goes in v6:
time: 486 us; the launch traced here: 485 us
  Pallas kernels  472 us (97%)
  local copies, waits for them, and re-layouts  8.46 us (2%)
    pallas_call x1, Pallas kernels, front_layer(): pl.pallas_call(front_kernel, in_specs=[vmem] + [anywhere] * 4 + [vmem] *...  185 us
    pallas_call x1, Pallas kernels, mlp_line(): pl.pallas_call(mlp_line_kernel, in_specs=[vmem] + [anywhere] * 8 + [pl.Bl...  140 us
    pallas_call x1, Pallas kernels, finish_layer(): pl.pallas_call(finish_kernel, in_specs=[anywhere] * 9 + [vmem, anywhere]...  88.3 us
    pallas_call x1, Pallas kernels, back_layer(): pl.pallas_call(back_kernel, in_specs=[vmem, anywhere, anywhere, vmem, any...  59.4 us

profile of v6, /device:TPU:13, one launch (start us, length us, event | category | flops | bytes accessed | tf_op | source)
XLA Modules:
  0.0 485.2 jit_solution(10408443414138447233)
XLA Ops:
  0.6 0.7 dynamic-slice_convert_fusion
  1.3 0.5 multiply_cosine_fusion
  1.9 0.8 pad_maximum_fusion.2.table_ref
  2.6 184.6 %shard_map.197 = (bf16[4,64,2048]{2,1,0:T(8,128)(2,1)}, bf16[256,2048]{1,0:T(8,128)(2,1)}, f32[256,2048]{1,0:T(8,128)}, bf16[256,2048]{1,0:T(8,128)(2,1)}, bf16[...) custom-call(bf16[4,64,2048]{2,1,0:T(8,128)(2,1)} %x_ref.1, ...), custom_call_target="tpu_custom_call" | custom-call | flops 149999992832 | bytes 1000000 | tf_op jit(solution)/shard_map/pallas_call | solution.py:1096
  187.2 140.0 %shard_map.198 = (bf16[256,2048]{1,0:T(8,128)(2,1)}, f32[256,2048]{1,0:T(8,128)}, bf16[4,64,2048]{2,1,0:T(8,128)(2,1)}, bf16[4,64,2048]{2,1,0:T(8,128)(2,1)}, bf...) custom-call(bf16[256,2048]{1,0:T(8,128)(2,1)} %get-tuple-element.48., ...), custom_call_target="tpu_custom_call" | custom-call | flops 109999996928 | bytes 1000000 | tf_op jit(solution)/shard_map/pallas_call | solution.py:1765
  327.3 59.4 %shard_map.199 = (bf16[2048,256]{1,0:T(8,128)(2,1)}, bf16[2048,256]{1,0:T(8,128)(2,1)}, bf16[2048,256]{1,0:T(8,128)(2,1)}, bf16[8,256,16]{2,1,0:T(8,128)(2,1)}, ...) custom-call(bf16[256,2048]{1,0:T(8,128)(2,1)} %get-tuple-element.51., ...), custom_call_target="tpu_custom_call" | custom-call | flops 60000002048 | bytes 1000000 | tf_op jit(solution)/shard_map/pallas_call | solution.py:1362
  386.6 88.3 %shard_map.200 = (bf16[4,64,2048]{2,1,0:T(8,128)(2,1)}, bf16[4,64,2048]{2,1,0:T(8,128)(2,1)}, f32[8,24,2048]{2,1,0:T(8,128)}, f32[8,24,2048]{2,1,0:T(8,128)}, f3...) custom-call(bf16[8,256,256]{2,1,0:T(8,128)(2,1)} %bitcast.31, ...), custom_call_target="tpu_custom_call" | custom-call | flops 80000000000 | bytes 1000000 | tf_op jit(solution)/shard_map/pallas_call | solution.py:2167
  475.0 0.0 copy-start.1
  475.0 1.3 copy.27
  476.2 0.2 reshape.77
  476.5 0.0 copy-start.2
  476.5 0.7 slice_bitcast_fusion.2
  477.1 0.8 slice.33
  477.9 0.0 copy-done.1
  477.9 0.0 copy-start
  477.9 0.8 slice.36
  478.8 1.0 slice.34
  479.8 0.0 copy-done.2
  479.8 0.1 slice.32
  479.9 0.0 copy-done
  479.9 0.1 slice_bitcast_fusion
  480.0 0.1 slice.24
  480.1 1.7 pad_maximum_fusion
  481.8 0.0 copy-start.4
  481.8 0.1 pad_maximum_fusion.1
  481.9 0.0 copy-start.3
  481.9 1.1 copy.25
  482.9 0.4 copy-done.4
  483.3 1.0 copy.30
  484.3 0.0 copy-done.3
  484.3 1.0 copy.31
  (1 shorter events, 0.0 us)
Async XLA Ops:
  475.0 3.0 copy-start.1
  476.5 3.3 copy-start.2
  477.9 2.0 copy-start
  481.8 1.5 copy-start.4
  481.9 2.4 copy-start.3
